TPU v7x, 32 devices: a whole 2x2x4 slice. The times are simulated.
32 devices in a mesh: img: 16 (over z, y, x), ch: 2 (over core).
Axes of the slice: x: 2, y: 2, z: 4, core: 2. Of those that a mesh axis runs over, the one named last changes fastest.
Arguments:
- pixels: bfloat16 [24064, 2016], P('img', 'ch'), may hold values from -30 to 30
- crop_counts: int32 [128], replicated, may hold values from 2 to 10, as said below
- first_weight: bfloat16 [2016, 2016], P(None, 'ch'), may hold values from -0.125 to 0.125
- first_gain: float32 [2016], P('ch'), may hold values from 0.5 to 1.5
- first_shift: float32 [2016], P('ch'), may hold values from -2 to 2
- group_weight: bfloat16 [3, 3, 56, 2016], P(None, None, None, 'ch'), may hold values from -0.25 to 0.25
- group_gain: float32 [2016], P('ch'), may hold values from 0.5 to 1.5
- group_shift: float32 [2016], P('ch'), may hold values from -2 to 2
- squeeze_weight: float32 [2016, 504], P(None, 'ch'), may hold values from -0.5 to 0.5
- squeeze_bias: float32 [504], P('ch'), may hold values from -3 to 3
- excite_weight: float32 [504, 2016], P(None, 'ch'), may hold values from -0.5 to 0.5
- excite_bias: float32 [2016], P('ch'), may hold values from -3 to 3
- last_weight: bfloat16 [2016, 2016], P(None, 'ch'), may hold values from -0.125 to 0.125
- last_gain: float32 [2016], P('ch'), may hold values from 0.5 to 1.5
- last_shift: float32 [2016], P('ch'), may hold values from -2 to 2
- output_grad: bfloat16 [24064, 2016], P('img', 'ch'), may hold values from -6 to 6
Outputs:
- block_out: bfloat16 [24064, 2016], P('img', 'ch')
- pixels_grad: float32 [24064, 2016], P('img', 'ch')
- first_weight_grad: float32 [2016, 2016], P(None, 'ch')
- first_gain_grad: float32 [2016], P('ch')
- first_shift_grad: float32 [2016], P('ch')
- group_weight_grad: float32 [3, 3, 56, 2016], P(None, None, None, 'ch')
- group_gain_grad: float32 [2016], P('ch')
- group_shift_grad: float32 [2016], P('ch')
- squeeze_weight_grad: float32 [2016, 504], P(None, 'ch')
- squeeze_bias_grad: float32 [504], P('ch')
- excite_weight_grad: float32 [504, 2016], P(None, 'ch')
- excite_bias_grad: float32 [2016], P('ch')
- last_weight_grad: float32 [2016, 2016], P(None, 'ch')
- last_gain_grad: float32 [2016], P('ch')
- last_shift_grad: float32 [2016], P('ch')
Inputs may be any that keep to these rules, and one draw needn't show every extreme that they name: `crop_counts`: every image has at least 2 and at most 10 small crops; some image has 10 and some image 2.
All inputs are finite; a program needn't handle non-finite values.
Results may differ from a plain program's by a relative error of at most 0.0095.
Values may be sent and summed in bfloat16 or wider, within the bound.
A program may use at most 320 MiB of HBM per device.

v0:
```python
import jax
import jax.numpy as jnp
from jax import lax
from jax.sharding import PartitionSpec as P

GROUP_WIDTH = 56
BIG_SIDE = 7
SMALL_SIDE = 3
BIG_CROPS = 2
ROWS_IMG = 188


EPSILON = 1e-05
HIGHEST = lax.Precision.HIGHEST


def live_mask(image_counts):
    big_rows = BIG_CROPS * BIG_SIDE * BIG_SIDE
    places = jnp.arange(ROWS_IMG, dtype=jnp.int32)
    slot_index = (places - big_rows) // (SMALL_SIDE * SMALL_SIDE)
    living = (places[None, :] < big_rows) | (slot_index[None, :] < image_counts[:, None])
    return living.astype(jnp.float32).reshape(-1)


def split_crops(activation):
    channels = activation.shape[-1]
    per_image = activation.reshape(-1, ROWS_IMG, channels)
    big_rows = BIG_CROPS * BIG_SIDE * BIG_SIDE
    larger = per_image[:, :big_rows].reshape(-1, BIG_SIDE, BIG_SIDE, channels)
    smaller = per_image[:, big_rows:].reshape(-1, SMALL_SIDE, SMALL_SIDE, channels)
    return (larger, smaller)


def join_crops(larger, smaller, images):
    channels = larger.shape[-1]
    joined = jnp.concatenate(
        [larger.reshape(images, -1, channels), smaller.reshape(images, -1, channels)], axis=1
    )
    return joined.reshape(-1, channels)


def silu_slope(values_in):
    logistic = jax.nn.sigmoid(values_in)
    return logistic * (1.0 + values_in * (1.0 - logistic))


def inner_rows(left_rows, right_rows):
    return lax.dot_general(
        left_rows, right_rows, (((0,), (0,)), ((), ())), preferred_element_type=jnp.float32
    )


def times_transpose(left_rows, matrix):
    return lax.dot_general(
        left_rows, matrix, (((1,), (1,)), ((), ())), preferred_element_type=jnp.float32
    )


def padded_tiles(crop_tiles):
    number, tile_side, _, channels = crop_tiles.shape
    groups = channels // GROUP_WIDTH
    padded = jnp.pad(crop_tiles, ((0, 0), (1, 1), (1, 1), (0, 0)))
    return padded.reshape(number, tile_side + 2, tile_side + 2, groups, GROUP_WIDTH)


def tap_forward(crop_tiles, kernel):
    number, tile_side, _, channels = crop_tiles.shape
    groups = channels // GROUP_WIDTH
    padded = padded_tiles(crop_tiles)
    blocks = kernel.reshape(3, 3, GROUP_WIDTH, groups, GROUP_WIDTH)
    summed = jnp.zeros((number, tile_side, tile_side, groups, GROUP_WIDTH), jnp.float32)
    for row_tap in range(3):
        for column_tap in range(3):
            window = padded[:, row_tap : row_tap + tile_side, column_tap : column_tap + tile_side]
            summed = summed + jnp.einsum(
                "nyxgi,igj->nyxgj",
                window,
                blocks[row_tap, column_tap],
                preferred_element_type=jnp.float32,
            )
    return summed.reshape(number, tile_side, tile_side, channels)


def tap_backward(crop_tiles, kernel, gradient):
    number, tile_side, _, channels = crop_tiles.shape
    groups = channels // GROUP_WIDTH
    padded = padded_tiles(crop_tiles)
    blocks = kernel.reshape(3, 3, GROUP_WIDTH, groups, GROUP_WIDTH)
    grad_tiles = gradient.reshape(number, tile_side, tile_side, groups, GROUP_WIDTH)
    padded_grad = jnp.zeros(
        (number, tile_side + 2, tile_side + 2, groups, GROUP_WIDTH), jnp.float32
    )
    kernel_parts = []
    for row_tap in range(3):
        for column_tap in range(3):
            window = padded[:, row_tap : row_tap + tile_side, column_tap : column_tap + tile_side]
            kernel_parts.append(
                jnp.einsum(
                    "nyxgi,nyxgj->igj", window, grad_tiles, preferred_element_type=jnp.float32
                )
            )
            spread_back = jnp.einsum(
                "nyxgj,igj->nyxgi",
                grad_tiles,
                blocks[row_tap, column_tap],
                preferred_element_type=jnp.float32,
            )
            padded_grad = padded_grad.at[
                :, row_tap : row_tap + tile_side, column_tap : column_tap + tile_side
            ].add(spread_back)
    kernel_grad = jnp.stack(kernel_parts).reshape(3, 3, GROUP_WIDTH, channels)
    input_grad = padded_grad[:, 1:-1, 1:-1].reshape(number, tile_side, tile_side, channels)
    return (input_grad, kernel_grad)


def group_forward(activation, kernel, images):
    larger, smaller = split_crops(activation)
    return join_crops(tap_forward(larger, kernel), tap_forward(smaller, kernel), images)


def group_backward(activation, kernel, gradient, images):
    larger, smaller = split_crops(activation)
    larger_grad, smaller_grad = split_crops(gradient)
    large_input, large_kernel = tap_backward(larger, kernel, larger_grad)
    small_input, small_kernel = tap_backward(smaller, kernel, smaller_grad)
    return (join_crops(large_input, small_input, images), large_kernel + small_kernel)


def normalize(values_in, norm_gain, norm_shift, row_mask, live_total):
    average = lax.psum(jnp.sum(values_in * row_mask, axis=0), "img") / live_total
    centred = values_in - average
    variance = lax.psum(jnp.sum(row_mask * centred * centred, axis=0), "img") / live_total
    scaling = lax.rsqrt(variance + EPSILON)
    normed = (values_in - average) * scaling
    return (normed, scaling, normed * norm_gain + norm_shift)


def norm_back(incoming, normed, scaling, norm_gain, row_mask, live_total):
    shift_grad, gain_grad = lax.psum(
        (jnp.sum(incoming * row_mask, axis=0), jnp.sum(incoming * normed * row_mask, axis=0)), "img"
    )
    outgoing = (
        row_mask
        * (norm_gain * scaling)
        * (incoming - shift_grad / live_total - normed * gain_grad / live_total)
    )
    return (outgoing, gain_grad, shift_grad)


def settle(gradients):
    flattened = jnp.concatenate([member.reshape(-1) for member in gradients])
    flattened = jnp.pad(flattened, (0, -flattened.shape[0] % lax.axis_size("img")))
    shared = lax.psum_scatter(flattened, "img", scatter_dimension=0, tiled=True)
    complete = lax.all_gather(shared.astype(jnp.bfloat16), "img", axis=0, tiled=True).astype(
        shared.dtype
    )
    results = []
    offset = 0
    for member in gradients:
        results.append(complete[offset : offset + member.size].reshape(member.shape))
        offset = offset + member.size
    return results


def body(
    pixels,
    crop_counts,
    first_weight,
    first_gain,
    first_shift,
    group_weight,
    group_gain,
    group_shift,
    squeeze_weight,
    squeeze_bias,
    excite_weight,
    excite_bias,
    last_weight,
    last_gain,
    last_shift,
    output_grad,
):
    images = pixels.shape[0] // ROWS_IMG
    channels = pixels.shape[1]
    local_counts = lax.dynamic_slice_in_dim(crop_counts, lax.axis_index("img") * images, images)
    row_mask = live_mask(local_counts)[:, None]
    image_mask = row_mask.reshape(images, ROWS_IMG, 1)
    per_image = (BIG_CROPS * BIG_SIDE * BIG_SIDE + SMALL_SIDE * SMALL_SIDE * local_counts).astype(
        jnp.float32
    )
    live_total = jnp.sum(
        (BIG_CROPS * BIG_SIDE * BIG_SIDE + SMALL_SIDE * SMALL_SIDE * crop_counts).astype(
            jnp.float32
        )
    )
    full_pixels = lax.all_gather(pixels, "ch", axis=1, tiled=True)
    first_out = jnp.dot(full_pixels, first_weight, preferred_element_type=jnp.float32)
    first_normed, first_scaling, first_pre = normalize(
        first_out, first_gain, first_shift, row_mask, live_total
    )
    first_act = jax.nn.silu(first_pre).astype(jnp.bfloat16)
    group_out = group_forward(first_act, group_weight, images)
    group_normed, group_scaling, group_pre = normalize(
        group_out, group_gain, group_shift, row_mask, live_total
    )
    group_act = jax.nn.silu(group_pre)
    by_image = group_act.reshape(images, ROWS_IMG, channels)
    pooled = jnp.sum(by_image * image_mask, axis=1) / per_image[:, None]
    full_pooled = lax.all_gather(pooled, "ch", axis=1, tiled=True)
    squeeze_pre = jnp.dot(full_pooled, squeeze_weight, precision=HIGHEST) + squeeze_bias
    squeezed = jax.nn.silu(squeeze_pre)
    full_squeezed = lax.all_gather(squeezed, "ch", axis=1, tiled=True)
    excited = jax.nn.sigmoid(jnp.dot(full_squeezed, excite_weight, precision=HIGHEST) + excite_bias)
    scaled = (by_image * excited[:, None, :]).reshape(-1, channels).astype(jnp.bfloat16)
    full_scaled = lax.all_gather(scaled, "ch", axis=1, tiled=True)
    last_out = jnp.dot(full_scaled, last_weight, preferred_element_type=jnp.float32)
    last_normed, last_scaling, last_pre = normalize(
        last_out, last_gain, last_shift, row_mask, live_total
    )
    merged = pixels.astype(jnp.float32) + last_pre
    block_out = (jax.nn.silu(merged) * row_mask).astype(jnp.bfloat16)
    merged_grad = output_grad.astype(jnp.float32) * row_mask * silu_slope(merged)
    last_grad, last_gain_grad, last_shift_grad = norm_back(
        merged_grad, last_normed, last_scaling, last_gain, row_mask, live_total
    )
    last_low = last_grad.astype(jnp.bfloat16)
    last_weight_grad = inner_rows(full_scaled, last_low)
    scaled_grad = lax.psum_scatter(
        times_transpose(last_low, last_weight), "ch", scatter_dimension=1, tiled=True
    )
    scaled_image = scaled_grad.reshape(images, ROWS_IMG, channels)
    excite_grad = jnp.sum(scaled_image * by_image, axis=1) * excited * (1.0 - excited)
    excite_weight_grad = jnp.dot(full_squeezed.T, excite_grad, precision=HIGHEST)
    excite_bias_grad = jnp.sum(excite_grad, axis=0)
    squeeze_terms = jnp.dot(excite_grad, excite_weight.T, precision=HIGHEST)
    squeeze_grad = lax.psum_scatter(
        squeeze_terms, "ch", scatter_dimension=1, tiled=True
    ) * silu_slope(squeeze_pre)
    squeeze_weight_grad = jnp.dot(full_pooled.T, squeeze_grad, precision=HIGHEST)
    squeeze_bias_grad = jnp.sum(squeeze_grad, axis=0)
    pooled_terms = jnp.dot(squeeze_grad, squeeze_weight.T, precision=HIGHEST)
    pooled_grad = lax.psum_scatter(
        pooled_terms.astype(jnp.bfloat16), "ch", scatter_dimension=1, tiled=True
    ).astype(jnp.float32)
    act_grad = (
        scaled_image * excited[:, None, :]
        + image_mask * (pooled_grad / per_image[:, None])[:, None, :]
    )
    group_pre_grad = act_grad.reshape(-1, channels) * silu_slope(group_pre)
    group_grad, group_gain_grad, group_shift_grad = norm_back(
        group_pre_grad, group_normed, group_scaling, group_gain, row_mask, live_total
    )
    first_act_grad, group_weight_grad = group_backward(
        first_act, group_weight, group_grad.astype(jnp.bfloat16), images
    )
    first_pre_grad = first_act_grad * silu_slope(first_pre)
    first_grad, first_gain_grad, first_shift_grad = norm_back(
        first_pre_grad, first_normed, first_scaling, first_gain, row_mask, live_total
    )
    first_low = first_grad.astype(jnp.bfloat16)
    first_weight_grad = inner_rows(full_pixels, first_low)
    pixels_grad = merged_grad + lax.psum_scatter(
        times_transpose(first_low, first_weight).astype(jnp.bfloat16),
        "ch",
        scatter_dimension=1,
        tiled=True,
    ).astype(jnp.float32)
    (
        first_weight_grad,
        group_weight_grad,
        squeeze_weight_grad,
        squeeze_bias_grad,
        excite_weight_grad,
        excite_bias_grad,
        last_weight_grad,
    ) = settle(
        (
            first_weight_grad,
            group_weight_grad,
            squeeze_weight_grad,
            squeeze_bias_grad,
            excite_weight_grad,
            excite_bias_grad,
            last_weight_grad,
        )
    )
    return (
        block_out,
        pixels_grad,
        first_weight_grad,
        first_gain_grad,
        first_shift_grad,
        group_weight_grad,
        group_gain_grad,
        group_shift_grad,
        squeeze_weight_grad,
        squeeze_bias_grad,
        excite_weight_grad,
        excite_bias_grad,
        last_weight_grad,
        last_gain_grad,
        last_shift_grad,
    )


def solution(mesh):
    return jax.shard_map(
        body,
        mesh=mesh,
        in_specs=(
            P("img", "ch"),
            P(),
            P(None, "ch"),
            P("ch"),
            P("ch"),
            P(None, None, None, "ch"),
            P("ch"),
            P("ch"),
            P(None, "ch"),
            P("ch"),
            P(None, "ch"),
            P("ch"),
            P(None, "ch"),
            P("ch"),
            P("ch"),
            P("img", "ch"),
        ),
        out_specs=(
            P("img", "ch"),
            P("img", "ch"),
            P(None, "ch"),
            P("ch"),
            P("ch"),
            P(None, None, None, "ch"),
            P("ch"),
            P("ch"),
            P(None, "ch"),
            P("ch"),
            P(None, "ch"),
            P("ch"),
            P(None, "ch"),
            P("ch"),
            P("ch"),
        ),
        check_vma=False,
    )
```

profile of v0, /device:TPU:10, one launch (start us, length us, event | category | flops | bytes accessed | tf_op | source)
XLA Modules:
  0.0 2628.2 jit_solution(13505842136318386300)
XLA Ops:
  36.2 11.9 multiply_reduce_fusion.10
  48.0 31.0 %psum.84 = f32[1008]{0:T(1024)S(1)} all-reduce(f32[1008]{0:T(1024)S(1)} %get-tuple-element.299), channel_id=1, replica_groups=mesh['img'=16,'ch'=2] {'img'}, use_global_device_ids=true, to_apply=%region_1.2 | all-reduce | flops 1008 | bytes 8064 | tf_op jit(solution)/shard_map/psum | solution.py:130
  83.3 41.9 %psum.85 = f32[1008]{0:T(1024)S(1)} all-reduce(f32[1008]{0:T(1024)S(1)} %fusion.9), channel_id=1, replica_groups=mesh['img'=16,'ch'=2] {'img'}, use_global_device_ids=true, to_apply=%region_4.5 | all-reduce | flops 1008 | bytes 8064 | tf_op jit(solution)/shard_map/psum | solution.py:132
  150.5 12.8 reshape.1112
  163.2 29.6 %fusion.217 = (bf16[16,7,7,18,56]{4,3,2,1,0:T(8,128)(2,1)}, bf16[16,7,7,18,56]{4,3,2,1,0:T(8,128)(2,1)}, bf16[16,7,7,18,56]{4,3,2,1,0:T(8,128)(2,1)}, bf16[16,7,...) fusion(bf16[16,9,9,18,56]{4,3,2,1,0:T(8,128)(2,1)} %reshape.1112), kind=kLoop, calls=%fused_computation.238 | loop fusion | bytes 28449792 | tf_op jit(solution)/shard_map/slice | solution.py:74
  229.9 20.5 add_bitcast_fusion
  313.1 15.1 add_bitcast_fusion.1
  349.0 36.6 %psum.86 = f32[1008]{0:T(1024)S(1)} all-reduce(f32[1008]{0:T(1024)S(1)} %get-tuple-element.256), channel_id=1, replica_groups=mesh['img'=16,'ch'=2] {'img'}, use_global_device_ids=true, to_apply=%region_6.7 | all-reduce | flops 1008 | bytes 8064 | tf_op jit(solution)/shard_map/psum | solution.py:130
  396.1 38.6 %psum.87 = f32[1008]{0:T(1024)S(1)} all-reduce(f32[1008]{0:T(1024)S(1)} %fusion.8), channel_id=1, replica_groups=mesh['img'=16,'ch'=2] {'img'}, use_global_device_ids=true, to_apply=%region_8.9 | all-reduce | flops 1008 | bytes 8064 | tf_op jit(solution)/shard_map/psum | solution.py:132
  463.8 20.5 all-gather.9.cloned.1.call-done
  492.9 11.9 multiply_reduce_fusion.9
  504.8 31.0 %psum.88 = f32[1008]{0:T(1024)S(1)} all-reduce(f32[1008]{0:T(1024)S(1)} %get-tuple-element.301), channel_id=1, replica_groups=mesh['img'=16,'ch'=2] {'img'}, use_global_device_ids=true, to_apply=%region_11.12 | all-reduce | flops 1008 | bytes 8064 | tf_op jit(solution)/shard_map/psum | solution.py:130
  540.0 41.6 %psum.89 = f32[1008]{0:T(1024)S(1)} all-reduce(f32[1008]{0:T(1024)S(1)} %fusion.10), channel_id=1, replica_groups=mesh['img'=16,'ch'=2] {'img'}, use_global_device_ids=true, to_apply=%region_13.14 | all-reduce | flops 1008 | bytes 8064 | tf_op jit(solution)/shard_map/psum | solution.py:132
  592.7 37.2 %all-reduce.10 = (f32[1008]{0:T(1024)S(1)}, f32[1008]{0:T(1024)S(1)}) all-reduce(f32[1008]{0:T(1024)S(1)} %get-tuple-element.236, f32[1008]{0:T(1024)S(1)} %get-tuple-element.235), channel_id=1, replica_groups=mesh['img'=16,'ch'=2] {'img'}, use_global_device_ids=true, to_apply=%region_17.18 | all-reduce | flops 2016 | bytes 16128 | tf_op jit(solution)/shard_map/psum | solution.py:139
  653.5 12.9 fusion.224
  736.8 12.3 multiply_reduce_fusion.6
  749.1 31.4 %all-reduce.9 = (f32[1008]{0:T(1024)S(1)}, f32[1008]{0:T(1024)S(1)}) all-reduce(f32[1008]{0:T(1024)S(1)} %get-tuple-element.234, f32[1008]{0:T(1024)S(1)} %get-tuple-element.233), channel_id=1, replica_groups=mesh['img'=16,'ch'=2] {'img'}, use_global_device_ids=true, to_apply=%region_25.26 | all-reduce | flops 2016 | bytes 16128 | tf_op jit(solution)/shard_map/psum | solution.py:139
  991.2 42.1 %all-reduce.8 = (f32[1008]{0:T(1024)S(1)}, f32[1008]{0:T(1024)S(1)}) all-reduce(f32[1008]{0:T(1024)S(1)} %get-tuple-element.232, f32[1008]{0:T(1024)S(1)} %get-tuple-element.231), channel_id=1, replica_groups=mesh['img'=16,'ch'=2] {'img'}, use_global_device_ids=true, to_apply=%region_30.31 | all-reduce | flops 2016 | bytes 16128 | tf_op jit(solution)/shard_map/psum | solution.py:139
  1072.5 177.4 %concatenate.59 = f32[5589612]{0:T(1024)} concatenate(f32[2032128]{0:T(1024)} %reshape.1044, f32[508032]{0:T(1024)} %add.430, f32[508032]{0:T(1024)} %reshape.1045, f32[252]{0:T(256)S(1)} %copy-done.77, f32[508032]{0:T(1024)S(1)} %copy-done.23, f32[1008]{0:T(1024)S(1)} %copy-done.72, f32[2032128]{0:T(1024)} %reshape.1047), dimensions={0} | concatenate | bytes 44716896 | tf_op jit(solution)/shard_map/concatenate | solution.py:151
  1249.9 16.3 pad.90
  1266.2 950.0 %all-reduce.15 = bf16[5589616]{0:T(1024)(128)(2,1)} all-reduce(f32[5589616]{0:T(1024)} %pad.90), channel_id=6, replica_groups=mesh['img'=16,'ch'=2] {'img'}, use_global_device_ids=true, to_apply=%region_34.35.clone | all-reduce | flops 5589616 | bytes 33537696
  2222.6 11.7 dynamic-update-slice.54
  2234.4 11.3 convolution_convert_fusion
  2254.4 303.8 %all-reduce.14.cloned.1.call-done = bf16[5589616]{0:T(1024)(128)(2,1)} async-done(((bf16[5589616]{0:T(1024)(128)(2,1)}), bf16[5589616]{0:T(1024)(128)(2,1)}) %all-reduce.14.cloned.1.call-update) | async-done | bytes 11179248
  (458 shorter events, 660.7 us)
Async XLA Ops:
  7.2 434.7 %copy-start = (f32[2016,252]{1,0:T(8,128)S(1)}, f32[2016,252]{1,0:T(8,128)}, u32[]{:S(2)}) copy-start(f32[2016,252]{1,0:T(8,128)} %param.60) | copy-start | bytes 6096388
  7.2 20.4 all-gather.7.cloned.1.call-start
  7.9 476.3 %all-gather.9.cloned.1.call-start = ((), (), s32[]{:S(2)}) async-start(), calls=%async_computation.5 | async-start | bytes 9240576 | tf_op jit(solution)/shard_map/all_gather | solution.py:215
  16.7 63.0 %copy-start.57 = (f32[1504]{0:T(1024)}, f32[1504]{0:T(1024)S(1)}, u32[]{:S(2)}) copy-start(f32[1504]{0:T(1024)S(1)} %get-tuple-element.292) | copy-start | bytes 18052
  20.6 176.8 %copy-start.29 = (bf16[1,1,56,18,56]{4,3,2,1,0:T(8,128)(2,1)}, bf16[1,1,56,18,56]{4,3,2,1,0:T(8,128)(2,1)S(1)}, u32[]{:S(2)}) copy-start(bf16[1,1,56,18,56]{4,3,2,1,0:T(8,128)(2,1)S(1)} %get-tuple-element.283) | copy-start | bytes 338692
  20.6 265.5 %copy-start.27 = (bf16[1,1,56,18,56]{4,3,2,1,0:T(8,128)(2,1)}, bf16[1,1,56,18,56]{4,3,2,1,0:T(8,128)(2,1)S(1)}, u32[]{:S(2)}) copy-start(bf16[1,1,56,18,56]{4,3,2,1,0:T(8,128)(2,1)S(1)} %get-tuple-element.290) | copy-start | bytes 338692
  20.7 292.4 %copy-start.25 = (bf16[1,1,56,18,56]{4,3,2,1,0:T(8,128)(2,1)}, bf16[1,1,56,18,56]{4,3,2,1,0:T(8,128)(2,1)S(1)}, u32[]{:S(2)}) copy-start(bf16[1,1,56,18,56]{4,3,2,1,0:T(8,128)(2,1)S(1)} %get-tuple-element.282) | copy-start | bytes 338692
  48.0 77.2 %copy-start.67 = (f32[1008]{0:T(1024)S(1)}, f32[1008]{0:T(1024)}, u32[]{:S(2)}) copy-start(f32[1008]{0:T(1024)} %param.55) | copy-start | bytes 12100
  48.0 78.4 %copy-start.70 = (f32[1008]{0:T(1024)S(1)}, f32[1008]{0:T(1024)}, u32[]{:S(2)}) copy-start(f32[1008]{0:T(1024)} %param.56) | copy-start | bytes 12100
  79.7 51.7 %copy-start.62 = (f32[1008]{0:T(1024)}, f32[1008]{0:T(1024)S(1)}, u32[]{:S(2)}) copy-start(f32[1008]{0:T(1024)S(1)} %broadcast_divide_fusion.5) | copy-start | bytes 12100
  286.2 26.9 %copy-start.6 = (bf16[80,3,3,18,56]{0,4,3,2,1:T(8,128)(2,1)}, bf16[80,3,3,18,56]{0,4,3,2,1:T(8,128)(2,1)S(1)}, u32[]{:S(2)}) copy-start(bf16[80,3,3,18,56]{0,4,3,2,1:T(8,128)(2,1)S(1)} %get-tuple-element.273) | copy-start | bytes 4354564
  392.4 42.3 %copy-start.61 = (f32[1008]{0:T(1024)S(1)}, f32[1008]{0:T(1024)}, u32[]{:S(2)}) copy-start(f32[1008]{0:T(1024)} %param.58) | copy-start | bytes 12100
  392.4 43.0 %copy-start.64 = (f32[1008]{0:T(1024)S(1)}, f32[1008]{0:T(1024)}, u32[]{:S(2)}) copy-start(f32[1008]{0:T(1024)} %param.59) | copy-start | bytes 12100
  392.4 47.4 %copy-start.75 = (f32[8]{0:T(128)S(1)}, f32[8]{0:T(128)}, u32[]{:S(2)}) copy-start(f32[8]{0:T(128)} %get-tuple-element.254) | copy-start | bytes 100
  396.1 45.8 %copy-start.86 = (f32[252]{0:T(256)S(1)}, f32[252]{0:T(256)}, u32[]{:S(2)}) copy-start(f32[252]{0:T(256)} %param.61) | copy-start | bytes 3028
  396.1 48.7 %copy-start.76 = (f32[1008]{0:T(1024)S(1)}, f32[1008]{0:T(1024)}, u32[]{:S(2)}) copy-start(f32[1008]{0:T(1024)} %param.63) | copy-start | bytes 12100
  463.7 29.1 %copy-start.58 = (f32[1504]{0:T(1024)S(1)}, f32[1504]{0:T(1024)}, u32[]{:S(2)}) copy-start(f32[1504]{0:T(1024)} %copy-done.57) | copy-start | bytes 18052
  463.8 213.4 %reduce-scatter.11.cloned.1.call-start = ((), (), s32[]{:S(2)}) async-start(), calls=%async_computation.6 | async-start | bytes 18579456
  504.8 76.9 %copy-start.73 = (f32[1008]{0:T(1024)S(1)}, f32[1008]{0:T(1024)}, u32[]{:S(2)}) copy-start(f32[1008]{0:T(1024)} %param.65) | copy-start | bytes 12100
  504.8 77.6 %copy-start.81 = (f32[1008]{0:T(1024)S(1)}, f32[1008]{0:T(1024)}, u32[]{:S(2)}) copy-start(f32[1008]{0:T(1024)} %param.66) | copy-start | bytes 12100
  647.8 78.4 %reduce-scatter.13.cloned.1.call-start = ((), (), s32[]{:S(2)}) async-start(), calls=%async_computation.7 | async-start | bytes 774144
  713.3 1844.9 %all-reduce.14.cloned.1.call-start = ((), (), s32[]{:S(2)}) async-start(), calls=%async_computation.3 | async-start | bytes 22360064
  982.6 51.3 %copy-start.74 = (f32[1008]{0:T(1024)S(1)}, f32[1008]{0:T(1024)}, u32[]{:S(2)}) copy-start(f32[1008]{0:T(1024)} %get-tuple-element.245) | copy-start | bytes 12100
  2234.4 373.7 %reduce-scatter.15.cloned.1.call-start = ((), (), s32[]{:S(2)}) async-start(), calls=%async_computation.8 | async-start | bytes 9289728
  (104 other events, 479.3 us)
Sparse Core Ops, SparseCore 0:
  9.6 17.9 all-gather.6
  463.9 20.3 all-gather.8
  647.9 24.9 reduce-scatter.10
  713.4 12.7 reduce-scatter.12
  2234.5 323.6 all-reduce.13
  2560.3 14.7 reduce-scatter.14
where the time goes:
time: 2650 us; the launch traced here: 2630 us
  blocking collectives  1290 us (49%)
  local copies, waits for them, and re-layouts  606 us (23%)
  waiting for transfers between devices  341 us (13%)
  matrix products  255 us (10%)
  other arithmetic  119 us (4%)
    unnamed x2, blocking collectives  953 us
    unnamed x10, waiting for transfers between devices  313 us
    concatenate x1, local copies, waits for them, and re-layouts, settle(): flattened = jnp.concatenate([member.reshape(-1) for member in gradients])  177 us
    psum x3, blocking collectives, normalize(): lax.psum(jnp.sum(row_mask * centred * centred, axis=0), 'img') / live_total  122 us
    psum x3, blocking collectives, norm_back(): lax.psum((jnp.sum(incoming * row_mask, axis=0), jnp.sum(incoming * normed...  111 us
    dot_general x18, matrix products, tap_forward(): jnp.einsum('nyxgi,igj->nyxgj', window, blocks[row_tap, column_tap], prefe...  99.1 us
    psum x3, blocking collectives, normalize(): lax.psum(jnp.sum(values_in * row_mask, axis=0), 'img') / live_total  98.5 us
    unnamed x255, local copies, waits for them, and re-layouts  53.2 us
  transfers between devices with their start and end apart: 6, of which 4 were waited for; matrix products, arithmetic and copies ran while one was open for 4% of the time, Pallas kernels for 0%

commit v1 on v0

v1 whole, which is shorter than its diff:
```python
import functools

import jax
import jax.numpy as jnp
from jax import lax
from jax.experimental import pallas as pl
from jax.experimental.pallas import tpu as pltpu
from jax.sharding import PartitionSpec as P


GROUP_WIDTH = 56
ROWS_IMG = 188
BIG_ROWS = 98
IMGS = 8
ROWS = IMGS * ROWS_IMG
HALF = 1008
TILES = 8
LAST = HALF - 7 * 128
EPSILON = 1e-05
F32 = jnp.float32
BF16 = jnp.bfloat16
HIGHEST = lax.Precision.HIGHEST
MESH = pl.DeviceIdType.MESH
VMEM = pl.BlockSpec(memory_space=pltpu.VMEM)
ANY = pl.BlockSpec(memory_space=pl.ANY)
VMEM_LIMIT = 60 * 1024 * 1024
SPANS = ((0, 256), (256, 512), (512, 768), (768, 1008))
WINDOWS = ((0, 3), (1, 5), (3, 7), (5, 8))
BIG_PAD = 73 * 16
PAD_ROWS = BIG_PAD + 21 * 80
TAPS = tuple((dy, dx) for dy in (-1, 0, 1) for dx in (-1, 0, 1))
DMA = pltpu.SemaphoreType.DMA


def big_place(y, x):
    return (1 + (y + 1) * 8 + x) * 16


def small_place(y, x):
    return BIG_PAD + (1 + (y + 1) * 4 + x) * 80


def natural_row(tile):
    if tile < BIG_ROWS:
        return (tile % 2) * 49 + tile // 2
    tile = tile - BIG_ROWS
    return BIG_ROWS + (tile % 10) * 9 + tile // 10


def padded_row(tile):
    if tile < BIG_ROWS:
        pixel = tile // 2
        return big_place(pixel // 7, pixel % 7) + (tile % 2) * 8
    tile = tile - BIG_ROWS
    pixel = tile // 10
    return small_place(pixel // 3, pixel % 3) + (tile % 10) * 8


REAL_ROWS = frozenset(padded_row(tile) for tile in range(0, ROWS_IMG, 2))
ZERO_ROWS = tuple(row for row in range(0, PAD_ROWS, 16) if row not in REAL_ROWS)


def sigmoid(v):
    return 0.5 + 0.5 * jnp.tanh(0.5 * v)


def slope_of(v, s):
    return s * (1.0 + v * (1.0 - s))


def dot(a, b, dims=((1,), (0,)), **kw):
    return lax.dot_general(a, b, (dims, ((), ())), preferred_element_type=F32, **kw)


def for_each(count, step):
    if count <= 16:
        for index in range(count):
            step(index)
    else:
        lax.fori_loop(0, count, lambda index, _: (step(index), 0)[1], 0)


def for_tiles(step):
    lax.fori_loop(0, TILES, lambda j, _: (step(j), 0)[1], 0)


def for_ragged_tiles(step):
    def full(j, _):
        step(j, pl.ds(pl.multiple_of(j * 128, 128), 128), 128)
        return 0

    lax.fori_loop(0, TILES - 1, full, 0)
    step(TILES - 1, pl.ds(7 * 128, LAST), LAST)


def greet(n, all_images=True, partner=True):
    barrier = pltpu.get_barrier_semaphore()
    me = lax.axis_index("img")
    count = 0
    if all_images:
        for_each(
            n - 1,
            lambda d: pl.semaphore_signal(
                barrier, 1, device_id={"img": lax.rem(me + d + 1, n)}, device_id_type=MESH
            ),
        )
        count += n - 1
    if partner:
        pl.semaphore_signal(
            barrier, 1, device_id={"ch": 1 - lax.axis_index("ch")}, device_id_type=MESH
        )
        count += 1
    return lambda: pl.semaphore_wait(barrier, count)


class Gather:
    def __init__(self, n, source, target, send, recv):
        self.n, self.source, self.target, self.send, self.recv = n, source, target, send, recv
        self.me = lax.axis_index("img")

    def copy(self, d):
        return pltpu.make_async_remote_copy(
            src_ref=self.source,
            dst_ref=self.target.at[self.me],
            send_sem=self.send.at[d],
            recv_sem=self.recv.at[d],
            device_id={"img": lax.rem(self.me + d + 1, self.n)},
            device_id_type=MESH,
        )

    def start(self):
        for_each(self.n - 1, lambda d: self.copy(d).start())
        self.target[self.me] = self.source[...]

    def wait(self):
        for_each(self.n - 1, lambda d: self.copy(d).wait())


def swap(source, target, send, recv):
    return pltpu.make_async_remote_copy(
        src_ref=source,
        dst_ref=target,
        send_sem=send,
        recv_sem=recv,
        device_id={"ch": 1 - lax.axis_index("ch")},
        device_id_type=MESH,
    )


def put_span(ref, span, rows, value, add=False):
    left, right = value[:, :128], value[:, 128:]
    width = right.shape[1]
    if add:
        ref[2 * span, rows, :] += left
        ref[2 * span + 1, rows, 0:width] += right
    else:
        ref[2 * span, rows, :] = left
        ref[2 * span + 1, rows, 0:width] = right


def norm_constants(n, stats, live, gain_shift, consts):
    def total(step):
        return lax.fori_loop(0, n, lambda i, acc: acc + step(i), jnp.zeros((TILES, 128), F32))

    number = total(lambda i: live[i])
    average = total(lambda i: live[i] * stats[i, 0]) / number

    def centred(i):
        off = stats[i, 0] - average
        return stats[i, 1] + live[i] * off * off

    variance = total(centred) / number
    consts[0] = average
    consts[1] = lax.rsqrt(variance + EPSILON)
    consts[2] = gain_shift[0]
    consts[3] = gain_shift[1]
    consts[4] = number


def back_constants(n, sums, consts, grads):
    shift_grad = lax.fori_loop(
        0, n, lambda i, acc: acc + sums[i, 0], jnp.zeros((TILES, 128), F32)
    )
    gain_grad = lax.fori_loop(
        0, n, lambda i, acc: acc + sums[i, 1], jnp.zeros((TILES, 128), F32)
    )
    grads[0] = gain_grad
    grads[1] = shift_grad
    consts[5] = shift_grad / consts[4]
    consts[6] = gain_grad / consts[4]
    consts[7] = consts[1] * consts[2]


def row_of(consts, k, j):
    return consts[k, pl.ds(j, 1), :]


def natural_stats(ref, mask, count, local):
    def step(j):
        x = ref[j]
        m = mask[...]
        average = jnp.sum(x * m, axis=0, keepdims=True) / count
        off = x - average
        local[0, pl.ds(j, 1), :] = average
        local[1, pl.ds(j, 1), :] = jnp.sum(m * off * off, axis=0, keepdims=True)

    for_tiles(step)


def crop_sum(value, mask10):
    big = jnp.sum(value[:BIG_ROWS], axis=0)
    small = jnp.sum(value[BIG_ROWS:].reshape(9, 10, IMGS, 128), axis=0)
    return big + jnp.sum(small * mask10[...], axis=0)


def crop_stats(ref, mask10, count, local):
    def step(j):
        x = ref[j].reshape(ROWS_IMG, IMGS, 128)
        average = jnp.sum(crop_sum(x, mask10), axis=0, keepdims=True) / count
        off = x - average[None]
        local[0, pl.ds(j, 1), :] = average
        local[1, pl.ds(j, 1), :] = jnp.sum(crop_sum(off * off, mask10), axis=0, keepdims=True)

    for_tiles(step)


def window(ref, tiles, dy, dx, big):
    pieces = []
    for y in range(7 if big else 3):
        start = big_place(y + dy, dx) if big else small_place(y + dy, dx)
        rows = slice(start, start + (112 if big else 240))
        pieces.append(jnp.concatenate([ref[t, rows, :] for t in tiles], axis=1))
    return jnp.concatenate(pieces, axis=0)


def build_bands(kernel, bands):
    for span, (first, end) in enumerate(WINDOWS):
        base = first * 128
        depth = (end - first) * 128
        lane = lax.broadcasted_iota(jnp.int32, (GROUP_WIDTH, 256), 1) + span * 256
        groups = range(span * 256 // GROUP_WIDTH, min(18, (span * 256 + 255) // GROUP_WIDTH + 1))
        masks = [
            (lane >= g * GROUP_WIDTH) & (lane < (g + 1) * GROUP_WIDTH) for g in groups
        ]
        head = groups[0] * GROUP_WIDTH - base
        tail = depth - head - len(groups) * GROUP_WIDTH
        for tap in range(9):
            piece = kernel[
                tap * GROUP_WIDTH : (tap + 1) * GROUP_WIDTH, span * 256 : span * 256 + 256
            ]
            parts = [jnp.where(m, piece, 0.0) for m in masks]
            if head:
                parts.insert(0, jnp.zeros((head, 256), F32))
            if tail:
                parts.append(jnp.zeros((tail, 256), F32))
            bands[span][:, tap * 256 : tap * 256 + 256] = jnp.concatenate(parts, axis=0).astype(
                BF16
            )


def zero_pads(ref, j):
    for row in ZERO_ROWS:
        ref[j, row : row + 16, :] = jnp.zeros((16, 128), BF16)


def first_kernel(
    n, count, pixels, weight, mask, first, other, stats, local, swap_s, swap_r, send, recv
):
    ch = lax.axis_index("ch")
    wait_all = greet(n)
    own = pl.multiple_of(ch * HALF, 16)
    far = pl.multiple_of((1 - ch) * HALF, 16)
    wait_all()
    chunks = ((0, 384), (384, 384), (768, 384), (1152, 352))
    swaps = []
    for k, (start, size) in enumerate(chunks):
        rows = pl.ds(start, size)
        swaps.append(swap(pixels.at[rows], other.at[rows], swap_s.at[k], swap_r.at[k]))
        swaps[-1].start()
    first[7, :, LAST:128] = jnp.zeros((ROWS, 128 - LAST), F32)
    for t, (a, b) in enumerate(SPANS):
        put_span(first, t, slice(0, ROWS), dot(pixels[...], weight[pl.ds(own, HALF), a:b]))
    for k, (start, size) in enumerate(chunks):
        swaps[k].wait()
        rows = slice(start, start + size)
        for t, (a, b) in enumerate(SPANS):
            put_span(first, t, rows, dot(other[rows, :], weight[pl.ds(far, HALF), a:b]), add=True)
    natural_stats(first, mask, count[0, 0], local)
    gather = Gather(n, local, stats, send, recv)
    gather.start()
    gather.wait()


def group_kernel(
    n,
    count,
    first,
    stats1,
    live,
    norm1,
    mask10,
    kernel,
    weight1,
    weight3,
    padded,
    group,
    stats2,
    far1,
    far3,
    consts,
    local,
    band0,
    band1,
    band2,
    band3,
    swap_s,
    swap_r,
    send,
    recv,
):
    wait_all = greet(n)
    norm_constants(n, stats1, live, norm1, consts)
    wait_all()
    far = pl.multiple_of((1 - lax.axis_index("ch")) * HALF, 16)
    swaps = [
        swap(w.at[pl.ds(far, HALF)], f, swap_s.at[k], swap_r.at[k])
        for k, (w, f) in enumerate(((weight1, far1), (weight3, far3)))
    ]
    for s in swaps:
        s.start()
    bands = (band0, band1, band2, band3)
    build_bands(kernel, bands)

    def step(j):
        average = row_of(consts, 0, j)
        scale = row_of(consts, 1, j) * row_of(consts, 2, j)
        shift = row_of(consts, 3, j)
        zero_pads(padded, j)
        for tile in range(0, ROWS_IMG, 2):
            both = []
            for half in range(2):
                x = first[j, pl.ds(natural_row(tile + half), IMGS, stride=ROWS_IMG), :]
                pre = (x - average) * scale + shift
                both.append(pre * sigmoid(pre))
            row = padded_row(tile)
            padded[j, row : row + 16, :] = jnp.concatenate(both, axis=0).astype(BF16)

    for_tiles(step)
    for span, (start, end) in enumerate(WINDOWS):
        tiles = range(start, end)
        right = jnp.concatenate(
            [bands[span][:, tap * 256 : tap * 256 + 256] for tap in range(9)], axis=0
        )
        for big in (True, False):
            left = jnp.concatenate([window(padded, tiles, dy, dx, big) for dy, dx in TAPS], axis=1)
            rows = slice(0, 784) if big else slice(784, ROWS)
            put_span(group, span, rows, dot(left, right))
    crop_stats(group, mask10, count[0, 0], local)
    gather = Gather(n, local, stats2, send, recv)
    gather.start()
    for s in swaps:
        s.wait()
    gather.wait()


def gate_kernel(
    n,
    count,
    group,
    stats2,
    live,
    norm2,
    mask10,
    inverse,
    squeeze_w,
    squeeze_b,
    excite_w,
    excite_b,
    mask,
    weight,
    scaled,
    scaled_far,
    last,
    stats3,
    pooled,
    pooled_far,
    squeezed,
    squeezed_far,
    squeeze_pre,
    excited,
    consts,
    local,
    act,
    turned,
    swap_s,
    swap_r,
    small_s,
    small_r,
    send,
    recv,
):
    ch = lax.axis_index("ch")
    wait_all = greet(n)
    norm_constants(n, stats2, live, norm2, consts)

    def activate(j):
        average = row_of(consts, 0, j)
        scale = row_of(consts, 1, j) * row_of(consts, 2, j)
        pre = (group[j] - average) * scale + row_of(consts, 3, j)
        value = pre * sigmoid(pre)
        act[j] = value
        pooled[j] = crop_sum(value.reshape(ROWS_IMG, IMGS, 128), mask10) * inverse[...]

    for_tiles(activate)
    wait_all()
    pool_swap = swap(pooled, pooled_far, small_s.at[0], small_r.at[0])
    pool_swap.start()
    pool_swap.wait()
    mine = jnp.concatenate([pooled[j] for j in range(TILES)], axis=1)[:, :HALF]
    theirs = jnp.concatenate([pooled_far[j] for j in range(TILES)], axis=1)[:, :HALF]
    is_low = ch == 0
    pre = (
        dot(jnp.where(is_low, mine, theirs), squeeze_w[0:HALF, :], precision=HIGHEST)
        + dot(jnp.where(is_low, theirs, mine), squeeze_w[HALF:, :], precision=HIGHEST)
        + squeeze_b[...]
    )
    squeeze_pre[...] = pre
    squeezed[...] = pre * sigmoid(pre)
    squeeze_swap = swap(squeezed, squeezed_far, small_s.at[1], small_r.at[1])
    squeeze_swap.start()
    squeeze_swap.wait()
    mine, theirs = squeezed[...], squeezed_far[...]
    width = mine.shape[1]
    gate = sigmoid(
        dot(jnp.where(is_low, mine, theirs), excite_w[0:width, :], precision=HIGHEST)
        + dot(jnp.where(is_low, theirs, mine), excite_w[width:, :], precision=HIGHEST)
        + excite_b[...]
    )
    excited[7] = jnp.zeros((IMGS, 128), F32)
    for j in range(TILES - 1):
        excited[j] = gate[:, j * 128 : j * 128 + 128]
    excited[7, :, 0:LAST] = gate[:, 7 * 128 :]

    def apply(j):
        gate_j = excited[j]
        for tile in range(ROWS_IMG):
            turned[pl.ds(natural_row(tile), IMGS, stride=ROWS_IMG), :] = (
                act[j, tile * 8 : tile * 8 + 8, :] * gate_j
            )
        scaled[j] = turned[...].astype(BF16)
        swap(scaled.at[j], scaled_far.at[j], swap_s.at[j], swap_r.at[j]).start()

    for_tiles(apply)
    own = pl.multiple_of(ch * HALF, 16)
    far = pl.multiple_of((1 - ch) * HALF, 16)
    last[7, :, LAST:128] = jnp.zeros((ROWS, 128 - LAST), F32)
    for t, (a, b) in enumerate(SPANS):
        left = jnp.concatenate([scaled[j] for j in range(TILES)], axis=1)[:, :HALF]
        put_span(last, t, slice(0, ROWS), dot(left, weight[pl.ds(own, HALF), a:b]))
    for_tiles(lambda j: swap(scaled.at[j], scaled_far.at[j], swap_s.at[j], swap_r.at[j]).wait())
    for t, (a, b) in enumerate(SPANS):
        left = jnp.concatenate([scaled_far[j] for j in range(TILES)], axis=1)[:, :HALF]
        put_span(last, t, slice(0, ROWS), dot(left, weight[pl.ds(far, HALF), a:b]), add=True)
    natural_stats(last, mask, count[0, 0], local)
    gather = Gather(n, local, stats3, send, recv)
    gather.start()
    gather.wait()


def merge_kernel(
    n, last, stats3, live, norm3, mask, pixels, output_grad, block, merged_grad, sums3, consts, local, send, recv
):
    wait_all = greet(n, partner=False)
    norm_constants(n, stats3, live, norm3, consts)
    merged_grad[7, :, LAST:128] = jnp.zeros((ROWS, 128 - LAST), F32)
    local[...] = jnp.zeros_like(local)

    def step(j, lanes, width):
        def vec(k):
            return consts[k, pl.ds(j, 1), 0:width]

        m = mask[:, 0:width]
        normed = (last[j, :, 0:width] - vec(0)) * vec(1)
        merged = pixels[:, lanes].astype(F32) + normed * vec(2) + vec(3)
        s = sigmoid(merged)
        block[:, lanes] = (merged * s * m).astype(BF16)
        grad = output_grad[:, lanes].astype(F32) * m * slope_of(merged, s)
        merged_grad[j, :, 0:width] = grad
        local[0, pl.ds(j, 1), 0:width] = jnp.sum(grad, axis=0, keepdims=True)
        local[1, pl.ds(j, 1), 0:width] = jnp.sum(grad * normed, axis=0, keepdims=True)

    for_ragged_tiles(step)
    wait_all()
    gather = Gather(n, local, sums3, send, recv)
    gather.start()
    gather.wait()


def weight_grad(left_tiles, right_tiles, target):
    for a, b in SPANS:
        tiles = range(a // 128, (b + 127) // 128)
        left = jnp.concatenate([left_tiles(t) for t in tiles], axis=1)[:, : b - a]
        for span in range(4):
            right = jnp.concatenate([right_tiles(2 * span), right_tiles(2 * span + 1)], axis=1)
            value = dot(left, right, ((0,), (0,))).astype(BF16)
            target[2 * span, a:b, :] = value[:, :128]
            target[2 * span + 1, a:b, :] = value[:, 128:]


def last_grad_kernel(
    n,
    last,
    stats3,
    live,
    norm3,
    sums3,
    mask,
    merged_grad,
    scaled,
    scaled_far,
    weight,
    weight_far,
    grad_own,
    grad_far,
    scaled_grad,
    vectors,
    consts,
    low,
    low_far,
    swap_s,
    swap_r,
):
    ch = lax.axis_index("ch")
    wait_partner = greet(n, all_images=False)
    norm_constants(n, stats3, live, norm3, consts)
    back_constants(n, sums3, consts, vectors)
    wait_partner()

    def step(j):
        normed = (last[j] - row_of(consts, 0, j)) * row_of(consts, 1, j)
        inner = merged_grad[j] - row_of(consts, 5, j) - normed * row_of(consts, 6, j)
        low[j] = (mask[...] * row_of(consts, 7, j) * inner).astype(BF16)
        swap(low.at[j], low_far.at[j], swap_s.at[j], swap_r.at[j]).start()

    for_tiles(step)
    weight_grad(lambda t: scaled[t], lambda t: low[t], grad_own)
    weight_grad(lambda t: scaled_far[t], lambda t: low[t], grad_far)
    own = pl.multiple_of(ch * HALF, 16)
    scaled_grad[7, :, LAST:128] = jnp.zeros((ROWS, 128 - LAST), F32)
    for t, (a, b) in enumerate(SPANS):
        left = jnp.concatenate([low[j] for j in range(TILES)], axis=1)[:, :HALF]
        right = weight[pl.ds(own + a, b - a), :]
        put_span(scaled_grad, t, slice(0, ROWS), dot(left, right, ((1,), (1,))))
    for_tiles(lambda j: swap(low.at[j], low_far.at[j], swap_s.at[j], swap_r.at[j]).wait())
    for t, (a, b) in enumerate(SPANS):
        left = jnp.concatenate([low_far[j] for j in range(TILES)], axis=1)[:, :HALF]
        put_span(
            scaled_grad,
            t,
            slice(0, ROWS),
            dot(left, weight_far[a:b, :], ((1,), (1,))),
            add=True,
        )


def gate_grad_kernel(
    n,
    scaled_grad,
    group,
    stats2,
    live,
    norm2,
    mask10,
    inverse,
    excited,
    squeeze_pre,
    squeeze_w,
    excite_w,
    pre_grad,
    sums2,
    excite_grad,
    squeeze_grad,
    consts,
    local,
    terms,
    terms_in,
    pool_terms,
    pool_in,
    pool_tiles,
    small_s,
    small_r,
    send,
    recv,
):
    ch = lax.axis_index("ch")
    wait_all = greet(n)
    norm_constants(n, stats2, live, norm2, consts)

    def gate_sum(j):
        average = row_of(consts, 0, j)
        scale = row_of(consts, 1, j) * row_of(consts, 2, j)
        shift = row_of(consts, 3, j)
        total = jnp.zeros((IMGS, 128), F32)
        for tile in range(ROWS_IMG):
            pre = (group[j, tile * 8 : tile * 8 + 8, :] - average) * scale + shift
            act = pre * sigmoid(pre)
            total = total + act * scaled_grad[j, pl.ds(natural_row(tile), IMGS, stride=ROWS_IMG), :]
        gate = excited[j]
        excite_grad[j] = total * gate * (1.0 - gate)

    for_tiles(gate_sum)
    wide = jnp.concatenate([excite_grad[j] for j in range(TILES)], axis=1)[:, :HALF]
    width = squeeze_w.shape[1]
    is_low = ch == 0
    part0 = dot(wide, excite_w[0:width, :], ((1,), (1,)), precision=HIGHEST)
    part1 = dot(wide, excite_w[width:, :], ((1,), (1,)), precision=HIGHEST)
    terms[...] = jnp.where(is_low, part1, part0)
    wait_all()
    term_swap = swap(terms, terms_in, small_s.at[0], small_r.at[0])
    term_swap.start()
    term_swap.wait()
    pre = squeeze_pre[...]
    grad = (jnp.where(is_low, part0, part1) + terms_in[...]) * slope_of(pre, sigmoid(pre))
    squeeze_grad[...] = grad
    pool0 = dot(grad, squeeze_w[0:HALF, :], ((1,), (1,)), precision=HIGHEST)
    pool1 = dot(grad, squeeze_w[HALF:, :], ((1,), (1,)), precision=HIGHEST)
    pool_terms[...] = jnp.where(is_low, pool1, pool0)
    pool_swap = swap(pool_terms, pool_in, small_s.at[1], small_r.at[1])
    pool_swap.start()
    pool_swap.wait()
    pool = jnp.where(is_low, pool0, pool1) + pool_in[...]
    for j in range(TILES):
        part = pool[:, j * 128 : min(HALF, j * 128 + 128)]
        pool_tiles[j, :, 0 : part.shape[1]] = part * inverse[:, 0 : part.shape[1]]

    def grads(j):
        average, scale = row_of(consts, 0, j), row_of(consts, 1, j)
        gain, shift = row_of(consts, 2, j), row_of(consts, 3, j)
        gate, pooled = excited[j], pool_tiles[j]
        total = jnp.zeros((IMGS, 128), F32)
        total_normed = jnp.zeros((IMGS, 128), F32)
        for tile in range(ROWS_IMG):
            rows = slice(tile * 8, tile * 8 + 8)
            normed = (group[j, rows, :] - average) * scale
            pre = normed * gain + shift
            lead = pooled if tile < BIG_ROWS else pooled * mask10[(tile - BIG_ROWS) % 10]
            act = scaled_grad[j, pl.ds(natural_row(tile), IMGS, stride=ROWS_IMG), :] * gate + lead
            grad = act * slope_of(pre, sigmoid(pre))
            pre_grad[j, rows, :] = grad
            total = total + grad
            total_normed = total_normed + grad * normed
        local[0, pl.ds(j, 1), :] = jnp.sum(total, axis=0, keepdims=True)
        local[1, pl.ds(j, 1), :] = jnp.sum(total_normed, axis=0, keepdims=True)

    pool_tiles[7, :, LAST:128] = jnp.zeros((IMGS, 128 - LAST), F32)
    for_tiles(grads)
    gather = Gather(n, local, sums2, send, recv)
    gather.start()
    gather.wait()


def group_grad_kernel(
    n,
    pre_grad,
    group,
    stats2,
    live,
    norm2,
    sums2,
    mask10,
    kernel,
    padded,
    first,
    stats1,
    norm1,
    kernel_grad,
    first_pre_grad,
    sums1,
    vectors,
    consts,
    consts1,
    local,
    padded_grad,
    band0,
    band1,
    band2,
    band3,
    full,
    send,
    recv,
):
    wait_all = greet(n, partner=False)
    norm_constants(n, stats2, live, norm2, consts)
    back_constants(n, sums2, consts, vectors)
    norm_constants(n, stats1, live, norm1, consts1)
    bands = (band0, band1, band2, band3)
    build_bands(kernel, bands)

    def step(j):
        average, scale = row_of(consts, 0, j), row_of(consts, 1, j)
        less, slope, front = row_of(consts, 5, j), row_of(consts, 6, j), row_of(consts, 7, j)
        zero_pads(padded_grad, j)
        for tile in range(0, ROWS_IMG, 2):
            both = []
            for half in range(2):
                rows = slice(tile * 8 + half * 8, tile * 8 + half * 8 + 8)
                normed = (group[j, rows, :] - average) * scale
                grad = front * (pre_grad[j, rows, :] - less - normed * slope)
                if tile >= BIG_ROWS:
                    grad = grad * mask10[(tile + half - BIG_ROWS) % 10]
                both.append(grad)
            row = padded_row(tile)
            padded_grad[j, row : row + 16, :] = jnp.concatenate(both, axis=0).astype(BF16)

    for_tiles(step)
    started = 0
    for span, (start, end) in enumerate(WINDOWS):
        tiles = (2 * span, 2 * span + 1)
        shifted = [
            jnp.concatenate([window(padded_grad, tiles, -dy, -dx, big) for dy, dx in TAPS], axis=1)
            for big in (True, False)
        ]
        for rows, left in ((slice(0, 784), shifted[0]), (slice(784, ROWS), shifted[1])):
            value = dot(left, bands[span][...], ((1,), (1,)))
            for t in range(start, end):
                part = value[:, (t - start) * 128 : (t - start) * 128 + 128]
                if t < started:
                    first_pre_grad[t, rows, :] += part
                else:
                    first_pre_grad[t, rows, :] = part
        started = end
        right = jnp.concatenate(shifted, axis=0)
        for t in range(start, end, 2):
            pair = range(t, min(t + 2, end))
            left = jnp.concatenate([window(padded, pair, 0, 0, big) for big in (True, False)], axis=0)
            base = (t - start) * 128
            full[base : base + 128 * len(pair), :] = dot(left, right, ((0,), (0,)))
        lane = lax.broadcasted_iota(jnp.int32, (GROUP_WIDTH, 256), 1) + span * 256
        pieces = []
        for tap in range(9):
            piece = jnp.zeros((GROUP_WIDTH, 256), F32)
            for g in range(span * 256 // GROUP_WIDTH, min(18, (span * 256 + 255) // GROUP_WIDTH + 1)):
                row = g * GROUP_WIDTH - start * 128
                inside = (lane >= g * GROUP_WIDTH) & (lane < (g + 1) * GROUP_WIDTH)
                block = full[row : row + GROUP_WIDTH, tap * 256 : tap * 256 + 256]
                piece = jnp.where(inside, block, piece)
            pieces.append(piece)
        pieces.append(jnp.zeros((8, 256), F32))
        value = jnp.concatenate(pieces, axis=0).astype(BF16)
        kernel_grad[2 * span] = value[:, :128]
        kernel_grad[2 * span + 1] = value[:, 128:]

    def slopes(j):
        average, scale = row_of(consts1, 0, j), row_of(consts1, 1, j)
        gain, shift = row_of(consts1, 2, j), row_of(consts1, 3, j)
        total = jnp.zeros((IMGS, 128), F32)
        total_normed = jnp.zeros((IMGS, 128), F32)
        for tile in range(ROWS_IMG):
            rows = slice(tile * 8, tile * 8 + 8)
            x = first[j, pl.ds(natural_row(tile), IMGS, stride=ROWS_IMG), :]
            normed = (x - average) * scale
            pre = normed * gain + shift
            grad = first_pre_grad[j, rows, :] * slope_of(pre, sigmoid(pre))
            if tile >= BIG_ROWS:
                grad = grad * mask10[(tile - BIG_ROWS) % 10]
            first_pre_grad[j, rows, :] = grad
            total = total + grad
            total_normed = total_normed + grad * normed
        local[0, pl.ds(j, 1), :] = jnp.sum(total, axis=0, keepdims=True)
        local[1, pl.ds(j, 1), :] = jnp.sum(total_normed, axis=0, keepdims=True)

    for_tiles(slopes)
    wait_all()
    gather = Gather(n, local, sums1, send, recv)
    gather.start()
    gather.wait()


def first_grad_kernel(
    n,
    pre_grad,
    first,
    stats1,
    live,
    norm1,
    sums1,
    mask10,
    pixels,
    pixels_far,
    weight,
    weight_far,
    merged_grad,
    grad_own,
    grad_far,
    pixels_grad,
    vectors,
    consts,
    low,
    low_far,
    turned,
    swap_s,
    swap_r,
):
    ch = lax.axis_index("ch")
    wait_partner = greet(n, all_images=False)
    norm_constants(n, stats1, live, norm1, consts)
    back_constants(n, sums1, consts, vectors)
    wait_partner()

    def step(j):
        average, scale = row_of(consts, 0, j), row_of(consts, 1, j)
        less, slope, front = row_of(consts, 5, j), row_of(consts, 6, j), row_of(consts, 7, j)
        for tile in range(ROWS_IMG):
            there = pl.ds(natural_row(tile), IMGS, stride=ROWS_IMG)
            normed = (first[j, there, :] - average) * scale
            grad = front * (pre_grad[j, tile * 8 : tile * 8 + 8, :] - less - normed * slope)
            if tile >= BIG_ROWS:
                grad = grad * mask10[(tile - BIG_ROWS) % 10]
            turned[there, :] = grad
        low[j] = turned[...].astype(BF16)
        swap(low.at[j], low_far.at[j], swap_s.at[j], swap_r.at[j]).start()

    for_tiles(step)
    weight_grad(lambda t: pixels[:, t * 128 : min(HALF, t * 128 + 128)], lambda t: low[t], grad_own)
    weight_grad(
        lambda t: pixels_far[:, t * 128 : min(HALF, t * 128 + 128)], lambda t: low[t], grad_far
    )
    own = pl.multiple_of(ch * HALF, 16)
    for t, (a, b) in enumerate(SPANS):
        left = jnp.concatenate([low[j] for j in range(TILES)], axis=1)[:, :HALF]
        value = dot(left, weight[pl.ds(own + a, b - a), :], ((1,), (1,)))
        more = jnp.concatenate([merged_grad[2 * t], merged_grad[2 * t + 1]], axis=1)[:, : b - a]
        pixels_grad[:, a:b] = value + more
    for_tiles(lambda j: swap(low.at[j], low_far.at[j], swap_s.at[j], swap_r.at[j]).wait())
    for t, (a, b) in enumerate(SPANS):
        left = jnp.concatenate([low_far[j] for j in range(TILES)], axis=1)[:, :HALF]
        pixels_grad[:, a:b] += dot(left, weight_far[a:b, :], ((1,), (1,)))


def image_axes(n):
    return {16: (2, 2, 4), 128: (8, 4, 4)}.get(n, (n, 1, 1))


class Part:
    def __init__(self, n, order, source, result, room, sems):
        sizes = image_axes(n)
        strides = (1, sizes[0], sizes[0] * sizes[1])
        self.n, self.me = n, lax.axis_index("img")
        self.sizes = [sizes[a] for a in order]
        self.strides = [strides[a] for a in order]
        self.place = [lax.rem(self.me // s, e) for s, e in zip(self.strides, self.sizes)]
        self.source, self.result, self.room, self.sems = source, result, room, sems
        self.reduces = source is not None
        self.live = []

    def send(self, axis, stage, source, target):
        for d in range(1, self.sizes[axis]):
            q = lax.rem(self.place[axis] + d, self.sizes[axis])
            peer = self.me + (q - self.place[axis]) * self.strides[axis]
            copy = pltpu.make_async_remote_copy(
                src_ref=source(q),
                dst_ref=target(d),
                send_sem=self.sems[0].at[stage, d],
                recv_sem=self.sems[1].at[stage, d],
                device_id={"img": peer},
                device_id_type=MESH,
            )
            copy.start()
            self.live.append(copy)

    def settle(self):
        for copy in self.live:
            copy.wait()
        self.live = []

    def add(self, target, own, arrived, count):
        total = own[...].astype(F32)
        for d in range(1, count):
            total = total + arrived[d - 1][...].astype(F32)
        target[...] = total.astype(BF16)

    def step(self, stage):
        r0, r1, r2, a0, a1 = self.room if self.reduces else (None,) * 5
        p0, p1, p2 = self.place
        if stage == 0 and self.reduces:
            self.send(0, 0, lambda q: self.source.at[q], lambda d: r0.at[d - 1])
        elif stage == 1 and self.reduces:
            self.settle()
            for k in range(self.sizes[1]):
                self.add(
                    a0.at[k], self.source.at[p0, k], [r0.at[d, k] for d in range(self.sizes[0] - 1)], self.sizes[0]
                )
            self.send(1, 1, lambda q: a0.at[q], lambda d: r1.at[d - 1])
        elif stage == 2 and self.reduces:
            self.settle()
            self.add(a1, a0.at[p1], [r1.at[d] for d in range(self.sizes[1] - 1)], self.sizes[1])
            self.send(2, 2, lambda q: a1.at[q], lambda d: r2.at[d - 1])
        elif stage == 3:
            if self.reduces:
                self.settle()
                self.add(
                    self.result.at[p0, p1, p2], a1.at[p2], [r2.at[d] for d in range(self.sizes[2] - 1)], self.sizes[2]
                )
            block = self.result.at[p0, p1, p2]
            self.send(2, 3, lambda q: block, lambda d: block)
        elif stage == 4:
            self.settle()
            block = self.result.at[p0, p1]
            self.send(1, 4, lambda q: block, lambda d: block)
        elif stage == 5:
            self.settle()
            block = self.result.at[p0]
            self.send(0, 5, lambda q: block, lambda d: block)
        elif stage == 6:
            self.settle()

    @staticmethod
    def scratch(n, order, shape, reduces):
        sizes = [image_axes(n)[a] for a in order]
        most = max(sizes)
        sems = [DMA((6, most)), DMA((6, most))]
        if not reduces:
            return sems
        e0, e1, e2, rows, lanes = shape
        room = [
            (max(e0 - 1, 1), e1, e2, rows, lanes),
            (max(e1 - 1, 1), e2, rows, lanes),
            (max(e2 - 1, 1), rows, lanes),
            (e1, e2, rows, lanes),
            (e2, rows, lanes),
        ]
        return [pltpu.VMEM(s, BF16) for s in room] + sems


def settle_kernel(n, orders, reduces, *refs):
    count = len(orders)
    sources, refs = refs[:count], refs[count:]
    results, refs = refs[:count], refs[count:]
    wait_all = greet(n, partner=False)
    parts = []
    for order, reduce, source, result in zip(orders, reduces, sources, results):
        size = 7 if reduce else 2
        own, refs = refs[:size], refs[size:]
        part = Part(n, order, source if reduce else None, result, own[:5], own[-2:])
        if not reduce:
            p0, p1, p2 = part.place
            result[p0, p1, p2] = source[...]
        parts.append(part)
    wait_all()
    ticks = 7 + (count + 1) // 2
    for tick in range(ticks):
        for k, part in enumerate(parts):
            stage = tick - k // 2
            if 0 <= stage <= 6:
                part.step(stage)


def spread_kernel(own, far, out):
    ch = lax.axis_index("ch")
    for source, place in ((own, ch), (far, 1 - ch)):
        rows = pl.ds(pl.multiple_of(place * HALF, 8), HALF)
        for j in range(TILES):
            width = 128 if j < 7 else LAST
            out[rows, j * 128 : j * 128 + width] = source[j, 0:HALF, 0:width].astype(F32)


def finish_kernel(low_half, high_half, factors, group_out, squeeze_w, squeeze_b, excite_w, excite_b):
    ch = lax.axis_index("ch")
    se = squeeze_w.shape[1]
    split = low_half.shape[1]
    for j in range(TILES):
        width = 128 if j < 7 else LAST
        lanes = slice(j * 128, j * 128 + width)
        group_out[0:split, lanes] = low_half[j, :, 0:width].astype(F32)
        rest = 9 * GROUP_WIDTH - split
        group_out[split:, lanes] = high_half[j, :, 0:width].astype(F32)[:rest]
    n = factors.shape[0]
    whole = factors[...].astype(F32).reshape(n, -1, IMGS, 128)

    def columns(start, tiles, width):
        parts = [whole[:, t].reshape(n * IMGS, 128) for t in range(start, start + tiles)]
        return jnp.concatenate(parts, axis=1)[:, :width]

    excite_all, squeeze_all = columns(16, 8, HALF), columns(28, 2, se)
    squeeze_b[...] = jnp.sum(squeeze_all, axis=0, keepdims=True)
    excite_b[...] = jnp.sum(excite_all, axis=0, keepdims=True)
    excite_all, squeeze_all = excite_all.astype(BF16), squeeze_all.astype(BF16)
    for start, place in ((0, ch), (8, 1 - ch)):
        rows = pl.ds(pl.multiple_of(place * HALF, 8), HALF)
        squeeze_w[rows, :] = dot(columns(start, 8, HALF).astype(BF16), squeeze_all, ((0,), (0,)))
    own, far = columns(24, 2, se), columns(26, 2, se)
    for k, left in enumerate((jnp.where(ch == 0, own, far), jnp.where(ch == 0, far, own))):
        excite_w[k * se : (k + 1) * se, :] = dot(left.astype(BF16), excite_all, ((0,), (0,)))


def call(kernel, ins, outs, scratch, ident=None, in_specs=None, out_specs=None):
    params = {"vmem_limit_bytes": VMEM_LIMIT}
    if ident is not None:
        params.update(collective_id=ident, has_side_effects=True)
    return pl.pallas_call(
        kernel,
        out_shape=[jax.ShapeDtypeStruct(shape, dtype) for shape, dtype in outs],
        in_specs=in_specs or [VMEM] * len(ins),
        out_specs=out_specs or [VMEM] * len(outs),
        scratch_shapes=scratch,
        compiler_params=pltpu.CompilerParams(**params),
    )(*ins)


def lane_tiles(vector):
    return jnp.pad(vector, (0, 1024 - HALF)).reshape(TILES, 128)


def body(
    n,
    pixels,
    crop_counts,
    first_weight,
    first_gain,
    first_shift,
    group_weight,
    group_gain,
    group_shift,
    squeeze_weight,
    squeeze_bias,
    excite_weight,
    excite_bias,
    last_weight,
    last_gain,
    last_shift,
    output_grad,
):
    me = lax.axis_index("img")
    assert pixels.shape == (ROWS, HALF)
    se = squeeze_weight.shape[1]
    wide = (TILES, ROWS, 128)
    stat = (n, 2, TILES, 128)
    sem = DMA((n - 1,))

    local_counts = lax.dynamic_slice_in_dim(crop_counts, me * IMGS, IMGS)
    places = jnp.arange(ROWS_IMG, dtype=jnp.int32)
    living = (places[None, :] < BIG_ROWS) | (
        (places[None, :] - BIG_ROWS) // 9 < local_counts[:, None]
    )
    mask = jnp.broadcast_to(living.reshape(ROWS, 1).astype(F32), (ROWS, 128))
    slots = jnp.arange(10, dtype=jnp.int32)[:, None] < local_counts[None, :]
    mask10 = jnp.broadcast_to(slots[:, :, None].astype(F32), (10, IMGS, 128))
    per_image = (BIG_ROWS + 9 * crop_counts).astype(F32)
    live = jnp.sum(per_image.reshape(n, IMGS), axis=1)
    count = lax.dynamic_slice_in_dim(live, me, 1).reshape(1, 1)
    live = jnp.broadcast_to(live[:, None, None], (n, TILES, 128))
    inverse = 1.0 / (BIG_ROWS + 9 * local_counts).astype(F32)
    inverse = jnp.broadcast_to(inverse[:, None], (IMGS, 128))
    norm1, norm2, norm3 = (
        jnp.stack([lane_tiles(gain), lane_tiles(shift)])
        for gain, shift in (
            (first_gain, first_shift),
            (group_gain, group_shift),
            (last_gain, last_shift),
        )
    )
    kernel = jnp.pad(
        group_weight.reshape(9 * GROUP_WIDTH, HALF).astype(F32), ((0, 0), (0, 1024 - HALF))
    )
    local = pltpu.VMEM((2, TILES, 128), F32)
    consts = pltpu.VMEM((8, TILES, 128), F32)
    vectors = ((2, TILES, 128), F32)
    bands = [pltpu.VMEM(((e - s) * 128, 9 * 256), BF16) for s, e in WINDOWS]
    smem = pl.BlockSpec(memory_space=pltpu.SMEM)

    first, pixels_far, stats1 = call(
        functools.partial(first_kernel, n),
        (count, pixels, first_weight, mask),
        [(wide, F32), ((ROWS, HALF), BF16), (stat, F32)],
        [local, DMA((4,)), DMA((4,)), sem, sem],
        0,
        in_specs=[smem, VMEM, VMEM, VMEM],
    )
    padded, group, stats2, first_far, last_far = call(
        functools.partial(group_kernel, n),
        (count, first, stats1, live, norm1, mask10, kernel, first_weight, last_weight),
        [
            ((TILES, PAD_ROWS, 128), BF16),
            (wide, F32),
            (stat, F32),
            ((HALF, HALF), BF16),
            ((HALF, HALF), BF16),
        ],
        [consts, local, *bands, DMA((2,)), DMA((2,)), sem, sem],
        1,
        in_specs=[smem] + [VMEM] * 6 + [ANY] * 2,
        out_specs=[VMEM] * 3 + [ANY] * 2,
    )
    small = (TILES, IMGS, 128)
    (
        scaled,
        scaled_far,
        last,
        stats3,
        pooled,
        pooled_far,
        squeezed,
        squeezed_far,
        squeeze_pre,
        excited,
    ) = call(
        functools.partial(gate_kernel, n),
        (
            count,
            group,
            stats2,
            live,
            norm2,
            mask10,
            inverse,
            squeeze_weight,
            squeeze_bias[None],
            excite_weight,
            excite_bias[None],
            mask,
            last_weight,
        ),
        [
            (wide, BF16),
            (wide, BF16),
            (wide, F32),
            (stat, F32),
            (small, F32),
            (small, F32),
            ((IMGS, se), F32),
            ((IMGS, se), F32),
            ((IMGS, se), F32),
            (small, F32),
        ],
        [
            consts,
            local,
            pltpu.VMEM(wide, F32),
            pltpu.VMEM((ROWS, 128), F32),
            DMA((TILES,)),
            DMA((TILES,)),
            DMA((2,)),
            DMA((2,)),
            sem,
            sem,
        ],
        2,
        in_specs=[smem] + [VMEM] * 12,
    )
    block_out, merged_grad, sums3 = call(
        functools.partial(merge_kernel, n),
        (last, stats3, live, norm3, mask, pixels, output_grad),
        [((ROWS, HALF), BF16), (wide, F32), (stat, F32)],
        [consts, local, sem, sem],
        3,
    )
    half_grad = ((TILES, 1024, 128), BF16)
    last_grad_own, last_grad_far, scaled_grad, vectors3 = call(
        functools.partial(last_grad_kernel, n),
        (
            last,
            stats3,
            live,
            norm3,
            sums3,
            mask,
            merged_grad,
            scaled,
            scaled_far,
            last_weight,
            last_far,
        ),
        [half_grad, half_grad, (wide, F32), vectors],
        [
            consts,
            pltpu.VMEM(wide, BF16),
            pltpu.VMEM(wide, BF16),
            DMA((TILES,)),
            DMA((TILES,)),
        ],
        4,
    )
    pre_grad, sums2, excite_grad, squeeze_grad = call(
        functools.partial(gate_grad_kernel, n),
        (
            scaled_grad,
            group,
            stats2,
            live,
            norm2,
            mask10,
            inverse,
            excited,
            squeeze_pre,
            squeeze_weight,
            excite_weight,
        ),
        [(wide, F32), (stat, F32), (small, F32), ((IMGS, se), F32)],
        [
            consts,
            local,
            pltpu.VMEM((IMGS, se), F32),
            pltpu.VMEM((IMGS, se), F32),
            pltpu.VMEM((IMGS, HALF), F32),
            pltpu.VMEM((IMGS, HALF), F32),
            pltpu.VMEM(small, F32),
            DMA((2,)),
            DMA((2,)),
            sem,
            sem,
        ],
        5,
    )
    kernel_grad, first_pre_grad, sums1, vectors2 = call(
        functools.partial(group_grad_kernel, n),
        (
            pre_grad,
            group,
            stats2,
            live,
            norm2,
            sums2,
            mask10,
            kernel,
            padded,
            first,
            stats1,
            norm1,
        ),
        [((TILES, 512, 128), BF16), (wide, F32), (stat, F32), vectors],
        [
            consts,
            consts,
            local,
            pltpu.VMEM((TILES, PAD_ROWS, 128), BF16),
            *bands,
            pltpu.VMEM((512, 9 * 256), F32),
            sem,
            sem,
        ],
        6,
    )
    first_grad_own, first_grad_far, pixels_grad, vectors1 = call(
        functools.partial(first_grad_kernel, n),
        (
            first_pre_grad,
            first,
            stats1,
            live,
            norm1,
            sums1,
            mask10,
            pixels,
            pixels_far,
            first_weight,
            first_far,
            merged_grad,
        ),
        [half_grad, half_grad, ((ROWS, HALF), F32), vectors],
        [
            consts,
            pltpu.VMEM(wide, BF16),
            pltpu.VMEM(wide, BF16),
            pltpu.VMEM((ROWS, 128), F32),
            DMA((TILES,)),
            DMA((TILES,)),
        ],
        7,
    )

    def tiles_of(value):
        return jnp.pad(value, ((0, 0), (0, 256 - se))).reshape(IMGS, 2, 128).swapaxes(0, 1)

    factors = jnp.concatenate(
        [
            pooled,
            pooled_far,
            excite_grad,
            tiles_of(squeezed),
            tiles_of(squeezed_far),
            tiles_of(squeeze_grad),
        ]
    )
    count_tiles = factors.shape[0]
    factors = factors.reshape(count_tiles * IMGS, 128).astype(BF16)

    sizes = image_axes(n)
    forth, back = (0, 1, 2), (1, 0, 2)

    def split(array, order):
        rows = array.shape[0] * array.shape[1]
        return array.reshape(*(sizes[a] for a in order), rows // n, 128)

    half = kernel_grad.shape[1] // 2
    sources = [
        split(last_grad_own, forth),
        split(last_grad_far, back),
        split(first_grad_own, forth),
        split(first_grad_far, back),
        split(kernel_grad[:, :half], forth),
        split(kernel_grad[:, half:], back),
        factors,
    ]
    orders = (forth, back, forth, back, forth, back, forth)
    reduces = (True,) * 6 + (False,)
    shapes = [s.shape for s in sources[:-1]] + [sizes + factors.shape]
    scratch = []
    for order, shape, reduce in zip(orders, shapes, reduces):
        scratch.extend(Part.scratch(n, order, shape, reduce))
    results = call(
        functools.partial(settle_kernel, n, orders, reduces),
        sources,
        [(shape, BF16) for shape in shapes],
        scratch,
        8,
    )
    grads = [r.reshape(TILES, -1, 128) for r in results[:-1]]

    def spread(own, far):
        return call(spread_kernel, (own, far), [((2 * HALF, HALF), F32)], [])[0]

    last_weight_grad = spread(grads[0], grads[1])
    first_weight_grad = spread(grads[2], grads[3])
    group_weight_grad, squeeze_weight_grad, squeeze_bias_grad, excite_weight_grad, excite_bias_grad = call(
        finish_kernel,
        (grads[4], grads[5], results[-1].reshape(n, count_tiles * IMGS, 128)),
        [
            ((9 * GROUP_WIDTH, HALF), F32),
            ((2 * HALF, se), F32),
            ((1, se), F32),
            ((2 * se, HALF), F32),
            ((1, HALF), F32),
        ],
        [],
    )
    group_weight_grad = group_weight_grad.reshape(3, 3, GROUP_WIDTH, HALF)
    squeeze_bias_grad, excite_bias_grad = squeeze_bias_grad[0], excite_bias_grad[0]

    def pair(vector):
        flat = vector.reshape(2, 1024)[:, :HALF]
        return flat[0], flat[1]

    first_gain_grad, first_shift_grad = pair(vectors1)
    group_gain_grad, group_shift_grad = pair(vectors2)
    last_gain_grad, last_shift_grad = pair(vectors3)
    return (
        block_out,
        pixels_grad,
        first_weight_grad,
        first_gain_grad,
        first_shift_grad,
        group_weight_grad,
        group_gain_grad,
        group_shift_grad,
        squeeze_weight_grad,
        squeeze_bias_grad,
        excite_weight_grad,
        excite_bias_grad,
        last_weight_grad,
        last_gain_grad,
        last_shift_grad,
    )


def solution(mesh):
    wide = P("img", "ch")
    matrix, vector = P(None, "ch"), P("ch")
    cube = P(None, None, None, "ch")
    weights = (matrix, vector, vector, cube, vector, vector, matrix, vector, matrix, vector, matrix, vector, vector)
    return jax.shard_map(
        functools.partial(body, mesh.shape["img"]),
        mesh=mesh,
        in_specs=(wide, P(), *weights, wide),
        out_specs=(wide, wide, *weights),
        check_vma=False,
    )
```

time: 2650 us -> 511 us (0.19)
  blocking collectives: 1290 us -> 0 us
  local copies, waits for them, and re-layouts: 606 us -> 18.6 us
  Pallas kernels: 0 us -> 474 us
  waiting for transfers between devices: 341 us -> 0 us
  matrix products: 255 us -> 0 us
  other arithmetic: 119 us -> 9.88 us
    unnamed x2 -> x0, blocking collectives: 953 us -> none
    pallas_call x0 -> x12, Pallas kernels: none -> 474 us  [call(): pl.pallas_call(kernel, out_shape=[jax.ShapeDtypeStruct(shape, dtype) for...]
    psum x9 -> x0, blocking collectives: 331 us -> none  [the longest x3 122 us: normalize(): lax.psum(jnp.sum(row_mask * centred * centred, axis=0), 'img') / live_total]
    unnamed x10 -> x0, waiting for transfers between devices: 313 us -> none
    dot_general x65 -> x0, matrix products: 246 us -> none  [the longest x18 99.1 us: tap_forward(): jnp.einsum('nyxgi,igj->nyxgj', window, blocks[row_tap, column_tap], prefe...]
    concatenate x2 -> x1, local copies, waits for them, and re-layouts: 184 us -> 0.01 us  [body(): jnp.concatenate([pooled, pooled_far, excite_grad, tiles_of(squeezed), til...]
    reshape x17 -> x1, local copies, waits for them, and re-layouts: 109 us -> 0.08 us  [body(): live = jnp.sum(per_image.reshape(n, IMGS), axis=1)]
    slice x16 -> x4, local copies, waits for them, and re-layouts: 91.7 us -> 2.88 us  [the longest x3 1.81 us: pair(): return (flat[0], flat[1])]
  transfers between devices with their start and end apart: 6 -> 0, of which waited for: 4 -> 0; matrix products, arithmetic and copies ran while one was open for 4% -> 0% of each run, Pallas kernels for 0% -> 0%
where the time goes in v1:
time: 511 us; the launch traced here: 503 us
  Pallas kernels  474 us (93%)
  local copies, waits for them, and re-layouts  18.6 us (4%)
  other arithmetic  9.88 us (2%)
    pallas_call x12, Pallas kernels, call(): pl.pallas_call(kernel, out_shape=[jax.ShapeDtypeStruct(shape, dtype) for...  474 us

profile of v1, /device:TPU:10, one launch (start us, length us, event | category | flops | bytes accessed | tf_op | source)
XLA Modules:
  0.0 503.4 jit_solution(16680952713446868054)
XLA Ops:
  1.3 0.7 convert_divide_fusion
  6.3 0.7 pad_bitcast_fusion
  8.3 0.7 broadcast_in_dim.13.live
  9.0 1.1 broadcast_in_dim.12.mask
  10.2 2.8 pad_convert_fusion.kernel
  12.9 27.1 %shard_map.271 = (f32[8,1504,128]{2,1,0:T(8,128)}, bf16[1504,1008]{1,0:T(8,128)(2,1)}, f32[16,2,8,128]{3,2,1,0:T(8,128)}) custom-call(f32[1,1]{1,0:T(1,128)} %bitcast.count, bf16[1504,1008]{1,0:T(8,128)(2,1)} %pixels.5, bf16[2016,1008]{1,0:T(8,128)(2,1)} %weight.7, f32[1504,128]{1,0:T(8,128)} %broadcast_in_dim.12.mask), custom_call_target="tpu_custom_call" | custom-call | tf_op jit(solution)/shard_map/pallas_call | solution.py:1000
  40.0 34.4 %shard_map.272 = (bf16[8,2848,128]{2,1,0:T(8,128)(2,1)}, f32[8,1504,128]{2,1,0:T(8,128)}, f32[16,2,8,128]{3,2,1,0:T(8,128)}, bf16[1008,1008]{1,0:T(8,128)(2,1)}, bf16[1008,1008]{1,0:T(8,128)(2,1)}) custom-call(f32[1,1]{1,0:T(1,128)} %bitcast.count, f32[8,1504,128]{2,1,0:T(8,128)} %get-tuple-element.64.first, f32[16,2,8,128]{3,2,1,0:T(8,128)} %get-tuple-element.65.stats1, ...), custom_call_target="tpu_custom_call" | custom-call | tf_op jit(solution)/shard_map/pallas_call | solution.py:1000
  74.5 37.8 %shard_map.273 = (bf16[8,1504,128]{2,1,0:T(8,128)(2,1)}, bf16[8,1504,128]{2,1,0:T(8,128)(2,1)}, f32[8,1504,128]{2,1,0:T(8,128)}, f32[16,2,8,128]{3,2,1,0:T(8,128...) custom-call(f32[1,1]{1,0:T(1,128)} %bitcast.count, ...), custom_call_target="tpu_custom_call" | custom-call | tf_op jit(solution)/shard_map/pallas_call | solution.py:1000
  113.7 0.8 convert_dynamic-update-slice_fusion.2
  114.5 0.8 convert_dynamic-update-slice_fusion.1
  115.2 19.8 %shard_map.274 = (bf16[1504,1008]{1,0:T(8,128)(2,1)}, f32[8,1504,128]{2,1,0:T(8,128)}, f32[16,2,8,128]{3,2,1,0:T(8,128)}) custom-call(f32[8,1504,128]{2,1,0:T(8,128)} %get-tuple-element.68.last, f32[16,2,8,128]{3,2,1,0:T(8,128)} %get-tuple-element.69.stats3, f32[16,8,128]{2,1,0:T(8,128)} %broadcast_in_dim.13.live, f32[2,8,128]{2,1,0:T(8,128)} %pad_maximum_fusion.2.norm3, ...), custom_call_target="tpu_custom_call" | custom-call | tf_op jit(solution)/shard_map/pallas_call | solution.py:1000
  135.1 27.1 %shard_map.275 = (bf16[8,1024,128]{2,1,0:T(8,128)(2,1)}, bf16[8,1024,128]{2,1,0:T(8,128)(2,1)}, f32[8,1504,128]{2,1,0:T(8,128)}, f32[2,8,128]{2,1,0:T(8,128)}) custom-call(f32[8,1504,128]{2,1,0:T(8,128)} %get-tuple-element.68.last, f32[16,2,8,128]{3,2,1,0:T(8,128)} %get-tuple-element.69.stats3, f32[16,8,128]{2,1,0:T(8,128)} %broadcast_in_dim.13.live, ...), custom_call_target="tpu_custom_call" | custom-call | tf_op jit(solution)/shard_map/pallas_call | solution.py:1000
  163.4 25.8 %shard_map.276 = (f32[8,1504,128]{2,1,0:T(8,128)}, f32[16,2,8,128]{3,2,1,0:T(8,128)}, f32[8,8,128]{2,1,0:T(8,128)}, f32[8,252]{1,0:T(8,128)}) custom-call(f32[8,1504,128]{2,1,0:T(8,128)} %get-tuple-element.76.scaled_grad, f32[8,1504,128]{2,1,0:T(8,128)} %get-tuple-element.66.group, f32[16,2,8,128]{3,2,1,0:T(8,128)} %get-tuple-element.67.stats2, ...), custom_call_target="tpu_custom_call" | custom-call | tf_op jit(solution)/shard_map/pallas_call | solution.py:1000
  189.2 0.8 convert_dynamic-update-slice_fusion
  190.0 51.7 %shard_map.277 = (bf16[8,512,128]{2,1,0:T(8,128)(2,1)}, f32[8,1504,128]{2,1,0:T(8,128)}, f32[16,2,8,128]{3,2,1,0:T(8,128)}, f32[2,8,128]{2,1,0:T(8,128)}) custom-call(f32[8,1504,128]{2,1,0:T(8,128)} %get-tuple-element.79.pre_grad, f32[8,1504,128]{2,1,0:T(8,128)} %get-tuple-element.66.group, f32[16,2,8,128]{3,2,1,0:T(8,128)} %get-tuple-element.67.stats2, ...), custom_call_target="tpu_custom_call" | custom-call | tf_op jit(solution)/shard_map/pallas_call | solution.py:1000
  241.7 28.6 %shard_map.278 = (bf16[8,1024,128]{2,1,0:T(8,128)(2,1)}, bf16[8,1024,128]{2,1,0:T(8,128)(2,1)}, f32[1504,1008]{1,0:T(8,128)}, f32[2,8,128]{2,1,0:T(8,128)}) custom-call(f32[8,1504,128]{2,1,0:T(8,128)} %get-tuple-element.82.pre_grad, f32[8,1504,128]{2,1,0:T(8,128)} %get-tuple-element.64.first, f32[16,2,8,128]{3,2,1,0:T(8,128)} %get-tuple-element.65.stats1, ...), custom_call_target="tpu_custom_call" | custom-call | tf_op jit(solution)/shard_map/pallas_call | solution.py:1000
  270.4 0.7 copy.39
  272.3 1.1 fusion.1
  273.4 203.5 %shard_map.279 = (bf16[2,2,4,512,128]{4,3,2,1,0:T(8,128)(2,1)}, bf16[2,2,4,512,128]{4,3,2,1,0:T(8,128)(2,1)}, bf16[2,2,4,512,128]{4,3,2,1,0:T(8,128)(2,1)}, bf16...) custom-call(bf16[2,2,4,512,128]{4,3,2,1,0:T(8,128)(2,1)} %bitcast.63, ...), custom_call_target="tpu_custom_call" | custom-call | tf_op jit(solution)/shard_map/pallas_call | solution.py:1000
  476.9 6.7 %shard_map.280 = f32[2016,1008]{1,0:T(8,128)} custom-call(bf16[8,1024,128]{2,1,0:T(8,128)(2,1)} %bitcast.71, bf16[8,1024,128]{2,1,0:T(8,128)(2,1)} %bitcast.72), custom_call_target="tpu_custom_call" | custom-call | tf_op jit(solution)/shard_map/pallas_call | solution.py:1000
  483.5 4.6 shard_map.281
  488.2 6.8 %shard_map.282 = f32[2016,1008]{1,0:T(8,128)} custom-call(bf16[8,1024,128]{2,1,0:T(8,128)(2,1)} %bitcast.69, bf16[8,1024,128]{2,1,0:T(8,128)(2,1)} %bitcast.70), custom_call_target="tpu_custom_call" | custom-call | tf_op jit(solution)/shard_map/pallas_call | solution.py:1000
  495.0 1.6 copy.47
  496.6 6.5 %copy.48 = f32[1504,1008]{1,0:T(8,128)} copy(f32[1504,1008]{1,0:T(8,128)} %get-tuple-element.145) | data formatting | bytes 12128256
  (37 shorter events, 10.2 us)
Async XLA Ops:
  241.7 28.6 %copy-start.3 = (f32[8,252]{1,0:T(8,128)S(1)}, f32[8,252]{1,0:T(8,128)}, u32[]{:S(2)}) copy-start(f32[8,252]{1,0:T(8,128)} %get-tuple-element.97) | copy-start | bytes 24196
  241.7 30.0 %copy-start.4 = (f32[2,8,128]{2,1,0:T(8,128)S(1)}, f32[2,8,128]{2,1,0:T(8,128)}, u32[]{:S(2)}) copy-start(f32[2,8,128]{2,1,0:T(8,128)} %get-tuple-element.105) | copy-start | bytes 24580
  241.7 30.6 %copy-start.1 = (bf16[8,512,128]{2,1,0:T(8,128)(2,1)S(1)}, bf16[8,512,128]{2,1,0:T(8,128)(2,1)}, u32[]{:S(2)}) copy-start(bf16[8,512,128]{2,1,0:T(8,128)(2,1)} %get-tuple-element.91) | copy-start | bytes 3145732
  270.4 3.0 copy-start.2
  488.2 6.8 %copy-start = (bf16[1504,1008]{1,0:T(8,128)(2,1)S(1)}, bf16[1504,1008]{1,0:T(8,128)(2,1)}, u32[]{:S(2)}) copy-start(bf16[1504,1008]{1,0:T(8,128)(2,1)} %get-tuple-element.144) | copy-start | bytes 9096196

commit v2 on v1

--- a/solution.py
+++ b/solution.py
@@ -496,126 +496,268 @@
     gather.wait()
 
 
-def weight_grad(left_tiles, right_tiles, target):
+def part_extents(n, order):
+    sizes = image_axes(n)
+    return tuple(sizes[a] for a in order)
+
+
+def part_shape(n, order, rows):
+    return part_extents(n, order) + (rows // n, 128)
+
+
+def put_blocks(target, tile, tile_rows, start, value):
+    _, e1, e2, rows, _ = target.shape
+    size = value.shape[0]
+    first = start
+    while first < start + size:
+        block = tile * (tile_rows // rows) + first // rows
+        inside = first % rows
+        take = min(rows - inside, start + size - first)
+        place = (block // (e1 * e2), block // e2 % e1, block % e2)
+        target[place[0], place[1], place[2], inside : inside + take, :] = value[
+            first - start : first - start + take
+        ]
+        first += take
+
+
+def weight_grad(left_span, right_tiles, target, spans):
     for a, b in SPANS:
-        tiles = range(a // 128, (b + 127) // 128)
-        left = jnp.concatenate([left_tiles(t) for t in tiles], axis=1)[:, : b - a]
-        for span in range(4):
+        left = left_span(a, b)
+        for k, span in enumerate(spans):
             right = jnp.concatenate([right_tiles(2 * span), right_tiles(2 * span + 1)], axis=1)
             value = dot(left, right, ((0,), (0,))).astype(BF16)
-            target[2 * span, a:b, :] = value[:, :128]
-            target[2 * span + 1, a:b, :] = value[:, 128:]
-
-
-def last_grad_kernel(
-    n,
-    last,
-    stats3,
-    live,
-    norm3,
-    sums3,
-    mask,
-    merged_grad,
-    scaled,
-    scaled_far,
-    weight,
-    weight_far,
-    grad_own,
-    grad_far,
-    scaled_grad,
-    vectors,
-    consts,
-    low,
-    low_far,
-    swap_s,
-    swap_r,
-):
+            put_blocks(target, 2 * k, 1024, a, value[:, :128])
+            put_blocks(target, 2 * k + 1, 1024, a, value[:, 128:])
+
+
+def tile_span(ref):
+    def span(a, b):
+        tiles = range(a // 128, (b + 127) // 128)
+        return jnp.concatenate([ref[t] for t in tiles], axis=1)[:, : b - a]
+
+    return span
+
+
+def image_axes(n):
+    return {16: (2, 2, 4), 128: (8, 4, 4)}.get(n, (n, 1, 1))
+
+
+class Part:
+    def __init__(self, n, order, sems):
+        sizes = image_axes(n)
+        strides = (1, sizes[0], sizes[0] * sizes[1])
+        self.me = lax.axis_index("img")
+        self.sizes = [sizes[a] for a in order]
+        self.strides = [strides[a] for a in order]
+        self.place = [lax.rem(self.me // s, e) for s, e in zip(self.strides, self.sizes)]
+        self.sems = sems
+        self.live = []
+
+    def send(self, axis, stage, source, target):
+        for d in range(1, self.sizes[axis]):
+            q = lax.rem(self.place[axis] + d, self.sizes[axis])
+            peer = self.me + (q - self.place[axis]) * self.strides[axis]
+            copy = pltpu.make_async_remote_copy(
+                src_ref=source(q),
+                dst_ref=target(d),
+                send_sem=self.sems[0].at[stage, d],
+                recv_sem=self.sems[1].at[stage, d],
+                device_id={"img": peer},
+                device_id_type=MESH,
+            )
+            copy.start()
+            self.live.append(copy)
+
+    def keep(self, source, target, stage):
+        copy = pltpu.make_async_copy(source, target, self.sems[0].at[stage, 0])
+        copy.start()
+        self.live.append(copy)
+
+    def settle(self):
+        for copy in self.live:
+            copy.wait()
+        self.live = []
+
+    def add(self, target, own, arrived):
+        total = own[...].astype(F32)
+        for block in arrived:
+            total = total + block[...].astype(F32)
+        target[...] = total.astype(BF16)
+
+    def send0(self, source, r0):
+        self.send(0, 0, lambda q: source.at[q], lambda d: r0.at[d - 1])
+
+    def sum0(self, source, r0, a0):
+        self.settle()
+        for k in range(self.sizes[1]):
+            self.add(
+                a0.at[k],
+                source.at[self.place[0], k],
+                [r0.at[d, k] for d in range(self.sizes[0] - 1)],
+            )
+
+    def send1(self, a0, r1):
+        self.send(1, 1, lambda q: a0.at[q], lambda d: r1.at[d - 1])
+
+    def sum1(self, a0, r1, a1):
+        self.settle()
+        self.add(a1, a0.at[self.place[1]], [r1.at[d] for d in range(self.sizes[1] - 1)])
+
+    def send2(self, a1, r2):
+        self.send(2, 2, lambda q: a1.at[q], lambda d: r2.at[d - 1])
+
+    def sum2(self, a1, r2, column):
+        self.settle()
+        p2 = self.place[2]
+        self.add(column.at[p2], a1.at[p2], [r2.at[d] for d in range(self.sizes[2] - 1)])
+
+    def spread2(self, column):
+        block = column.at[self.place[2]]
+        self.send(2, 3, lambda q: block, lambda d: block)
+
+    def spread1(self, column, result):
+        self.settle()
+        block = result.at[self.place[0], self.place[1]]
+        self.send(1, 4, lambda q: column, lambda d: block)
+        self.keep(column, block, 4)
+
+    def spread0(self, result):
+        self.settle()
+        block = result.at[self.place[0]]
+        self.send(0, 5, lambda q: block, lambda d: block)
+
+    @staticmethod
+    def room(n, order, shape):
+        e0, e1, e2, rows, lanes = shape
+        return (
+            (max(e0 - 1, 1), e1, e2, rows, lanes),
+            (e1, e2, rows, lanes),
+            (max(e1 - 1, 1), e2, rows, lanes),
+            (e2, rows, lanes),
+            (max(e2 - 1, 1), rows, lanes),
+            (e2, rows, lanes),
+        )
+
+
+def part_sems(n, count):
+    most = max(image_axes(n))
+    return [DMA((6, most)) for _ in range(2 * count)]
+
+
+def fetch(source, target, sem):
+    copy = pltpu.make_async_copy(source, target, sem)
+    copy.start()
+    return copy
+
+
+class Refs:
+    def __init__(self, refs):
+        self.refs = list(refs)
+
+    def take(self, count=None):
+        if count is None:
+            return self.refs.pop(0)
+        head, self.refs = self.refs[:count], self.refs[count:]
+        return head
+
+
+ORDERS = ((0, 1, 2), (1, 0, 2), (0, 1, 2), (1, 0, 2))
+
+
+def last_grad_kernel(n, *refs):
+    r = Refs(refs)
+    last_any, merged_any, group_any, scaled_any, scaled_far_any, weight_any, weight_far_any = r.take(7)
+    stats3, live, norm3, sums3, mask = r.take(5)
+    stats2, norm2, mask10, inverse, excited, squeeze_pre, squeeze_any, excite_any = r.take(8)
+    pre_grad, sums2, excite_grad, squeeze_grad, vectors = r.take(5)
+    mid1, mid3 = r.take(2), r.take(2)
+    arrive1 = r.take(2)
+    consts, consts2, local, buf_a, buf_b, low, low_far, scaled, scaled_far = r.take(9)
+    weight, weight_far, squeeze_w, excite_w = r.take(4)
+    terms, terms_in, pool_terms, pool_in, pool_tiles = r.take(5)
+    grads, rooms = r.take(4), r.take(4)
+    load, swap_s, swap_r, small_s, small_r, send, recv = r.take(7)
+    sems = r.take(8)
     ch = lax.axis_index("ch")
-    wait_partner = greet(n, all_images=False)
+    own = pl.multiple_of(ch * HALF, 16)
+    wait_all = greet(n)
+    loads = [
+        fetch(source, target, load.at[k])
+        for k, (source, target) in enumerate(
+            (
+                (last_any, buf_a),
+                (merged_any, buf_b),
+                (scaled_any, scaled),
+                (scaled_far_any, scaled_far),
+                (weight_any.at[pl.ds(own, HALF)], weight),
+                (weight_far_any, weight_far),
+                (squeeze_any, squeeze_w),
+                (excite_any, excite_w),
+            )
+        )
+    ]
     norm_constants(n, stats3, live, norm3, consts)
     back_constants(n, sums3, consts, vectors)
-    wait_partner()
+    norm_constants(n, stats2, live, norm2, consts2)
+    parts = [Part(n, order, sems[2 * k : 2 * k + 2]) for k, order in enumerate(ORDERS)]
+    wait_all()
+    loads[0].wait()
+    loads[1].wait()
 
     def step(j):
-        normed = (last[j] - row_of(consts, 0, j)) * row_of(consts, 1, j)
-        inner = merged_grad[j] - row_of(consts, 5, j) - normed * row_of(consts, 6, j)
+        normed = (buf_a[j] - row_of(consts, 0, j)) * row_of(consts, 1, j)
+        inner = buf_b[j] - row_of(consts, 5, j) - normed * row_of(consts, 6, j)
         low[j] = (mask[...] * row_of(consts, 7, j) * inner).astype(BF16)
         swap(low.at[j], low_far.at[j], swap_s.at[j], swap_r.at[j]).start()
 
     for_tiles(step)
-    weight_grad(lambda t: scaled[t], lambda t: low[t], grad_own)
-    weight_grad(lambda t: scaled_far[t], lambda t: low[t], grad_far)
-    own = pl.multiple_of(ch * HALF, 16)
-    scaled_grad[7, :, LAST:128] = jnp.zeros((ROWS, 128 - LAST), F32)
+    load_group = fetch(group_any, buf_a, load.at[0])
+    for part in range(4):
+        if part < 2:
+            loads[2 + part].wait()
+        left = tile_span((scaled, scaled_far)[part % 2])
+        weight_grad(left, lambda t: low[t], grads[part], (0, 1) if part < 2 else (2, 3))
+        if part < 2:
+            parts[part].send0(grads[part], rooms[part])
+    loads[4].wait()
     for t, (a, b) in enumerate(SPANS):
         left = jnp.concatenate([low[j] for j in range(TILES)], axis=1)[:, :HALF]
-        right = weight[pl.ds(own + a, b - a), :]
-        put_span(scaled_grad, t, slice(0, ROWS), dot(left, right, ((1,), (1,))))
+        put_span(buf_b, t, slice(0, ROWS), dot(left, weight[a:b, :], ((1,), (1,))))
+    buf_b[7, :, LAST:128] = jnp.zeros((ROWS, 128 - LAST), F32)
     for_tiles(lambda j: swap(low.at[j], low_far.at[j], swap_s.at[j], swap_r.at[j]).wait())
+    loads[5].wait()
     for t, (a, b) in enumerate(SPANS):
         left = jnp.concatenate([low_far[j] for j in range(TILES)], axis=1)[:, :HALF]
         put_span(
-            scaled_grad,
-            t,
-            slice(0, ROWS),
-            dot(left, weight_far[a:b, :], ((1,), (1,))),
-            add=True,
+            buf_b, t, slice(0, ROWS), dot(left, weight_far[a:b, :], ((1,), (1,))), add=True
         )
-
-
-def gate_grad_kernel(
-    n,
-    scaled_grad,
-    group,
-    stats2,
-    live,
-    norm2,
-    mask10,
-    inverse,
-    excited,
-    squeeze_pre,
-    squeeze_w,
-    excite_w,
-    pre_grad,
-    sums2,
-    excite_grad,
-    squeeze_grad,
-    consts,
-    local,
-    terms,
-    terms_in,
-    pool_terms,
-    pool_in,
-    pool_tiles,
-    small_s,
-    small_r,
-    send,
-    recv,
-):
-    ch = lax.axis_index("ch")
-    wait_all = greet(n)
-    norm_constants(n, stats2, live, norm2, consts)
+    load_group.wait()
 
     def gate_sum(j):
-        average = row_of(consts, 0, j)
-        scale = row_of(consts, 1, j) * row_of(consts, 2, j)
-        shift = row_of(consts, 3, j)
+        average = row_of(consts2, 0, j)
+        scale = row_of(consts2, 1, j) * row_of(consts2, 2, j)
+        shift = row_of(consts2, 3, j)
         total = jnp.zeros((IMGS, 128), F32)
         for tile in range(ROWS_IMG):
-            pre = (group[j, tile * 8 : tile * 8 + 8, :] - average) * scale + shift
+            pre = (buf_a[j, tile * 8 : tile * 8 + 8, :] - average) * scale + shift
             act = pre * sigmoid(pre)
-            total = total + act * scaled_grad[j, pl.ds(natural_row(tile), IMGS, stride=ROWS_IMG), :]
+            total = total + act * buf_b[j, pl.ds(natural_row(tile), IMGS, stride=ROWS_IMG), :]
         gate = excited[j]
         excite_grad[j] = total * gate * (1.0 - gate)
 
     for_tiles(gate_sum)
+    for k in range(2):
+        parts[k].sum0(grads[k], rooms[k], mid1[k])
+        parts[k].send1(mid1[k], arrive1[k])
+        parts[k + 2].send0(grads[k + 2], rooms[k + 2])
     wide = jnp.concatenate([excite_grad[j] for j in range(TILES)], axis=1)[:, :HALF]
     width = squeeze_w.shape[1]
     is_low = ch == 0
+    loads[6].wait()
+    loads[7].wait()
     part0 = dot(wide, excite_w[0:width, :], ((1,), (1,)), precision=HIGHEST)
     part1 = dot(wide, excite_w[width:, :], ((1,), (1,)), precision=HIGHEST)
     terms[...] = jnp.where(is_low, part1, part0)
-    wait_all()
     term_swap = swap(terms, terms_in, small_s.at[0], small_r.at[0])
     term_swap.start()
     term_swap.wait()
@@ -629,72 +771,73 @@
     pool_swap.start()
     pool_swap.wait()
     pool = jnp.where(is_low, pool0, pool1) + pool_in[...]
+    pool_tiles[7, :, LAST:128] = jnp.zeros((IMGS, 128 - LAST), F32)
     for j in range(TILES):
         part = pool[:, j * 128 : min(HALF, j * 128 + 128)]
         pool_tiles[j, :, 0 : part.shape[1]] = part * inverse[:, 0 : part.shape[1]]
 
-    def grads(j):
-        average, scale = row_of(consts, 0, j), row_of(consts, 1, j)
-        gain, shift = row_of(consts, 2, j), row_of(consts, 3, j)
+    def slopes(j):
+        average, scale = row_of(consts2, 0, j), row_of(consts2, 1, j)
+        gain, shift = row_of(consts2, 2, j), row_of(consts2, 3, j)
         gate, pooled = excited[j], pool_tiles[j]
         total = jnp.zeros((IMGS, 128), F32)
         total_normed = jnp.zeros((IMGS, 128), F32)
         for tile in range(ROWS_IMG):
             rows = slice(tile * 8, tile * 8 + 8)
-            normed = (group[j, rows, :] - average) * scale
+            normed = (buf_a[j, rows, :] - average) * scale
             pre = normed * gain + shift
             lead = pooled if tile < BIG_ROWS else pooled * mask10[(tile - BIG_ROWS) % 10]
-            act = scaled_grad[j, pl.ds(natural_row(tile), IMGS, stride=ROWS_IMG), :] * gate + lead
+            act = buf_b[j, pl.ds(natural_row(tile), IMGS, stride=ROWS_IMG), :] * gate + lead
             grad = act * slope_of(pre, sigmoid(pre))
-            pre_grad[j, rows, :] = grad
+            buf_a[j, rows, :] = grad
             total = total + grad
             total_normed = total_normed + grad * normed
         local[0, pl.ds(j, 1), :] = jnp.sum(total, axis=0, keepdims=True)
         local[1, pl.ds(j, 1), :] = jnp.sum(total_normed, axis=0, keepdims=True)
 
-    pool_tiles[7, :, LAST:128] = jnp.zeros((IMGS, 128 - LAST), F32)
-    for_tiles(grads)
+    for_tiles(slopes)
     gather = Gather(n, local, sums2, send, recv)
     gather.start()
+    store = fetch(buf_a, pre_grad, load.at[0])
     gather.wait()
-
-
-def group_grad_kernel(
-    n,
-    pre_grad,
-    group,
-    stats2,
-    live,
-    norm2,
-    sums2,
-    mask10,
-    kernel,
-    padded,
-    first,
-    stats1,
-    norm1,
-    kernel_grad,
-    first_pre_grad,
-    sums1,
-    vectors,
-    consts,
-    consts1,
-    local,
-    padded_grad,
-    band0,
-    band1,
-    band2,
-    band3,
-    full,
-    send,
-    recv,
-):
+    for k in range(2):
+        parts[k].settle()
+        parts[k + 2].sum0(grads[k + 2], rooms[k + 2], mid3[k])
+    store.wait()
+
+
+def group_grad_kernel(n, *refs):
+    r = Refs(refs)
+    pre_any, group_any, padded_any, first_any = r.take(4)
+    stats2, live, norm2, sums2, mask10, kernel, stats1, norm1 = r.take(8)
+    mid1, mid3, arrive1 = r.take(2), r.take(2), r.take(2)
+    first_pre_grad, sums1, vectors = r.take(3)
+    kernel_grads = r.take(2)
+    columns = r.take(4)
+    consts, consts1, local, buf_a, buf_b, padded_grad, padded, full = r.take(8)
+    bands = r.take(4)
+    arrive3, a1, r2 = r.take(2), r.take(4), r.take(4)
+    load, send, recv = r.take(3)
+    sems = r.take(8)
     wait_all = greet(n, partner=False)
+    loads = [
+        fetch(source, target, load.at[k])
+        for k, (source, target) in enumerate(
+            ((pre_any, buf_a), (group_any, buf_b), (padded_any, padded))
+        )
+    ]
+    parts = [Part(n, order, sems[2 * k : 2 * k + 2]) for k, order in enumerate(ORDERS)]
     norm_constants(n, stats2, live, norm2, consts)
     back_constants(n, sums2, consts, vectors)
     norm_constants(n, stats1, live, norm1, consts1)
-    bands = (band0, band1, band2, band3)
+    wait_all()
+    for k in range(2):
+        parts[k].sum1(mid1[k], arrive1[k], a1[k])
+        parts[k].send2(a1[k], r2[k])
+        parts[k + 2].send1(mid3[k], arrive3[k])
     build_bands(kernel, bands)
+    loads[0].wait()
+    loads[1].wait()
 
     def step(j):
         average, scale = row_of(consts, 0, j), row_of(consts, 1, j)
@@ -704,8 +847,8 @@
             both = []
             for half in range(2):
                 rows = slice(tile * 8 + half * 8, tile * 8 + half * 8 + 8)
-                normed = (group[j, rows, :] - average) * scale
-                grad = front * (pre_grad[j, rows, :] - less - normed * slope)
+                normed = (buf_b[j, rows, :] - average) * scale
+                grad = front * (buf_a[j, rows, :] - less - normed * slope)
                 if tile >= BIG_ROWS:
                     grad = grad * mask10[(tile + half - BIG_ROWS) % 10]
                 both.append(grad)
@@ -713,6 +856,23 @@
             padded_grad[j, row : row + 16, :] = jnp.concatenate(both, axis=0).astype(BF16)
 
     for_tiles(step)
+    load_first = fetch(first_any, buf_b, load.at[0])
+    loads[2].wait()
+
+    def advance(span):
+        if span == 0:
+            for k in range(2, 4):
+                parts[k].sum1(mid3[k - 2], arrive3[k - 2], a1[k])
+                parts[k].send2(a1[k], r2[k])
+        elif span == 1:
+            for k in range(2):
+                parts[k].sum2(a1[k], r2[k], columns[k])
+                parts[k].spread2(columns[k])
+        elif span == 2:
+            for k in range(2, 4):
+                parts[k].sum2(a1[k], r2[k], columns[k])
+                parts[k].spread2(columns[k])
+
     started = 0
     for span, (start, end) in enumerate(WINDOWS):
         tiles = (2 * span, 2 * span + 1)
@@ -725,9 +885,9 @@
             for t in range(start, end):
                 part = value[:, (t - start) * 128 : (t - start) * 128 + 128]
                 if t < started:
-                    first_pre_grad[t, rows, :] += part
+                    buf_a[t, rows, :] += part
                 else:
-                    first_pre_grad[t, rows, :] = part
+                    buf_a[t, rows, :] = part
         started = end
         right = jnp.concatenate(shifted, axis=0)
         for t in range(start, end, 2):
@@ -747,8 +907,12 @@
             pieces.append(piece)
         pieces.append(jnp.zeros((8, 256), F32))
         value = jnp.concatenate(pieces, axis=0).astype(BF16)
-        kernel_grad[2 * span] = value[:, :128]
-        kernel_grad[2 * span + 1] = value[:, 128:]
+        for half in range(2):
+            rows = slice(half * 256, half * 256 + 256)
+            put_blocks(kernel_grads[half], 2 * span, 256, 0, value[rows, :128])
+            put_blocks(kernel_grads[half], 2 * span + 1, 256, 0, value[rows, 128:])
+        advance(span)
+    load_first.wait()
 
     def slopes(j):
         average, scale = row_of(consts1, 0, j), row_of(consts1, 1, j)
@@ -757,63 +921,81 @@
         total_normed = jnp.zeros((IMGS, 128), F32)
         for tile in range(ROWS_IMG):
             rows = slice(tile * 8, tile * 8 + 8)
-            x = first[j, pl.ds(natural_row(tile), IMGS, stride=ROWS_IMG), :]
+            x = buf_b[j, pl.ds(natural_row(tile), IMGS, stride=ROWS_IMG), :]
             normed = (x - average) * scale
             pre = normed * gain + shift
-            grad = first_pre_grad[j, rows, :] * slope_of(pre, sigmoid(pre))
+            grad = buf_a[j, rows, :] * slope_of(pre, sigmoid(pre))
             if tile >= BIG_ROWS:
                 grad = grad * mask10[(tile - BIG_ROWS) % 10]
-            first_pre_grad[j, rows, :] = grad
+            buf_a[j, rows, :] = grad
             total = total + grad
             total_normed = total_normed + grad * normed
         local[0, pl.ds(j, 1), :] = jnp.sum(total, axis=0, keepdims=True)
         local[1, pl.ds(j, 1), :] = jnp.sum(total_normed, axis=0, keepdims=True)
 
     for_tiles(slopes)
-    wait_all()
     gather = Gather(n, local, sums1, send, recv)
     gather.start()
+    store = fetch(buf_a, first_pre_grad, load.at[0])
     gather.wait()
-
-
-def first_grad_kernel(
-    n,
-    pre_grad,
-    first,
-    stats1,
-    live,
-    norm1,
-    sums1,
-    mask10,
-    pixels,
-    pixels_far,
-    weight,
-    weight_far,
-    merged_grad,
-    grad_own,
-    grad_far,
-    pixels_grad,
-    vectors,
-    consts,
-    low,
-    low_far,
-    turned,
-    swap_s,
-    swap_r,
-):
-    ch = lax.axis_index("ch")
-    wait_partner = greet(n, all_images=False)
+    for part in parts:
+        part.settle()
+    store.wait()
+
+
+def first_grad_kernel(n, *refs):
+    r = Refs(refs)
+    pre_any, first_any, pixels_any, pixels_far_any, weight_any, weight_far_any, merged_any = r.take(7)
+    stats1, live, norm1, sums1, mask10, factors = r.take(6)
+    kernel_grads, columns = r.take(2), r.take(4)
+    pixels_grad, vectors = r.take(2)
+    last_sums, first_sums, kernel_sums = r.take(4), r.take(4), r.take(2)
+    factor_sums = r.take()
+    consts, buf_a, buf_b, low, low_far, pixels, pixels_far, weight, weight_far, turned = r.take(10)
+    grads = r.take(4)
+    first_rooms = [r.take(6) for _ in range(4)]
+    kernel_rooms = [r.take(6) for _ in range(2)]
+    factor_column = r.take()
+    load, swap_s, swap_r = r.take(3)
+    sems = [r.take(2) for _ in range(11)]
+    own = pl.multiple_of(lax.axis_index("ch") * HALF, 16)
+    wait_all = greet(n)
+    loads = [
+        fetch(source, target, load.at[k])
+        for k, (source, target) in enumerate(
+            (
+                (pre_any, buf_a),
+                (first_any, buf_b),
+                (pixels_any, pixels),
+                (pixels_far_any, pixels_far),
+                (weight_any.at[pl.ds(own, HALF)], weight),
+                (weight_far_any, weight_far),
+            )
+        )
+    ]
+    firsts = [Part(n, order, sems[k]) for k, order in enumerate(ORDERS)]
+    lasts = [Part(n, order, sems[4 + k]) for k, order in enumerate(ORDERS)]
+    kernels = [Part(n, ORDERS[k], sems[8 + k]) for k in range(2)]
+    factor = Part(n, ORDERS[0], sems[10])
     norm_constants(n, stats1, live, norm1, consts)
     back_constants(n, sums1, consts, vectors)
-    wait_partner()
+    wait_all()
+    for k in range(4):
+        lasts[k].spread1(columns[k], last_sums[k])
+    for k in range(2):
+        kernels[k].send0(kernel_grads[k], kernel_rooms[k][0])
+    factor_column[factor.place[2]] = factors[...]
+    factor.spread2(factor_column)
+    loads[0].wait()
+    loads[1].wait()
 
     def step(j):
         average, scale = row_of(consts, 0, j), row_of(consts, 1, j)
         less, slope, front = row_of(consts, 5, j), row_of(consts, 6, j), row_of(consts, 7, j)
         for tile in range(ROWS_IMG):
             there = pl.ds(natural_row(tile), IMGS, stride=ROWS_IMG)
-            normed = (first[j, there, :] - average) * scale
-            grad = front * (pre_grad[j, tile * 8 : tile * 8 + 8, :] - less - normed * slope)
+            normed = (buf_b[j, there, :] - average) * scale
+            grad = front * (buf_a[j, tile * 8 : tile * 8 + 8, :] - less - normed * slope)
             if tile >= BIG_ROWS:
                 grad = grad * mask10[(tile - BIG_ROWS) % 10]
             turned[there, :] = grad
@@ -821,147 +1003,89 @@
         swap(low.at[j], low_far.at[j], swap_s.at[j], swap_r.at[j]).start()
 
     for_tiles(step)
-    weight_grad(lambda t: pixels[:, t * 128 : min(HALF, t * 128 + 128)], lambda t: low[t], grad_own)
-    weight_grad(
-        lambda t: pixels_far[:, t * 128 : min(HALF, t * 128 + 128)], lambda t: low[t], grad_far
-    )
-    own = pl.multiple_of(ch * HALF, 16)
+    load_merged = fetch(merged_any, buf_a, load.at[0])
+    for part in range(4):
+        if part < 2:
+            loads[2 + part].wait()
+        rows = (pixels, pixels_far)[part % 2]
+        weight_grad(
+            lambda a, b: rows[:, a:b], lambda t: low[t], grads[part], (0, 1) if part < 2 else (2, 3)
+        )
+        if part < 2:
+            firsts[part].send0(grads[part], first_rooms[part][0])
+    load_merged.wait()
+    loads[4].wait()
     for t, (a, b) in enumerate(SPANS):
         left = jnp.concatenate([low[j] for j in range(TILES)], axis=1)[:, :HALF]
-        value = dot(left, weight[pl.ds(own + a, b - a), :], ((1,), (1,)))
-        more = jnp.concatenate([merged_grad[2 * t], merged_grad[2 * t + 1]], axis=1)[:, : b - a]
-        pixels_grad[:, a:b] = value + more
+        put_span(buf_a, t, slice(0, ROWS), dot(left, weight[a:b, :], ((1,), (1,))), add=True)
     for_tiles(lambda j: swap(low.at[j], low_far.at[j], swap_s.at[j], swap_r.at[j]).wait())
+    loads[5].wait()
     for t, (a, b) in enumerate(SPANS):
         left = jnp.concatenate([low_far[j] for j in range(TILES)], axis=1)[:, :HALF]
-        pixels_grad[:, a:b] += dot(left, weight_far[a:b, :], ((1,), (1,)))
-
-
-def image_axes(n):
-    return {16: (2, 2, 4), 128: (8, 4, 4)}.get(n, (n, 1, 1))
-
-
-class Part:
-    def __init__(self, n, order, source, result, room, sems):
-        sizes = image_axes(n)
-        strides = (1, sizes[0], sizes[0] * sizes[1])
-        self.n, self.me = n, lax.axis_index("img")
-        self.sizes = [sizes[a] for a in order]
-        self.strides = [strides[a] for a in order]
-        self.place = [lax.rem(self.me // s, e) for s, e in zip(self.strides, self.sizes)]
-        self.source, self.result, self.room, self.sems = source, result, room, sems
-        self.reduces = source is not None
-        self.live = []
-
-    def send(self, axis, stage, source, target):
-        for d in range(1, self.sizes[axis]):
-            q = lax.rem(self.place[axis] + d, self.sizes[axis])
-            peer = self.me + (q - self.place[axis]) * self.strides[axis]
-            copy = pltpu.make_async_remote_copy(
-                src_ref=source(q),
-                dst_ref=target(d),
-                send_sem=self.sems[0].at[stage, d],
-                recv_sem=self.sems[1].at[stage, d],
-                device_id={"img": peer},
-                device_id_type=MESH,
-            )
-            copy.start()
-            self.live.append(copy)
-
-    def settle(self):
-        for copy in self.live:
-            copy.wait()
-        self.live = []
-
-    def add(self, target, own, arrived, count):
-        total = own[...].astype(F32)
-        for d in range(1, count):
-            total = total + arrived[d - 1][...].astype(F32)
-        target[...] = total.astype(BF16)
-
-    def step(self, stage):
-        r0, r1, r2, a0, a1 = self.room if self.reduces else (None,) * 5
-        p0, p1, p2 = self.place
-        if stage == 0 and self.reduces:
-            self.send(0, 0, lambda q: self.source.at[q], lambda d: r0.at[d - 1])
-        elif stage == 1 and self.reduces:
-            self.settle()
-            for k in range(self.sizes[1]):
-                self.add(
-                    a0.at[k], self.source.at[p0, k], [r0.at[d, k] for d in range(self.sizes[0] - 1)], self.sizes[0]
-                )
-            self.send(1, 1, lambda q: a0.at[q], lambda d: r1.at[d - 1])
-        elif stage == 2 and self.reduces:
-            self.settle()
-            self.add(a1, a0.at[p1], [r1.at[d] for d in range(self.sizes[1] - 1)], self.sizes[1])
-            self.send(2, 2, lambda q: a1.at[q], lambda d: r2.at[d - 1])
+        put_span(buf_a, t, slice(0, ROWS), dot(left, weight_far[a:b, :], ((1,), (1,))), add=True)
+    store = fetch(buf_a, pixels_grad, load.at[0])
+
+    def advance(part, stage, source, room, result):
+        r0, a0, r1, a1, r2, column = room
+        if stage == 0:
+            part.send0(source, r0)
+        elif stage == 1:
+            part.sum0(source, r0, a0)
+            part.send1(a0, r1)
+        elif stage == 2:
+            part.sum1(a0, r1, a1)
+            part.send2(a1, r2)
         elif stage == 3:
-            if self.reduces:
-                self.settle()
-                self.add(
-                    self.result.at[p0, p1, p2], a1.at[p2], [r2.at[d] for d in range(self.sizes[2] - 1)], self.sizes[2]
-                )
-            block = self.result.at[p0, p1, p2]
-            self.send(2, 3, lambda q: block, lambda d: block)
+            part.sum2(a1, r2, column)
+            part.spread2(column)
         elif stage == 4:
-            self.settle()
-            block = self.result.at[p0, p1]
-            self.send(1, 4, lambda q: block, lambda d: block)
+            part.spread1(column, result)
         elif stage == 5:
-            self.settle()
-            block = self.result.at[p0]
-            self.send(0, 5, lambda q: block, lambda d: block)
-        elif stage == 6:
-            self.settle()
-
-    @staticmethod
-    def scratch(n, order, shape, reduces):
-        sizes = [image_axes(n)[a] for a in order]
-        most = max(sizes)
-        sems = [DMA((6, most)), DMA((6, most))]
-        if not reduces:
-            return sems
-        e0, e1, e2, rows, lanes = shape
-        room = [
-            (max(e0 - 1, 1), e1, e2, rows, lanes),
-            (max(e1 - 1, 1), e2, rows, lanes),
-            (max(e2 - 1, 1), rows, lanes),
-            (e1, e2, rows, lanes),
-            (e2, rows, lanes),
-        ]
-        return [pltpu.VMEM(s, BF16) for s in room] + sems
-
-
-def settle_kernel(n, orders, reduces, *refs):
-    count = len(orders)
-    sources, refs = refs[:count], refs[count:]
-    results, refs = refs[:count], refs[count:]
-    wait_all = greet(n, partner=False)
-    parts = []
-    for order, reduce, source, result in zip(orders, reduces, sources, results):
-        size = 7 if reduce else 2
-        own, refs = refs[:size], refs[size:]
-        part = Part(n, order, source if reduce else None, result, own[:5], own[-2:])
-        if not reduce:
-            p0, p1, p2 = part.place
-            result[p0, p1, p2] = source[...]
-        parts.append(part)
-    wait_all()
-    ticks = 7 + (count + 1) // 2
-    for tick in range(ticks):
-        for k, part in enumerate(parts):
-            stage = tick - k // 2
-            if 0 <= stage <= 6:
-                part.step(stage)
-
-
-def spread_kernel(own, far, out):
+            part.spread0(result)
+        else:
+            part.settle()
+
+    def first_to(k, stage):
+        advance(firsts[k], stage, grads[k], first_rooms[k], first_sums[k])
+
+    def kernel_to(stage):
+        for k in range(2):
+            advance(kernels[k], stage, kernel_grads[k], kernel_rooms[k], kernel_sums[k])
+
+    for tick in range(1, 8):
+        for k in range(4):
+            stage = tick - (1 if k >= 2 else 0)
+            if 0 <= stage <= 6 and not (k < 2 and stage == 0):
+                first_to(k, stage)
+        if tick <= 6:
+            kernel_to(tick)
+        if tick == 1:
+            for k in range(4):
+                lasts[k].spread0(last_sums[k])
+            factor.spread1(factor_column, factor_sums)
+        if tick == 2:
+            factor.spread0(factor_sums)
+    for k in range(4):
+        lasts[k].settle()
+    factor.settle()
+    store.wait()
+
+
+def spread_kernel(*refs):
+    lasts, firsts, pixels_wide = refs[0:4], refs[4:8], refs[8]
+    last_out, first_out, pixels_out = refs[9:12]
     ch = lax.axis_index("ch")
-    for source, place in ((own, ch), (far, 1 - ch)):
-        rows = pl.ds(pl.multiple_of(place * HALF, 8), HALF)
-        for j in range(TILES):
-            width = 128 if j < 7 else LAST
-            out[rows, j * 128 : j * 128 + width] = source[j, 0:HALF, 0:width].astype(F32)
+    j = pl.program_id(0)
+    for sums, out in ((lasts, last_out), (firsts, first_out)):
+        for late in range(2):
+
+            @pl.when((j >= 4) == bool(late))
+            def _():
+                for k, place in ((0, ch), (1, 1 - ch)):
+                    rows = pl.ds(pl.multiple_of(place * HALF, 8), HALF)
+                    out[rows, :] = sums[2 * late + k][0, 0:HALF, :].astype(F32)
+
+    pixels_out[...] = pixels_wide[0]
 
 
 def finish_kernel(low_half, high_half, factors, group_out, squeeze_w, squeeze_b, excite_w, excite_b):
@@ -993,12 +1117,13 @@
         excite_w[k * se : (k + 1) * se, :] = dot(left.astype(BF16), excite_all, ((0,), (0,)))
 
 
-def call(kernel, ins, outs, scratch, ident=None, in_specs=None, out_specs=None):
+def call(kernel, ins, outs, scratch, ident=None, in_specs=None, out_specs=None, grid=()):
     params = {"vmem_limit_bytes": VMEM_LIMIT}
     if ident is not None:
         params.update(collective_id=ident, has_side_effects=True)
     return pl.pallas_call(
         kernel,
+        grid=grid,
         out_shape=[jax.ShapeDtypeStruct(shape, dtype) for shape, dtype in outs],
         in_specs=in_specs or [VMEM] * len(ins),
         out_specs=out_specs or [VMEM] * len(outs),
@@ -1154,39 +1279,30 @@
         [consts, local, sem, sem],
         3,
     )
-    half_grad = ((TILES, 1024, 128), BF16)
-    last_grad_own, last_grad_far, scaled_grad, vectors3 = call(
+    def vmem(shape, dtype=BF16):
+        return pltpu.VMEM(shape, dtype)
+
+    shapes = [part_shape(n, order, 4 * 1024) for order in ORDERS]
+    rooms = [Part.room(n, order, shape) for order, shape in zip(ORDERS, shapes)]
+    wide_buf = vmem(wide, F32)
+    low_buf = vmem(wide)
+    weight_buf = vmem((HALF, HALF))
+    pre_grad, sums2, excite_grad, squeeze_grad, vectors3, *carry = call(
         functools.partial(last_grad_kernel, n),
         (
             last,
+            merged_grad,
+            group,
+            scaled,
+            scaled_far,
+            last_weight,
+            last_far,
             stats3,
             live,
             norm3,
             sums3,
             mask,
-            merged_grad,
-            scaled,
-            scaled_far,
-            last_weight,
-            last_far,
-        ),
-        [half_grad, half_grad, (wide, F32), vectors],
-        [
-            consts,
-            pltpu.VMEM(wide, BF16),
-            pltpu.VMEM(wide, BF16),
-            DMA((TILES,)),
-            DMA((TILES,)),
-        ],
-        4,
-    )
-    pre_grad, sums2, excite_grad, squeeze_grad = call(
-        functools.partial(gate_grad_kernel, n),
-        (
-            scaled_grad,
-            group,
             stats2,
-            live,
             norm2,
             mask10,
             inverse,
@@ -1195,78 +1311,90 @@
             squeeze_weight,
             excite_weight,
         ),
-        [(wide, F32), (stat, F32), (small, F32), ((IMGS, se), F32)],
+        [(wide, F32), (stat, F32), (small, F32), ((IMGS, se), F32), vectors]
+        + [(rooms[k][1], BF16) for k in range(4)]
+        + [(rooms[k][2], BF16) for k in range(2)],
         [
             consts,
+            consts,
             local,
-            pltpu.VMEM((IMGS, se), F32),
-            pltpu.VMEM((IMGS, se), F32),
-            pltpu.VMEM((IMGS, HALF), F32),
-            pltpu.VMEM((IMGS, HALF), F32),
-            pltpu.VMEM(small, F32),
+            wide_buf,
+            wide_buf,
+            low_buf,
+            low_buf,
+            low_buf,
+            low_buf,
+            weight_buf,
+            weight_buf,
+            vmem((2 * HALF, se), F32),
+            vmem((2 * se, HALF), F32),
+            vmem((IMGS, se), F32),
+            vmem((IMGS, se), F32),
+            vmem((IMGS, HALF), F32),
+            vmem((IMGS, HALF), F32),
+            vmem(small, F32),
+            *(vmem(shape) for shape in shapes),
+            *(vmem(room[0]) for room in rooms),
+            DMA((8,)),
+            DMA((TILES,)),
+            DMA((TILES,)),
             DMA((2,)),
             DMA((2,)),
             sem,
             sem,
+            *part_sems(n, 4),
         ],
-        5,
-    )
-    kernel_grad, first_pre_grad, sums1, vectors2 = call(
+        4,
+        in_specs=[ANY] * 7 + [VMEM] * 11 + [ANY] * 2,
+        out_specs=[ANY] + [VMEM] * 10,
+    )
+    mid1, mid3, arrive1 = carry[0:2], carry[2:4], carry[4:6]
+    kernel_shapes = [part_shape(n, ORDERS[k], TILES * 256) for k in range(2)]
+    first_pre_grad, sums1, vectors2, *carry = call(
         functools.partial(group_grad_kernel, n),
         (
             pre_grad,
             group,
+            padded,
+            first,
             stats2,
             live,
             norm2,
             sums2,
             mask10,
             kernel,
-            padded,
-            first,
             stats1,
             norm1,
+            *mid1,
+            *mid3,
+            *arrive1,
         ),
-        [((TILES, 512, 128), BF16), (wide, F32), (stat, F32), vectors],
+        [(wide, F32), (stat, F32), vectors]
+        + [(shape, BF16) for shape in kernel_shapes]
+        + [(room[5], BF16) for room in rooms],
         [
             consts,
             consts,
             local,
-            pltpu.VMEM((TILES, PAD_ROWS, 128), BF16),
+            wide_buf,
+            wide_buf,
+            vmem((TILES, PAD_ROWS, 128)),
+            vmem((TILES, PAD_ROWS, 128)),
+            vmem((512, 9 * 256), F32),
             *bands,
-            pltpu.VMEM((512, 9 * 256), F32),
+            *(vmem(rooms[k][2]) for k in (2, 3)),
+            *(vmem(room[3]) for room in rooms),
+            *(vmem(room[4]) for room in rooms),
+            DMA((3,)),
             sem,
             sem,
+            *part_sems(n, 4),
         ],
-        6,
-    )
-    first_grad_own, first_grad_far, pixels_grad, vectors1 = call(
-        functools.partial(first_grad_kernel, n),
-        (
-            first_pre_grad,
-            first,
-            stats1,
-            live,
-            norm1,
-            sums1,
-            mask10,
-            pixels,
-            pixels_far,
-            first_weight,
-            first_far,
-            merged_grad,
-        ),
-        [half_grad, half_grad, ((ROWS, HALF), F32), vectors],
-        [
-            consts,
-            pltpu.VMEM(wide, BF16),
-            pltpu.VMEM(wide, BF16),
-            pltpu.VMEM((ROWS, 128), F32),
-            DMA((TILES,)),
-            DMA((TILES,)),
-        ],
-        7,
-    )
+        5,
+        in_specs=[ANY] * 4 + [VMEM] * 14,
+        out_specs=[ANY] + [VMEM] * 8,
+    )
+    kernel_grads, columns = carry[0:2], carry[2:6]
 
     def tiles_of(value):
         return jnp.pad(value, ((0, 0), (0, 256 - se))).reshape(IMGS, 2, 128).swapaxes(0, 1)
@@ -1283,47 +1411,74 @@
     )
     count_tiles = factors.shape[0]
     factors = factors.reshape(count_tiles * IMGS, 128).astype(BF16)
-
-    sizes = image_axes(n)
-    forth, back = (0, 1, 2), (1, 0, 2)
-
-    def split(array, order):
-        rows = array.shape[0] * array.shape[1]
-        return array.reshape(*(sizes[a] for a in order), rows // n, 128)
-
-    half = kernel_grad.shape[1] // 2
-    sources = [
-        split(last_grad_own, forth),
-        split(last_grad_far, back),
-        split(first_grad_own, forth),
-        split(first_grad_far, back),
-        split(kernel_grad[:, :half], forth),
-        split(kernel_grad[:, half:], back),
-        factors,
-    ]
-    orders = (forth, back, forth, back, forth, back, forth)
-    reduces = (True,) * 6 + (False,)
-    shapes = [s.shape for s in sources[:-1]] + [sizes + factors.shape]
-    scratch = []
-    for order, shape, reduce in zip(orders, shapes, reduces):
-        scratch.extend(Part.scratch(n, order, shape, reduce))
-    results = call(
-        functools.partial(settle_kernel, n, orders, reduces),
-        sources,
-        [(shape, BF16) for shape in shapes],
-        scratch,
-        8,
-    )
-    grads = [r.reshape(TILES, -1, 128) for r in results[:-1]]
-
-    def spread(own, far):
-        return call(spread_kernel, (own, far), [((2 * HALF, HALF), F32)], [])[0]
-
-    last_weight_grad = spread(grads[0], grads[1])
-    first_weight_grad = spread(grads[2], grads[3])
+    factor_shape = part_extents(n, ORDERS[0]) + factors.shape
+    kernel_rooms = [Part.room(n, ORDERS[k], kernel_shapes[k]) for k in range(2)]
+    pixels_wide, vectors1, *carry = call(
+        functools.partial(first_grad_kernel, n),
+        (
+            first_pre_grad,
+            first,
+            pixels,
+            pixels_far,
+            first_weight,
+            first_far,
+            merged_grad,
+            stats1,
+            live,
+            norm1,
+            sums1,
+            mask10,
+            factors,
+            *kernel_grads,
+            *columns,
+        ),
+        [(wide, F32), vectors]
+        + [(shape, BF16) for shape in shapes * 2 + kernel_shapes]
+        + [(factor_shape, BF16)],
+        [
+            consts,
+            wide_buf,
+            wide_buf,
+            low_buf,
+            low_buf,
+            vmem((ROWS, HALF)),
+            vmem((ROWS, HALF)),
+            weight_buf,
+            weight_buf,
+            vmem((ROWS, 128), F32),
+            *(vmem(shape) for shape in shapes),
+            *(vmem(shape) for room in rooms for shape in room),
+            *(vmem(shape) for room in kernel_rooms for shape in room),
+            vmem(factor_shape[2:]),
+            DMA((6,)),
+            DMA((TILES,)),
+            DMA((TILES,)),
+            *part_sems(n, 11),
+        ],
+        6,
+        in_specs=[ANY] * 7 + [VMEM] * 12,
+        out_specs=[ANY, VMEM] + [ANY] * 11,
+    )
+    sums = [s.reshape(4, 1024, 128) for s in carry[0:8]]
+    kernel_sums = [s.reshape(TILES, 256, 128) for s in carry[8:10]]
+    late = pl.BlockSpec((1, 1024, 128), lambda j: (jnp.maximum(j - 4, 0), 0, 0))
+    early = pl.BlockSpec((1, 1024, 128), lambda j: (jnp.minimum(j, 3), 0, 0))
+    last_weight_grad, first_weight_grad, pixels_grad = call(
+        spread_kernel,
+        (*sums, pixels_wide),
+        [((2 * HALF, HALF), F32), ((2 * HALF, HALF), F32), ((ROWS, HALF), F32)],
+        [],
+        in_specs=[early, early, late, late] * 2 + [pl.BlockSpec((1, ROWS, 128), lambda j: (j, 0, 0))],
+        out_specs=[
+            pl.BlockSpec((2 * HALF, 128), lambda j: (0, j)),
+            pl.BlockSpec((2 * HALF, 128), lambda j: (0, j)),
+            pl.BlockSpec((ROWS, 128), lambda j: (0, j)),
+        ],
+        grid=(TILES,),
+    )
     group_weight_grad, squeeze_weight_grad, squeeze_bias_grad, excite_weight_grad, excite_bias_grad = call(
         finish_kernel,
-        (grads[4], grads[5], results[-1].reshape(n, count_tiles * IMGS, 128)),
+        (*kernel_sums, carry[10].reshape(n, count_tiles * IMGS, 128)),
         [
             ((9 * GROUP_WIDTH, HALF), F32),
             ((2 * HALF, se), F32),

time: 511 us -> 424 us (0.83)
  Pallas kernels: 474 us -> 395 us
  local copies, waits for them, and re-layouts: 18.6 us -> 10.9 us
    pallas_call x12 -> x9, Pallas kernels: 474 us -> 395 us  [call(): pl.pallas_call(kernel, grid=grid, out_shape=[jax.ShapeDtypeStruct(shape,...]
    unnamed x17 -> x16, local copies, waits for them, and re-layouts: 9.62 us -> 3.02 us
where the time goes in v2:
time: 424 us; the launch traced here: 417 us
  Pallas kernels  395 us (93%)
  local copies, waits for them, and re-layouts  10.9 us (3%)
  other arithmetic  9.88 us (2%)
    pallas_call x9, Pallas kernels, call(): pl.pallas_call(kernel, grid=grid, out_shape=[jax.ShapeDtypeStruct(shape,...  395 us

profile of v2, /device:TPU:10, one launch (start us, length us, event | category | flops | bytes accessed | tf_op | source)
XLA Modules:
  0.0 416.6 jit_solution(13604505255437615859)
XLA Ops:
  1.3 0.7 convert_divide_fusion
  3.7 0.7 pad_bitcast_fusion.4
  5.0 0.7 pad_bitcast_fusion.2
  6.3 0.7 pad_bitcast_fusion
  7.6 0.7 broadcast_in_dim.14.mask10.refs_14_.refs_8_.refs_11_
  8.3 0.7 broadcast_in_dim.13.live.refs_8_.refs_5_
  9.0 1.1 broadcast_in_dim.12.mask.refs_11_
  10.2 2.8 pad_convert_fusion.kernel.refs_9_
  12.9 26.9 %shard_map.271 = (f32[8,1504,128]{2,1,0:T(8,128)}, bf16[1504,1008]{1,0:T(8,128)(2,1)}, f32[16,2,8,128]{3,2,1,0:T(8,128)}) custom-call(f32[1,1]{1,0:T(1,128)} %bitcast.count, bf16[1504,1008]{1,0:T(8,128)(2,1)} %refs_2_.1, bf16[2016,1008]{1,0:T(8,128)(2,1)} %refs_4_.1, f32[1504,128]{1,0:T(8,128)} %broadcast_in_dim.12.mask.refs_11_), custom_call_target="tpu_custom_call" | custom-call | tf_op jit(solution)/shard_map/pallas_call | solution.py:1124
  39.9 34.4 %shard_map.272 = (bf16[8,2848,128]{2,1,0:T(8,128)(2,1)}, f32[8,1504,128]{2,1,0:T(8,128)}, f32[16,2,8,128]{3,2,1,0:T(8,128)}, bf16[1008,1008]{1,0:T(8,128)(2,1)}, bf16[1008,1008]{1,0:T(8,128)(2,1)}) custom-call(f32[1,1]{1,0:T(1,128)} %bitcast.count, f32[8,1504,128]{2,1,0:T(8,128)} %get-tuple-element.77.first.refs_3_.refs_1_, ...), custom_call_target="tpu_custom_call" | custom-call | tf_op jit(solution)/shard_map/pallas_call | solution.py:1124
  74.3 37.8 %shard_map.273 = (bf16[8,1504,128]{2,1,0:T(8,128)(2,1)}, bf16[8,1504,128]{2,1,0:T(8,128)(2,1)}, f32[8,1504,128]{2,1,0:T(8,128)}, f32[16,2,8,128]{3,2,1,0:T(8,128...) custom-call(f32[1,1]{1,0:T(1,128)} %bitcast.count, ...), custom_call_target="tpu_custom_call" | custom-call | tf_op jit(solution)/shard_map/pallas_call | solution.py:1124
  112.0 0.7 convert.37
  112.7 0.7 convert.38
  113.4 0.8 convert_dynamic-update-slice_fusion.2
  114.2 0.8 convert_dynamic-update-slice_fusion.1
  114.9 19.9 %shard_map.274 = (bf16[1504,1008]{1,0:T(8,128)(2,1)}, f32[8,1504,128]{2,1,0:T(8,128)}, f32[16,2,8,128]{3,2,1,0:T(8,128)}) custom-call(f32[8,1504,128]{2,1,0:T(8,128)} %get-tuple-element.81.last.refs_0_, f32[16,2,8,128]{3,2,1,0:T(8,128)} %get-tuple-element.82.stats3.refs_7_, f32[16,8,128]{2,1,0:T(8,128)} %broadcast_in_dim.13.live.refs_8_.refs_5_, ...), custom_call_target="tpu_custom_call" | custom-call | tf_op jit(solution)/shard_map/pallas_call | solution.py:1124
  134.8 48.1 %shard_map.275 = (f32[8,1504,128]{2,1,0:T(8,128)}, f32[16,2,8,128]{3,2,1,0:T(8,128)}, f32[8,8,128]{2,1,0:T(8,128)}, f32[8,252]{1,0:T(8,128)}, f32[2,8,128]{2,1,0...) custom-call(f32[8,1504,128]{2,1,0:T(8,128)} %get-tuple-element.81.la, ...), custom_call_target="tpu_custom_call" | custom-call | tf_op jit(solution)/shard_map/pallas_call | solution.py:1124
  182.9 0.8 convert_dynamic-update-slice_fusion
  183.7 56.6 %shard_map.276 = (f32[8,1504,128]{2,1,0:T(8,128)}, f32[16,2,8,128]{3,2,1,0:T(8,128)}, f32[2,8,128]{2,1,0:T(8,128)}, bf16[2,2,4,128,128]{4,3,2,1,0:T(8,128)(2,1)}...) custom-call(f32[8,1504,128]{2,1,0:T(8,128)} %get-tuple-element.91.re, ...), custom_call_target="tpu_custom_call" | custom-call | tf_op jit(solution)/shard_map/pallas_call | solution.py:1124
  241.0 151.5 %shard_map.277 = (f32[8,1504,128]{2,1,0:T(8,128)}, f32[2,8,128]{2,1,0:T(8,128)}, bf16[2,2,4,256,128]{4,3,2,1,0:T(8,128)(2,1)}, bf16[2,2,4,256,128]{4,3,2,1,0:T(8...) custom-call(f32[8,1504,128]{2,1,0:T(8,128)} %get-tuple-element.100.r, ...), custom_call_target="tpu_custom_call" | custom-call | tf_op jit(solution)/shard_map/pallas_call | solution.py:1124
  392.5 0.7 copy.39
  395.1 4.6 %shard_map.279 = (f32[504,1008]{1,0:T(8,128)}, f32[2016,252]{1,0:T(8,128)}, f32[1,252]{1,0:T(1,128)}, f32[504,1008]{1,0:T(8,128)}, f32[1,1008]{1,0:T(1,128)}) custom-call(bf16[8,256,128]{2,1,0:T(8,128)(2,1)} %bitcast.71, bf16[8,256,128]{2,1,0:T(8,128)(2,1)} %bitcast.72, bf16[16,240,128]{2,1,0:T(8,128)(2,1)} %bitcast.70), custom_call_target="tpu_custom_call" | custom-call | tf_op jit(solution)/shard_map/pallas_call | solution.py:1124
  399.7 14.9 %shard_map.278 = (f32[2016,1008]{1,0:T(8,128)}, f32[2016,1008]{1,0:T(8,128)}, f32[1504,1008]{1,0:T(8,128)}) custom-call(bf16[4,1024,128]{2,1,0:T(8,128)(2,1)} %bitcast.61, bf16[4,1024,128]{2,1,0:T(8,128)(2,1)} %bitcast.62, bf16[4,1024,128]{2,1,0:T(8,128)(2,1)} %bitcast.63, bf16[4,1024,128]{2,1,0:T(8,128)(2,1)} %bitcast.64, bf16[4,1024,128]{2,1,0:T(8,128)(2,1)} %bitcast.65, ...), custom_call_target="tpu_custom_call" | custom-call | tf_op jit(solution)/shard_map/pallas_call | solution.py:1124
  414.7 1.6 copy.46
  (32 shorter events, 6.6 us)
Async XLA Ops:
  183.7 56.6 %copy-start.2 = (f32[8,252]{1,0:T(8,128)S(1)}, f32[8,252]{1,0:T(8,128)}, u32[]{:S(2)}) copy-start(f32[8,252]{1,0:T(8,128)} %get-tuple-element.109) | copy-start | bytes 24196
  240.4 0.6 copy-start.1
  241.0 152.8 %copy-start.4 = (f32[2,8,128]{2,1,0:T(8,128)S(1)}, f32[2,8,128]{2,1,0:T(8,128)}, u32[]{:S(2)}) copy-start(f32[2,8,128]{2,1,0:T(8,128)} %get-tuple-element.132) | copy-start | bytes 24580
  241.0 153.5 %copy-start.3 = (f32[2,8,128]{2,1,0:T(8,128)S(1)}, f32[2,8,128]{2,1,0:T(8,128)}, u32[]{:S(2)}) copy-start(f32[2,8,128]{2,1,0:T(8,128)} %get-tuple-element.138) | copy-start | bytes 24580
  399.7 15.0 %copy-start = (bf16[1504,1008]{1,0:T(8,128)(2,1)S(1)}, bf16[1504,1008]{1,0:T(8,128)(2,1)}, u32[]{:S(2)}) copy-start(bf16[1504,1008]{1,0:T(8,128)(2,1)} %get-tuple-element.168) | copy-start | bytes 9096196

commit v3 on v2

--- a/solution.py
+++ b/solution.py
@@ -19,7 +19,6 @@
 EPSILON = 1e-05
 F32 = jnp.float32
 BF16 = jnp.bfloat16
-HIGHEST = lax.Precision.HIGHEST
 MESH = pl.DeviceIdType.MESH
 VMEM = pl.BlockSpec(memory_space=pltpu.VMEM)
 ANY = pl.BlockSpec(memory_space=pl.ANY)
@@ -263,165 +262,178 @@
         ref[j, row : row + 16, :] = jnp.zeros((16, 128), BF16)
 
 
-def first_kernel(
-    n, count, pixels, weight, mask, first, other, stats, local, swap_s, swap_r, send, recv
-):
+def halves(value):
+    high = value.astype(BF16)
+    return high, (value - high.astype(F32)).astype(BF16)
+
+
+def fine_dot(left, right_high, right_low, dims=((1,), (0,))):
+    high, low = halves(left)
+    both = jnp.concatenate([high.astype(F32), low.astype(F32)], axis=0).astype(BF16)
+    value = dot(both, right_high, dims)
+    return value[:IMGS] + value[IMGS:] + dot(both, right_low, dims)[:IMGS]
+
+
+def load_vectors(vectors, first, norm):
+    norm[...] = jnp.zeros_like(norm)
+    for k in range(2):
+        for j in range(TILES):
+            width = 128 if j < 7 else LAST
+            norm[k, j : j + 1, 0:width] = vectors[
+                first + k : first + k + 1, j * 128 : j * 128 + width
+            ]
+
+
+def live_slots(counts, mask10):
+    for slot in range(10):
+        mask10[slot] = (counts[...] > slot).astype(F32)
+
+
+def natural_mask(mask10, mask):
+    for tile in range(ROWS_IMG):
+        there = pl.ds(natural_row(tile), IMGS, stride=ROWS_IMG)
+        if tile < BIG_ROWS:
+            mask[there, :] = jnp.ones((IMGS, 128), F32)
+        else:
+            mask[there, :] = mask10[(tile - BIG_ROWS) % 10]
+
+
+def forward_kernel(n, *refs):
+    r = Refs(refs)
+    pixels_any, weight1_any, weight3_any, kernel_any, squeeze_any, excite_any, output_any = r.take(7)
+    counts, live, vectors, squeeze_b, excite_b = r.take(5)
+    first_out, far_out, padded_out, group_out, scaled_out, scaled_far_out = r.take(6)
+    last_out, merged_out, block_out = r.take(3)
+    far1, far3 = r.take(2)
+    split_outs = r.take(4)
+    stats1, stats2, stats3, sums3 = r.take(4)
+    pooled, pooled_far, squeezed, squeezed_far, squeeze_pre, excited = r.take(6)
+    consts, norm, local, buf_a, buf_b, pixels, far, weight, zone = r.take(9)
+    kernel_low, kernel, squeeze_w, excite_w = r.take(4)
+    splits = r.take(4)
+    turned, mask, mask10 = r.take(3)
+    bands = r.take(4)
+    load, store, swap_s, swap_r, tile_s, tile_r, small_s, small_r = r.take(8)
+    gathers = [r.take(2) for _ in range(4)]
     ch = lax.axis_index("ch")
     wait_all = greet(n)
+    loads = [
+        fetch(source, target, load.at[k])
+        for k, (source, target) in enumerate(
+            (
+                (pixels_any, pixels),
+                (weight1_any, weight),
+                (kernel_any, kernel_low),
+                (squeeze_any, squeeze_w),
+                (excite_any, excite_w),
+            )
+        )
+    ]
     own = pl.multiple_of(ch * HALF, 16)
-    far = pl.multiple_of((1 - ch) * HALF, 16)
+    away = pl.multiple_of((1 - ch) * HALF, 16)
+    live_slots(counts, mask10)
+    natural_mask(mask10, mask)
+    count = live[lax.axis_index("img")][0:1, :]
     wait_all()
     chunks = ((0, 384), (384, 384), (768, 384), (1152, 352))
     swaps = []
     for k, (start, size) in enumerate(chunks):
         rows = pl.ds(start, size)
-        swaps.append(swap(pixels.at[rows], other.at[rows], swap_s.at[k], swap_r.at[k]))
+        swaps.append(swap(pixels_any.at[rows], far.at[rows], swap_s.at[k], swap_r.at[k]))
         swaps[-1].start()
-    first[7, :, LAST:128] = jnp.zeros((ROWS, 128 - LAST), F32)
+    loads[0].wait()
+    loads[1].wait()
     for t, (a, b) in enumerate(SPANS):
-        put_span(first, t, slice(0, ROWS), dot(pixels[...], weight[pl.ds(own, HALF), a:b]))
+        put_span(buf_a, t, slice(0, ROWS), dot(pixels[...], weight[pl.ds(own, HALF), a:b]))
+    buf_a[7, :, LAST:128] = jnp.zeros((ROWS, 128 - LAST), F32)
     for k, (start, size) in enumerate(chunks):
         swaps[k].wait()
         rows = slice(start, start + size)
         for t, (a, b) in enumerate(SPANS):
-            put_span(first, t, rows, dot(other[rows, :], weight[pl.ds(far, HALF), a:b]), add=True)
-    natural_stats(first, mask, count[0, 0], local)
-    gather = Gather(n, local, stats, send, recv)
+            put_span(buf_a, t, rows, dot(far[rows, :], weight[pl.ds(away, HALF), a:b]), add=True)
+    natural_stats(buf_a, mask, count, local)
+    gather = Gather(n, local, stats1, *gathers[0])
     gather.start()
+    weight_swaps = [
+        swap(w.at[pl.ds(away, HALF)], f, swap_s.at[4 + k], swap_r.at[4 + k])
+        for k, (w, f) in enumerate(((weight1_any, far1), (weight3_any, far3)))
+    ]
+    for s in weight_swaps:
+        s.start()
+    load_weight = fetch(weight3_any, weight, load.at[0])
+    store_far = fetch(far, far_out, store.at[0])
+    stores = []
+    store_first = fetch(buf_a, first_out, store.at[1])
+    loads[2].wait()
+    kernel[:, 0:HALF] = kernel_low[...].astype(F32)
+    kernel[:, HALF:1024] = jnp.zeros((9 * GROUP_WIDTH, 1024 - HALF), F32)
+    build_bands(kernel, bands)
+    loads[3].wait()
+    loads[4].wait()
+    for k, w in enumerate((squeeze_w, excite_w)):
+        splits[2 * k][...], splits[2 * k + 1][...] = halves(w[...])
+    stores += [fetch(splits[k], split_outs[k], store.at[2 + k]) for k in range(4)]
+    load_vectors(vectors, 0, norm)
     gather.wait()
-
-
-def group_kernel(
-    n,
-    count,
-    first,
-    stats1,
-    live,
-    norm1,
-    mask10,
-    kernel,
-    weight1,
-    weight3,
-    padded,
-    group,
-    stats2,
-    far1,
-    far3,
-    consts,
-    local,
-    band0,
-    band1,
-    band2,
-    band3,
-    swap_s,
-    swap_r,
-    send,
-    recv,
-):
-    wait_all = greet(n)
-    norm_constants(n, stats1, live, norm1, consts)
-    wait_all()
-    far = pl.multiple_of((1 - lax.axis_index("ch")) * HALF, 16)
-    swaps = [
-        swap(w.at[pl.ds(far, HALF)], f, swap_s.at[k], swap_r.at[k])
-        for k, (w, f) in enumerate(((weight1, far1), (weight3, far3)))
-    ]
-    for s in swaps:
-        s.start()
-    bands = (band0, band1, band2, band3)
-    build_bands(kernel, bands)
-
-    def step(j):
+    norm_constants(n, stats1, live, norm, consts)
+
+    def activate_first(j):
         average = row_of(consts, 0, j)
         scale = row_of(consts, 1, j) * row_of(consts, 2, j)
         shift = row_of(consts, 3, j)
-        zero_pads(padded, j)
+        zero_pads(zone, j)
         for tile in range(0, ROWS_IMG, 2):
             both = []
             for half in range(2):
-                x = first[j, pl.ds(natural_row(tile + half), IMGS, stride=ROWS_IMG), :]
+                x = buf_a[j, pl.ds(natural_row(tile + half), IMGS, stride=ROWS_IMG), :]
                 pre = (x - average) * scale + shift
                 both.append(pre * sigmoid(pre))
             row = padded_row(tile)
-            padded[j, row : row + 16, :] = jnp.concatenate(both, axis=0).astype(BF16)
-
-    for_tiles(step)
+            zone[j, row : row + 16, :] = jnp.concatenate(both, axis=0).astype(BF16)
+
+    for_tiles(activate_first)
+    store_padded = fetch(zone.at[:, pl.ds(0, PAD_ROWS)], padded_out, store.at[6])
     for span, (start, end) in enumerate(WINDOWS):
         tiles = range(start, end)
         right = jnp.concatenate(
             [bands[span][:, tap * 256 : tap * 256 + 256] for tap in range(9)], axis=0
         )
         for big in (True, False):
-            left = jnp.concatenate([window(padded, tiles, dy, dx, big) for dy, dx in TAPS], axis=1)
+            left = jnp.concatenate([window(zone, tiles, dy, dx, big) for dy, dx in TAPS], axis=1)
             rows = slice(0, 784) if big else slice(784, ROWS)
-            put_span(group, span, rows, dot(left, right))
-    crop_stats(group, mask10, count[0, 0], local)
-    gather = Gather(n, local, stats2, send, recv)
+            put_span(buf_b, span, rows, dot(left, right))
+    crop_stats(buf_b, mask10, count, local)
+    gather = Gather(n, local, stats2, *gathers[1])
     gather.start()
-    for s in swaps:
-        s.wait()
+    store_group = fetch(buf_b, group_out, store.at[7])
+    load_vectors(vectors, 2, norm)
+    store_first.wait()
+    store_padded.wait()
+    store_far.wait()
+    load_output = fetch(output_any, far, load.at[1])
     gather.wait()
-
-
-def gate_kernel(
-    n,
-    count,
-    group,
-    stats2,
-    live,
-    norm2,
-    mask10,
-    inverse,
-    squeeze_w,
-    squeeze_b,
-    excite_w,
-    excite_b,
-    mask,
-    weight,
-    scaled,
-    scaled_far,
-    last,
-    stats3,
-    pooled,
-    pooled_far,
-    squeezed,
-    squeezed_far,
-    squeeze_pre,
-    excited,
-    consts,
-    local,
-    act,
-    turned,
-    swap_s,
-    swap_r,
-    small_s,
-    small_r,
-    send,
-    recv,
-):
-    ch = lax.axis_index("ch")
-    wait_all = greet(n)
-    norm_constants(n, stats2, live, norm2, consts)
-
-    def activate(j):
+    norm_constants(n, stats2, live, norm, consts)
+    inverse = 1.0 / (BIG_ROWS + 9.0 * counts[...].astype(F32))
+
+    def activate_group(j):
         average = row_of(consts, 0, j)
         scale = row_of(consts, 1, j) * row_of(consts, 2, j)
-        pre = (group[j] - average) * scale + row_of(consts, 3, j)
+        pre = (buf_b[j] - average) * scale + row_of(consts, 3, j)
         value = pre * sigmoid(pre)
-        act[j] = value
-        pooled[j] = crop_sum(value.reshape(ROWS_IMG, IMGS, 128), mask10) * inverse[...]
-
-    for_tiles(activate)
-    wait_all()
+        buf_a[j] = value
+        pooled[j] = crop_sum(value.reshape(ROWS_IMG, IMGS, 128), mask10) * inverse
+
+    for_tiles(activate_group)
     pool_swap = swap(pooled, pooled_far, small_s.at[0], small_r.at[0])
     pool_swap.start()
     pool_swap.wait()
     mine = jnp.concatenate([pooled[j] for j in range(TILES)], axis=1)[:, :HALF]
     theirs = jnp.concatenate([pooled_far[j] for j in range(TILES)], axis=1)[:, :HALF]
     is_low = ch == 0
+    high, low = splits[0], splits[1]
     pre = (
-        dot(jnp.where(is_low, mine, theirs), squeeze_w[0:HALF, :], precision=HIGHEST)
-        + dot(jnp.where(is_low, theirs, mine), squeeze_w[HALF:, :], precision=HIGHEST)
+        fine_dot(jnp.where(is_low, mine, theirs), high[0:HALF, :], low[0:HALF, :])
+        + fine_dot(jnp.where(is_low, theirs, mine), high[HALF:, :], low[HALF:, :])
         + squeeze_b[...]
     )
     squeeze_pre[...] = pre
@@ -431,68 +443,75 @@
     squeeze_swap.wait()
     mine, theirs = squeezed[...], squeezed_far[...]
     width = mine.shape[1]
+    high, low = splits[2], splits[3]
     gate = sigmoid(
-        dot(jnp.where(is_low, mine, theirs), excite_w[0:width, :], precision=HIGHEST)
-        + dot(jnp.where(is_low, theirs, mine), excite_w[width:, :], precision=HIGHEST)
+        fine_dot(jnp.where(is_low, mine, theirs), high[0:width, :], low[0:width, :])
+        + fine_dot(jnp.where(is_low, theirs, mine), high[width:, :], low[width:, :])
         + excite_b[...]
     )
     excited[7] = jnp.zeros((IMGS, 128), F32)
     for j in range(TILES - 1):
         excited[j] = gate[:, j * 128 : j * 128 + 128]
     excited[7, :, 0:LAST] = gate[:, 7 * 128 :]
+    mine_rows, far_rows = pl.ds(0, ROWS), pl.ds(ROWS, ROWS)
+
+    def tile_swap(j):
+        return swap(zone.at[j, mine_rows], zone.at[j, far_rows], tile_s.at[j], tile_r.at[j])
 
     def apply(j):
         gate_j = excited[j]
         for tile in range(ROWS_IMG):
             turned[pl.ds(natural_row(tile), IMGS, stride=ROWS_IMG), :] = (
-                act[j, tile * 8 : tile * 8 + 8, :] * gate_j
+                buf_a[j, tile * 8 : tile * 8 + 8, :] * gate_j
             )
-        scaled[j] = turned[...].astype(BF16)
-        swap(scaled.at[j], scaled_far.at[j], swap_s.at[j], swap_r.at[j]).start()
+        zone[j, 0:ROWS, :] = turned[...].astype(BF16)
+        tile_swap(j).start()
 
     for_tiles(apply)
-    own = pl.multiple_of(ch * HALF, 16)
-    far = pl.multiple_of((1 - ch) * HALF, 16)
-    last[7, :, LAST:128] = jnp.zeros((ROWS, 128 - LAST), F32)
+    stores.append(fetch(zone.at[:, mine_rows], scaled_out, store.at[8]))
+    load_weight.wait()
+    store_group.wait()
     for t, (a, b) in enumerate(SPANS):
-        left = jnp.concatenate([scaled[j] for j in range(TILES)], axis=1)[:, :HALF]
-        put_span(last, t, slice(0, ROWS), dot(left, weight[pl.ds(own, HALF), a:b]))
-    for_tiles(lambda j: swap(scaled.at[j], scaled_far.at[j], swap_s.at[j], swap_r.at[j]).wait())
+        left = jnp.concatenate([zone[j, 0:ROWS, :] for j in range(TILES)], axis=1)[:, :HALF]
+        put_span(buf_b, t, slice(0, ROWS), dot(left, weight[pl.ds(own, HALF), a:b]))
+    buf_b[7, :, LAST:128] = jnp.zeros((ROWS, 128 - LAST), F32)
+    for_tiles(lambda j: tile_swap(j).wait())
+    stores.append(fetch(zone.at[:, far_rows], scaled_far_out, store.at[9]))
     for t, (a, b) in enumerate(SPANS):
-        left = jnp.concatenate([scaled_far[j] for j in range(TILES)], axis=1)[:, :HALF]
-        put_span(last, t, slice(0, ROWS), dot(left, weight[pl.ds(far, HALF), a:b]), add=True)
-    natural_stats(last, mask, count[0, 0], local)
-    gather = Gather(n, local, stats3, send, recv)
+        left = jnp.concatenate([zone[j, ROWS : 2 * ROWS, :] for j in range(TILES)], axis=1)[:, :HALF]
+        put_span(buf_b, t, slice(0, ROWS), dot(left, weight[pl.ds(away, HALF), a:b]), add=True)
+    natural_stats(buf_b, mask, count, local)
+    gather = Gather(n, local, stats3, *gathers[2])
     gather.start()
+    stores.append(fetch(buf_b, last_out, store.at[10]))
+    load_vectors(vectors, 4, norm)
+    buf_a[7, :, LAST:128] = jnp.zeros((ROWS, 128 - LAST), F32)
+    load_output.wait()
     gather.wait()
-
-
-def merge_kernel(
-    n, last, stats3, live, norm3, mask, pixels, output_grad, block, merged_grad, sums3, consts, local, send, recv
-):
-    wait_all = greet(n, partner=False)
-    norm_constants(n, stats3, live, norm3, consts)
-    merged_grad[7, :, LAST:128] = jnp.zeros((ROWS, 128 - LAST), F32)
+    norm_constants(n, stats3, live, norm, consts)
     local[...] = jnp.zeros_like(local)
 
-    def step(j, lanes, width):
+    def merge(j, lanes, width):
         def vec(k):
             return consts[k, pl.ds(j, 1), 0:width]
 
         m = mask[:, 0:width]
-        normed = (last[j, :, 0:width] - vec(0)) * vec(1)
+        normed = (buf_b[j, :, 0:width] - vec(0)) * vec(1)
         merged = pixels[:, lanes].astype(F32) + normed * vec(2) + vec(3)
         s = sigmoid(merged)
-        block[:, lanes] = (merged * s * m).astype(BF16)
-        grad = output_grad[:, lanes].astype(F32) * m * slope_of(merged, s)
-        merged_grad[j, :, 0:width] = grad
+        grad = far[:, lanes].astype(F32) * m * slope_of(merged, s)
+        far[:, lanes] = (merged * s * m).astype(BF16)
+        buf_a[j, :, 0:width] = grad
         local[0, pl.ds(j, 1), 0:width] = jnp.sum(grad, axis=0, keepdims=True)
         local[1, pl.ds(j, 1), 0:width] = jnp.sum(grad * normed, axis=0, keepdims=True)
 
-    for_ragged_tiles(step)
-    wait_all()
-    gather = Gather(n, local, sums3, send, recv)
+    for_ragged_tiles(merge)
+    gather = Gather(n, local, sums3, *gathers[3])
     gather.start()
+    stores.append(fetch(buf_a, merged_out, store.at[11]))
+    stores.append(fetch(far, block_out, store.at[12]))
+    for s in weight_swaps + stores:
+        s.wait()
     gather.wait()
 
 
@@ -667,13 +686,15 @@
 def last_grad_kernel(n, *refs):
     r = Refs(refs)
     last_any, merged_any, group_any, scaled_any, scaled_far_any, weight_any, weight_far_any = r.take(7)
-    stats3, live, norm3, sums3, mask = r.take(5)
-    stats2, norm2, mask10, inverse, excited, squeeze_pre, squeeze_any, excite_any = r.take(8)
+    stats3, live, sums3 = r.take(3)
+    stats2, counts, vectors_in, excited, squeeze_pre = r.take(5)
+    split_anys = r.take(4)
     pre_grad, sums2, excite_grad, squeeze_grad, vectors = r.take(5)
     mid1, mid3 = r.take(2), r.take(2)
     arrive1 = r.take(2)
     consts, consts2, local, buf_a, buf_b, low, low_far, scaled, scaled_far = r.take(9)
-    weight, weight_far, squeeze_w, excite_w = r.take(4)
+    weight, weight_far, norm, mask, mask10 = r.take(5)
+    splits = r.take(4)
     terms, terms_in, pool_terms, pool_in, pool_tiles = r.take(5)
     grads, rooms = r.take(4), r.take(4)
     load, swap_s, swap_r, small_s, small_r, send, recv = r.take(7)
@@ -691,14 +712,18 @@
                 (scaled_far_any, scaled_far),
                 (weight_any.at[pl.ds(own, HALF)], weight),
                 (weight_far_any, weight_far),
-                (squeeze_any, squeeze_w),
-                (excite_any, excite_w),
+                *zip(split_anys, splits),
             )
         )
     ]
-    norm_constants(n, stats3, live, norm3, consts)
+    live_slots(counts, mask10)
+    natural_mask(mask10, mask)
+    inverse = 1.0 / (BIG_ROWS + 9.0 * counts[...].astype(F32))
+    load_vectors(vectors_in, 4, norm)
+    norm_constants(n, stats3, live, norm, consts)
     back_constants(n, sums3, consts, vectors)
-    norm_constants(n, stats2, live, norm2, consts2)
+    load_vectors(vectors_in, 2, norm)
+    norm_constants(n, stats2, live, norm, consts2)
     parts = [Part(n, order, sems[2 * k : 2 * k + 2]) for k, order in enumerate(ORDERS)]
     wait_all()
     loads[0].wait()
@@ -751,12 +776,14 @@
         parts[k].send1(mid1[k], arrive1[k])
         parts[k + 2].send0(grads[k + 2], rooms[k + 2])
     wide = jnp.concatenate([excite_grad[j] for j in range(TILES)], axis=1)[:, :HALF]
-    width = squeeze_w.shape[1]
+    width = squeeze_pre.shape[1]
     is_low = ch == 0
-    loads[6].wait()
-    loads[7].wait()
-    part0 = dot(wide, excite_w[0:width, :], ((1,), (1,)), precision=HIGHEST)
-    part1 = dot(wide, excite_w[width:, :], ((1,), (1,)), precision=HIGHEST)
+    for k in range(6, 10):
+        loads[k].wait()
+    across = ((1,), (1,))
+    high, low_part = splits[2], splits[3]
+    part0 = fine_dot(wide, high[0:width, :], low_part[0:width, :], across)
+    part1 = fine_dot(wide, high[width:, :], low_part[width:, :], across)
     terms[...] = jnp.where(is_low, part1, part0)
     term_swap = swap(terms, terms_in, small_s.at[0], small_r.at[0])
     term_swap.start()
@@ -764,8 +791,9 @@
     pre = squeeze_pre[...]
     grad = (jnp.where(is_low, part0, part1) + terms_in[...]) * slope_of(pre, sigmoid(pre))
     squeeze_grad[...] = grad
-    pool0 = dot(grad, squeeze_w[0:HALF, :], ((1,), (1,)), precision=HIGHEST)
-    pool1 = dot(grad, squeeze_w[HALF:, :], ((1,), (1,)), precision=HIGHEST)
+    high, low_part = splits[0], splits[1]
+    pool0 = fine_dot(grad, high[0:HALF, :], low_part[0:HALF, :], across)
+    pool1 = fine_dot(grad, high[HALF:, :], low_part[HALF:, :], across)
     pool_terms[...] = jnp.where(is_low, pool1, pool0)
     pool_swap = swap(pool_terms, pool_in, small_s.at[1], small_r.at[1])
     pool_swap.start()
@@ -809,17 +837,21 @@
 def group_grad_kernel(n, *refs):
     r = Refs(refs)
     pre_any, group_any, padded_any, first_any = r.take(4)
-    stats2, live, norm2, sums2, mask10, kernel, stats1, norm1 = r.take(8)
+    stats2, live, sums2, counts, vectors_in, kernel_low, stats1 = r.take(7)
     mid1, mid3, arrive1 = r.take(2), r.take(2), r.take(2)
     first_pre_grad, sums1, vectors = r.take(3)
-    kernel_grads = r.take(2)
-    columns = r.take(4)
-    consts, consts1, local, buf_a, buf_b, padded_grad, padded, full = r.take(8)
+    kernel_grads, kernel_arrive = r.take(2), r.take(2)
+    columns = r.take(2)
+    last_sums = r.take(2)
+    early_columns = r.take(2)
+    consts, consts1, norm, mask10, kernel = r.take(5)
+    local, buf_a, buf_b, padded_grad, padded, full = r.take(6)
     bands = r.take(4)
     arrive3, a1, r2 = r.take(2), r.take(4), r.take(4)
     load, send, recv = r.take(3)
-    sems = r.take(8)
+    sems = r.take(12)
     wait_all = greet(n, partner=False)
+    columns = early_columns + columns
     loads = [
         fetch(source, target, load.at[k])
         for k, (source, target) in enumerate(
@@ -827,14 +859,20 @@
         )
     ]
     parts = [Part(n, order, sems[2 * k : 2 * k + 2]) for k, order in enumerate(ORDERS)]
-    norm_constants(n, stats2, live, norm2, consts)
+    kernels = [Part(n, ORDERS[k], sems[8 + 2 * k : 10 + 2 * k]) for k in range(2)]
+    live_slots(counts, mask10)
+    load_vectors(vectors_in, 2, norm)
+    norm_constants(n, stats2, live, norm, consts)
     back_constants(n, sums2, consts, vectors)
-    norm_constants(n, stats1, live, norm1, consts1)
+    load_vectors(vectors_in, 0, norm)
+    norm_constants(n, stats1, live, norm, consts1)
     wait_all()
     for k in range(2):
         parts[k].sum1(mid1[k], arrive1[k], a1[k])
         parts[k].send2(a1[k], r2[k])
         parts[k + 2].send1(mid3[k], arrive3[k])
+    kernel[:, 0:HALF] = kernel_low[...].astype(F32)
+    kernel[:, HALF:1024] = jnp.zeros((9 * GROUP_WIDTH, 1024 - HALF), F32)
     build_bands(kernel, bands)
     loads[0].wait()
     loads[1].wait()
@@ -859,6 +897,10 @@
     load_first = fetch(first_any, buf_b, load.at[0])
     loads[2].wait()
 
+    for k in range(2):
+        parts[k].sum2(a1[k], r2[k], columns[k])
+        parts[k].spread2(columns[k])
+
     def advance(span):
         if span == 0:
             for k in range(2, 4):
@@ -866,12 +908,16 @@
                 parts[k].send2(a1[k], r2[k])
         elif span == 1:
             for k in range(2):
-                parts[k].sum2(a1[k], r2[k], columns[k])
-                parts[k].spread2(columns[k])
+                parts[k].spread1(columns[k], last_sums[k])
         elif span == 2:
+            for k in range(2):
+                parts[k].spread0(last_sums[k])
             for k in range(2, 4):
                 parts[k].sum2(a1[k], r2[k], columns[k])
                 parts[k].spread2(columns[k])
+        else:
+            for k in range(2):
+                kernels[k].send0(kernel_grads[k], kernel_arrive[k])
 
     started = 0
     for span, (start, end) in enumerate(WINDOWS):
@@ -938,7 +984,7 @@
     gather.start()
     store = fetch(buf_a, first_pre_grad, load.at[0])
     gather.wait()
-    for part in parts:
+    for part in parts + kernels:
         part.settle()
     store.wait()
 
@@ -946,18 +992,19 @@
 def first_grad_kernel(n, *refs):
     r = Refs(refs)
     pre_any, first_any, pixels_any, pixels_far_any, weight_any, weight_far_any, merged_any = r.take(7)
-    stats1, live, norm1, sums1, mask10, factors = r.take(6)
-    kernel_grads, columns = r.take(2), r.take(4)
+    stats1, live, sums1, counts, vectors_in, factors = r.take(6)
+    kernel_grads, kernel_arrive, columns = r.take(2), r.take(2), r.take(2)
     pixels_grad, vectors = r.take(2)
-    last_sums, first_sums, kernel_sums = r.take(4), r.take(4), r.take(2)
+    last_sums, first_sums, kernel_sums = r.take(2), r.take(4), r.take(2)
     factor_sums = r.take()
-    consts, buf_a, buf_b, low, low_far, pixels, pixels_far, weight, weight_far, turned = r.take(10)
+    consts, norm, mask10 = r.take(3)
+    buf_a, buf_b, low, low_far, pixels, pixels_far, weight, weight_far, turned = r.take(9)
     grads = r.take(4)
     first_rooms = [r.take(6) for _ in range(4)]
-    kernel_rooms = [r.take(6) for _ in range(2)]
+    kernel_rooms = [r.take(5) for _ in range(2)]
     factor_column = r.take()
     load, swap_s, swap_r = r.take(3)
-    sems = [r.take(2) for _ in range(11)]
+    sems = [r.take(2) for _ in range(9)]
     own = pl.multiple_of(lax.axis_index("ch") * HALF, 16)
     wait_all = greet(n)
     loads = [
@@ -974,16 +1021,19 @@
         )
     ]
     firsts = [Part(n, order, sems[k]) for k, order in enumerate(ORDERS)]
-    lasts = [Part(n, order, sems[4 + k]) for k, order in enumerate(ORDERS)]
-    kernels = [Part(n, ORDERS[k], sems[8 + k]) for k in range(2)]
-    factor = Part(n, ORDERS[0], sems[10])
-    norm_constants(n, stats1, live, norm1, consts)
+    lasts = [Part(n, ORDERS[2 + k], sems[4 + k]) for k in range(2)]
+    kernels = [Part(n, ORDERS[k], sems[6 + k]) for k in range(2)]
+    factor = Part(n, ORDERS[0], sems[8])
+    live_slots(counts, mask10)
+    load_vectors(vectors_in, 0, norm)
+    norm_constants(n, stats1, live, norm, consts)
     back_constants(n, sums1, consts, vectors)
     wait_all()
-    for k in range(4):
+    for k in range(2):
         lasts[k].spread1(columns[k], last_sums[k])
-    for k in range(2):
-        kernels[k].send0(kernel_grads[k], kernel_rooms[k][0])
+        a0, r1, a1, r2, column = kernel_rooms[k]
+        kernels[k].sum0(kernel_grads[k], kernel_arrive[k], a0)
+        kernels[k].send1(a0, r1)
     factor_column[factor.place[2]] = factors[...]
     factor.spread2(factor_column)
     loads[0].wait()
@@ -1018,6 +1068,10 @@
     for t, (a, b) in enumerate(SPANS):
         left = jnp.concatenate([low[j] for j in range(TILES)], axis=1)[:, :HALF]
         put_span(buf_a, t, slice(0, ROWS), dot(left, weight[a:b, :], ((1,), (1,))), add=True)
+    for k in range(2):
+        a0, r1, a1, r2, column = kernel_rooms[k]
+        kernels[k].sum1(a0, r1, a1)
+        kernels[k].send2(a1, r2)
     for_tiles(lambda j: swap(low.at[j], low_far.at[j], swap_s.at[j], swap_r.at[j]).wait())
     loads[5].wait()
     for t, (a, b) in enumerate(SPANS):
@@ -1025,49 +1079,48 @@
         put_span(buf_a, t, slice(0, ROWS), dot(left, weight_far[a:b, :], ((1,), (1,))), add=True)
     store = fetch(buf_a, pixels_grad, load.at[0])
 
-    def advance(part, stage, source, room, result):
-        r0, a0, r1, a1, r2, column = room
-        if stage == 0:
-            part.send0(source, r0)
-        elif stage == 1:
-            part.sum0(source, r0, a0)
-            part.send1(a0, r1)
-        elif stage == 2:
-            part.sum1(a0, r1, a1)
-            part.send2(a1, r2)
-        elif stage == 3:
-            part.sum2(a1, r2, column)
-            part.spread2(column)
-        elif stage == 4:
-            part.spread1(column, result)
-        elif stage == 5:
-            part.spread0(result)
-        else:
-            part.settle()
-
-    def first_to(k, stage):
-        advance(firsts[k], stage, grads[k], first_rooms[k], first_sums[k])
-
-    def kernel_to(stage):
-        for k in range(2):
-            advance(kernels[k], stage, kernel_grads[k], kernel_rooms[k], kernel_sums[k])
-
-    for tick in range(1, 8):
-        for k in range(4):
-            stage = tick - (1 if k >= 2 else 0)
-            if 0 <= stage <= 6 and not (k < 2 and stage == 0):
-                first_to(k, stage)
-        if tick <= 6:
-            kernel_to(tick)
-        if tick == 1:
-            for k in range(4):
-                lasts[k].spread0(last_sums[k])
-            factor.spread1(factor_column, factor_sums)
-        if tick == 2:
-            factor.spread0(factor_sums)
-    for k in range(4):
-        lasts[k].settle()
-    factor.settle()
+    def reduce0(k):
+        r0, a0, r1, a1, r2, column = first_rooms[k]
+        firsts[k].sum0(grads[k], r0, a0)
+        firsts[k].send1(a0, r1)
+
+    def reduce1(k):
+        r0, a0, r1, a1, r2, column = first_rooms[k]
+        firsts[k].sum1(a0, r1, a1)
+        firsts[k].send2(a1, r2)
+
+    def reduce2(k):
+        r0, a0, r1, a1, r2, column = first_rooms[k]
+        firsts[k].sum2(a1, r2, column)
+        firsts[k].spread2(column)
+
+    def each(step, ks):
+        for k in ks:
+            step(k)
+
+    head, tail, two = (0, 1), (2, 3), range(2)
+    each(reduce0, head)
+    each(lambda k: firsts[k].send0(grads[k], first_rooms[k][0]), tail)
+    factor.spread1(factor_column, factor_sums)
+    for k in two:
+        a0, r1, a1, r2, column = kernel_rooms[k]
+        kernels[k].sum2(a1, r2, column)
+        kernels[k].spread2(column)
+    each(reduce1, head)
+    each(reduce0, tail)
+    each(lambda k: lasts[k].spread0(last_sums[k]), two)
+    factor.spread0(factor_sums)
+    each(lambda k: kernels[k].spread1(kernel_rooms[k][4], kernel_sums[k]), two)
+    each(reduce2, head)
+    each(reduce1, tail)
+    each(lambda k: kernels[k].spread0(kernel_sums[k]), two)
+    each(lambda k: firsts[k].spread1(first_rooms[k][5], first_sums[k]), head)
+    each(reduce2, tail)
+    each(lambda k: firsts[k].spread0(first_sums[k]), head)
+    each(lambda k: firsts[k].spread1(first_rooms[k][5], first_sums[k]), tail)
+    each(lambda k: firsts[k].spread0(first_sums[k]), tail)
+    for part in (*firsts, *lasts, *kernels, factor):
+        part.settle()
     store.wait()
 
 
@@ -1130,10 +1183,6 @@
         scratch_shapes=scratch,
         compiler_params=pltpu.CompilerParams(**params),
     )(*ins)
-
-
-def lane_tiles(vector):
-    return jnp.pad(vector, (0, 1024 - HALF)).reshape(TILES, 128)
 
 
 def body(
@@ -1163,128 +1212,113 @@
     sem = DMA((n - 1,))
 
     local_counts = lax.dynamic_slice_in_dim(crop_counts, me * IMGS, IMGS)
-    places = jnp.arange(ROWS_IMG, dtype=jnp.int32)
-    living = (places[None, :] < BIG_ROWS) | (
-        (places[None, :] - BIG_ROWS) // 9 < local_counts[:, None]
+    counts = jnp.broadcast_to(local_counts[:, None], (IMGS, 128))
+    live = jnp.sum((BIG_ROWS + 9 * crop_counts).reshape(n, IMGS), axis=1).astype(F32)
+    live = jnp.broadcast_to(live[:, None, None], (n, TILES, 128))
+    gains = jnp.stack(
+        [first_gain, first_shift, group_gain, group_shift, last_gain, last_shift]
     )
-    mask = jnp.broadcast_to(living.reshape(ROWS, 1).astype(F32), (ROWS, 128))
-    slots = jnp.arange(10, dtype=jnp.int32)[:, None] < local_counts[None, :]
-    mask10 = jnp.broadcast_to(slots[:, :, None].astype(F32), (10, IMGS, 128))
-    per_image = (BIG_ROWS + 9 * crop_counts).astype(F32)
-    live = jnp.sum(per_image.reshape(n, IMGS), axis=1)
-    count = lax.dynamic_slice_in_dim(live, me, 1).reshape(1, 1)
-    live = jnp.broadcast_to(live[:, None, None], (n, TILES, 128))
-    inverse = 1.0 / (BIG_ROWS + 9 * local_counts).astype(F32)
-    inverse = jnp.broadcast_to(inverse[:, None], (IMGS, 128))
-    norm1, norm2, norm3 = (
-        jnp.stack([lane_tiles(gain), lane_tiles(shift)])
-        for gain, shift in (
-            (first_gain, first_shift),
-            (group_gain, group_shift),
-            (last_gain, last_shift),
-        )
-    )
-    kernel = jnp.pad(
-        group_weight.reshape(9 * GROUP_WIDTH, HALF).astype(F32), ((0, 0), (0, 1024 - HALF))
-    )
+    kernel = group_weight.reshape(9 * GROUP_WIDTH, HALF)
     local = pltpu.VMEM((2, TILES, 128), F32)
     consts = pltpu.VMEM((8, TILES, 128), F32)
     vectors = ((2, TILES, 128), F32)
     bands = [pltpu.VMEM(((e - s) * 128, 9 * 256), BF16) for s, e in WINDOWS]
-    smem = pl.BlockSpec(memory_space=pltpu.SMEM)
-
-    first, pixels_far, stats1 = call(
-        functools.partial(first_kernel, n),
-        (count, pixels, first_weight, mask),
-        [(wide, F32), ((ROWS, HALF), BF16), (stat, F32)],
-        [local, DMA((4,)), DMA((4,)), sem, sem],
-        0,
-        in_specs=[smem, VMEM, VMEM, VMEM],
-    )
-    padded, group, stats2, first_far, last_far = call(
-        functools.partial(group_kernel, n),
-        (count, first, stats1, live, norm1, mask10, kernel, first_weight, last_weight),
-        [
-            ((TILES, PAD_ROWS, 128), BF16),
-            (wide, F32),
-            (stat, F32),
-            ((HALF, HALF), BF16),
-            ((HALF, HALF), BF16),
-        ],
-        [consts, local, *bands, DMA((2,)), DMA((2,)), sem, sem],
-        1,
-        in_specs=[smem] + [VMEM] * 6 + [ANY] * 2,
-        out_specs=[VMEM] * 3 + [ANY] * 2,
-    )
+    mask10 = pltpu.VMEM((10, IMGS, 128), F32)
+    mask = pltpu.VMEM((ROWS, 128), F32)
+    kernel_buf = pltpu.VMEM((9 * GROUP_WIDTH, 1024), F32)
     small = (TILES, IMGS, 128)
+    wide_buf = pltpu.VMEM(wide, F32)
+    tall = (ROWS, HALF)
+    split_shapes = [(2 * HALF, se)] * 2 + [(2 * se, HALF)] * 2
     (
+        first,
+        pixels_far,
+        padded,
+        group,
         scaled,
         scaled_far,
         last,
-        stats3,
-        pooled,
-        pooled_far,
-        squeezed,
-        squeezed_far,
-        squeeze_pre,
-        excited,
+        merged_grad,
+        block_out,
+        first_far,
+        last_far,
+        *rest,
     ) = call(
-        functools.partial(gate_kernel, n),
+        functools.partial(forward_kernel, n),
         (
-            count,
-            group,
-            stats2,
+            pixels,
+            first_weight,
+            last_weight,
+            kernel,
+            squeeze_weight,
+            excite_weight,
+            output_grad,
+            counts,
             live,
-            norm2,
-            mask10,
-            inverse,
-            squeeze_weight,
+            gains,
             squeeze_bias[None],
-            excite_weight,
             excite_bias[None],
-            mask,
-            last_weight,
         ),
         [
+            (wide, F32),
+            (tall, BF16),
+            ((TILES, PAD_ROWS, 128), BF16),
+            (wide, F32),
             (wide, BF16),
             (wide, BF16),
             (wide, F32),
-            (stat, F32),
-            (small, F32),
-            (small, F32),
-            ((IMGS, se), F32),
-            ((IMGS, se), F32),
-            ((IMGS, se), F32),
-            (small, F32),
-        ],
+            (wide, F32),
+            (tall, BF16),
+            ((HALF, HALF), BF16),
+            ((HALF, HALF), BF16),
+        ]
+        + [(shape, BF16) for shape in split_shapes]
+        + [(stat, F32)] * 4
+        + [(small, F32)] * 2
+        + [((IMGS, se), F32)] * 3
+        + [(small, F32)],
         [
             consts,
             local,
-            pltpu.VMEM(wide, F32),
-            pltpu.VMEM((ROWS, 128), F32),
+            local,
+            wide_buf,
+            wide_buf,
+            pltpu.VMEM(tall, BF16),
+            pltpu.VMEM(tall, BF16),
+            pltpu.VMEM((2 * HALF, HALF), BF16),
+            pltpu.VMEM((TILES, 2 * ROWS, 128), BF16),
+            pltpu.VMEM((9 * GROUP_WIDTH, HALF), BF16),
+            kernel_buf,
+            pltpu.VMEM((2 * HALF, se), F32),
+            pltpu.VMEM((2 * se, HALF), F32),
+            *(pltpu.VMEM(shape, BF16) for shape in split_shapes),
+            mask,
+            mask,
+            mask10,
+            *bands,
+            DMA((6,)),
+            DMA((13,)),
+            DMA((6,)),
+            DMA((6,)),
             DMA((TILES,)),
             DMA((TILES,)),
             DMA((2,)),
             DMA((2,)),
-            sem,
-            sem,
+            *[sem] * 8,
         ],
-        2,
-        in_specs=[smem] + [VMEM] * 12,
+        0,
+        in_specs=[ANY] * 7 + [VMEM] * 5,
+        out_specs=[ANY] * 15 + [VMEM] * 10,
     )
-    block_out, merged_grad, sums3 = call(
-        functools.partial(merge_kernel, n),
-        (last, stats3, live, norm3, mask, pixels, output_grad),
-        [((ROWS, HALF), BF16), (wide, F32), (stat, F32)],
-        [consts, local, sem, sem],
-        3,
-    )
+    splits, rest = rest[:4], rest[4:]
+    stats1, stats2, stats3, sums3, pooled, pooled_far = rest[:6]
+    squeezed, squeezed_far, squeeze_pre, excited = rest[6:]
+
     def vmem(shape, dtype=BF16):
         return pltpu.VMEM(shape, dtype)
 
     shapes = [part_shape(n, order, 4 * 1024) for order in ORDERS]
     rooms = [Part.room(n, order, shape) for order, shape in zip(ORDERS, shapes)]
-    wide_buf = vmem(wide, F32)
     low_buf = vmem(wide)
     weight_buf = vmem((HALF, HALF))
     pre_grad, sums2, excite_grad, squeeze_grad, vectors3, *carry = call(
@@ -1299,17 +1333,13 @@
             last_far,
             stats3,
             live,
-            norm3,
             sums3,
-            mask,
             stats2,
-            norm2,
-            mask10,
-            inverse,
+            counts,
+            gains,
             excited,
             squeeze_pre,
-            squeeze_weight,
-            excite_weight,
+            *splits,
         ),
         [(wide, F32), (stat, F32), (small, F32), ((IMGS, se), F32), vectors]
         + [(rooms[k][1], BF16) for k in range(4)]
@@ -1326,8 +1356,10 @@
             low_buf,
             weight_buf,
             weight_buf,
-            vmem((2 * HALF, se), F32),
-            vmem((2 * se, HALF), F32),
+            local,
+            mask,
+            mask10,
+            *(vmem(shape) for shape in split_shapes),
             vmem((IMGS, se), F32),
             vmem((IMGS, se), F32),
             vmem((IMGS, HALF), F32),
@@ -1335,7 +1367,7 @@
             vmem(small, F32),
             *(vmem(shape) for shape in shapes),
             *(vmem(room[0]) for room in rooms),
-            DMA((8,)),
+            DMA((10,)),
             DMA((TILES,)),
             DMA((TILES,)),
             DMA((2,)),
@@ -1345,11 +1377,12 @@
             *part_sems(n, 4),
         ],
         4,
-        in_specs=[ANY] * 7 + [VMEM] * 11 + [ANY] * 2,
+        in_specs=[ANY] * 7 + [VMEM] * 8 + [ANY] * 4,
         out_specs=[ANY] + [VMEM] * 10,
     )
     mid1, mid3, arrive1 = carry[0:2], carry[2:4], carry[4:6]
     kernel_shapes = [part_shape(n, ORDERS[k], TILES * 256) for k in range(2)]
+    kernel_rooms = [Part.room(n, ORDERS[k], kernel_shapes[k]) for k in range(2)]
     first_pre_grad, sums1, vectors2, *carry = call(
         functools.partial(group_grad_kernel, n),
         (
@@ -1359,22 +1392,27 @@
             first,
             stats2,
             live,
-            norm2,
             sums2,
-            mask10,
+            counts,
+            gains,
             kernel,
             stats1,
-            norm1,
             *mid1,
             *mid3,
             *arrive1,
         ),
         [(wide, F32), (stat, F32), vectors]
         + [(shape, BF16) for shape in kernel_shapes]
-        + [(room[5], BF16) for room in rooms],
+        + [(room[0], BF16) for room in kernel_rooms]
+        + [(room[5], BF16) for room in rooms[2:]]
+        + [(shape, BF16) for shape in shapes[:2]],
         [
+            *(vmem(room[5]) for room in rooms[:2]),
             consts,
             consts,
+            local,
+            mask10,
+            kernel_buf,
             local,
             wide_buf,
             wide_buf,
@@ -1388,13 +1426,13 @@
             DMA((3,)),
             sem,
             sem,
-            *part_sems(n, 4),
+            *part_sems(n, 6),
         ],
         5,
-        in_specs=[ANY] * 4 + [VMEM] * 14,
-        out_specs=[ANY] + [VMEM] * 8,
+        in_specs=[ANY] * 4 + [VMEM] * 13,
+        out_specs=[ANY] + [VMEM] * 8 + [ANY] * 2,
     )
-    kernel_grads, columns = carry[0:2], carry[2:6]
+    kernel_grads, kernel_arrive, columns, last_early = carry[0:2], carry[2:4], carry[4:6], carry[6:8]
 
     def tiles_of(value):
         return jnp.pad(value, ((0, 0), (0, 256 - se))).reshape(IMGS, 2, 128).swapaxes(0, 1)
@@ -1412,7 +1450,6 @@
     count_tiles = factors.shape[0]
     factors = factors.reshape(count_tiles * IMGS, 128).astype(BF16)
     factor_shape = part_extents(n, ORDERS[0]) + factors.shape
-    kernel_rooms = [Part.room(n, ORDERS[k], kernel_shapes[k]) for k in range(2)]
     pixels_wide, vectors1, *carry = call(
         functools.partial(first_grad_kernel, n),
         (
@@ -1425,18 +1462,21 @@
             merged_grad,
             stats1,
             live,
-            norm1,
             sums1,
-            mask10,
+            counts,
+            gains,
             factors,
             *kernel_grads,
+            *kernel_arrive,
             *columns,
         ),
         [(wide, F32), vectors]
-        + [(shape, BF16) for shape in shapes * 2 + kernel_shapes]
+        + [(shape, BF16) for shape in shapes[2:] + shapes + kernel_shapes]
         + [(factor_shape, BF16)],
         [
             consts,
+            local,
+            mask10,
             wide_buf,
             wide_buf,
             low_buf,
@@ -1448,19 +1488,19 @@
             vmem((ROWS, 128), F32),
             *(vmem(shape) for shape in shapes),
             *(vmem(shape) for room in rooms for shape in room),
-            *(vmem(shape) for room in kernel_rooms for shape in room),
+            *(vmem(shape) for room in kernel_rooms for shape in room[1:]),
             vmem(factor_shape[2:]),
             DMA((6,)),
             DMA((TILES,)),
             DMA((TILES,)),
-            *part_sems(n, 11),
+            *part_sems(n, 9),
         ],
         6,
         in_specs=[ANY] * 7 + [VMEM] * 12,
-        out_specs=[ANY, VMEM] + [ANY] * 11,
+        out_specs=[ANY, VMEM] + [ANY] * 9,
     )
-    sums = [s.reshape(4, 1024, 128) for s in carry[0:8]]
-    kernel_sums = [s.reshape(TILES, 256, 128) for s in carry[8:10]]
+    sums = [s.reshape(4, 1024, 128) for s in (*last_early, *carry[0:6])]
+    kernel_sums = [s.reshape(TILES, 256, 128) for s in carry[6:8]]
     late = pl.BlockSpec((1, 1024, 128), lambda j: (jnp.maximum(j - 4, 0), 0, 0))
     early = pl.BlockSpec((1, 1024, 128), lambda j: (jnp.minimum(j, 3), 0, 0))
     last_weight_grad, first_weight_grad, pixels_grad = call(
@@ -1478,7 +1518,7 @@
     )
     group_weight_grad, squeeze_weight_grad, squeeze_bias_grad, excite_weight_grad, excite_bias_grad = call(
         finish_kernel,
-        (*kernel_sums, carry[10].reshape(n, count_tiles * IMGS, 128)),
+        (*kernel_sums, carry[8].reshape(n, count_tiles * IMGS, 128)),
         [
             ((9 * GROUP_WIDTH, HALF), F32),
             ((2 * HALF, se), F32),

time: 424 us -> 351 us (0.83)
  Pallas kernels: 395 us -> 330 us
  other arithmetic: 9.88 us -> 4.48 us
    pallas_call x9 -> x6, Pallas kernels: 395 us -> 330 us  [call(): pl.pallas_call(kernel, grid=grid, out_shape=[jax.ShapeDtypeStruct(shape,...]
where the time goes in v3:
time: 351 us; the launch traced here: 344 us
  Pallas kernels  330 us (94%)
  local copies, waits for them, and re-layouts  8.45 us (2%)
  other arithmetic  4.48 us (1%)
    pallas_call x6, Pallas kernels, call(): pl.pallas_call(kernel, grid=grid, out_shape=[jax.ShapeDtypeStruct(shape,...  330 us

profile of v3, /device:TPU:10, one launch (start us, length us, event | category | flops | bytes accessed | tf_op | source)
XLA Modules:
  0.0 343.8 jit_solution(10936840397588278129)
XLA Ops:
  0.6 0.7 dynamic_slice.3
  1.4 0.7 multiply_add_fusion
  2.0 0.7 broadcast_in_dim.8.refs_7_.refs_11_.refs_10_
  2.7 0.1 reshape.100
  2.8 0.1 reduce_sum.9
  2.9 1.4 stack.27.refs_9_.refs_12_.refs_8_.refs_11_
  4.3 0.7 broadcast_in_dim.9.refs_8_.refs_5_
  5.0 78.3 %shard_map.271 = (f32[8,1504,128]{2,1,0:T(8,128)}, bf16[1504,1008]{1,0:T(8,128)(2,1)}, bf16[8,2848,128]{2,1,0:T(8,128)(2,1)}, f32[8,1504,128]{2,1,0:T(8,128)}, b...) custom-call(bf16[1504,1008]{1,0:T(8,128)(2,1)} %refs_2_.3, ...), custom_call_target="tpu_custom_call" | custom-call | tf_op jit(solution)/shard_map/pallas_call | solution.py:1177
  83.3 0.7 convert.33
  84.0 0.7 convert.34
  84.7 0.8 convert_dynamic-update-slice_fusion.2
  85.5 0.8 convert_dynamic-update-slice_fusion.1
  86.2 47.1 %shard_map.272 = (f32[8,1504,128]{2,1,0:T(8,128)}, f32[16,2,8,128]{3,2,1,0:T(8,128)}, f32[8,8,128]{2,1,0:T(8,128)}, f32[8,252]{1,0:T(8,128)}, f32[2,8,128]{2,1,0...) custom-call(f32[8,1504,128]{2,1,0:T(8,128)} %get-tuple-element.82.re, ...), custom_call_target="tpu_custom_call" | custom-call | tf_op jit(solution)/shard_map/pallas_call | solution.py:1177
  133.4 0.8 convert_dynamic-update-slice_fusion
  134.2 65.3 %shard_map.273 = (f32[8,1504,128]{2,1,0:T(8,128)}, f32[16,2,8,128]{3,2,1,0:T(8,128)}, f32[2,8,128]{2,1,0:T(8,128)}, bf16[2,2,4,128,128]{4,3,2,1,0:T(8,128)(2,1)}...) custom-call(f32[8,1504,128]{2,1,0:T(8,128)} %get-tuple-element.97.re, ...), custom_call_target="tpu_custom_call" | custom-call | tf_op jit(solution)/shard_map/pallas_call | solution.py:1177
  199.6 0.6 copy-done.1
  200.2 119.6 %shard_map.274 = (f32[8,1504,128]{2,1,0:T(8,128)}, f32[2,8,128]{2,1,0:T(8,128)}, bf16[2,2,4,256,128]{4,3,2,1,0:T(8,128)(2,1)}, bf16[2,2,4,256,128]{4,3,2,1,0:T(8...) custom-call(f32[8,1504,128]{2,1,0:T(8,128)} %get-tuple-element.110.r, ...), custom_call_target="tpu_custom_call" | custom-call | tf_op jit(solution)/shard_map/pallas_call | solution.py:1177
  319.7 0.7 copy.39
  320.5 0.6 fusion.2
  321.1 0.6 fusion.1
  321.7 0.6 fusion
  322.3 4.6 %shard_map.276 = (f32[504,1008]{1,0:T(8,128)}, f32[2016,252]{1,0:T(8,128)}, f32[1,252]{1,0:T(1,128)}, f32[504,1008]{1,0:T(8,128)}, f32[1,1008]{1,0:T(1,128)}) custom-call(bf16[8,256,128]{2,1,0:T(8,128)(2,1)} %bitcast.65, bf16[8,256,128]{2,1,0:T(8,128)(2,1)} %bitcast.66, bf16[16,240,128]{2,1,0:T(8,128)(2,1)} %bitcast.64), custom_call_target="tpu_custom_call" | custom-call | tf_op jit(solution)/shard_map/pallas_call | solution.py:1177
  326.9 14.9 %shard_map.275 = (f32[2016,1008]{1,0:T(8,128)}, f32[2016,1008]{1,0:T(8,128)}, f32[1504,1008]{1,0:T(8,128)}) custom-call(bf16[4,1024,128]{2,1,0:T(8,128)(2,1)} %bitcast.56, bf16[4,1024,128]{2,1,0:T(8,128)(2,1)} %bitcast.57, bf16[4,1024,128]{2,1,0:T(8,128)(2,1)} %bitcast.58, bf16[4,1024,128]{2,1,0:T(8,128)(2,1)} %bitcast.59, bf16[4,1024,128]{2,1,0:T(8,128)(2,1)} %bitcast.60, ...), custom_call_target="tpu_custom_call" | custom-call | tf_op jit(solution)/shard_map/pallas_call | solution.py:1177
  341.9 1.6 copy.46
  (16 shorter events, 0.1 us)
Async XLA Ops:
  134.2 65.4 %copy-start.2 = (f32[8,252]{1,0:T(8,128)S(1)}, f32[8,252]{1,0:T(8,128)}, u32[]{:S(2)}) copy-start(f32[8,252]{1,0:T(8,128)} %get-tuple-element.119) | copy-start | bytes 24196
  199.5 0.6 copy-start.1
  200.2 120.9 %copy-start.4 = (f32[2,8,128]{2,1,0:T(8,128)S(1)}, f32[2,8,128]{2,1,0:T(8,128)}, u32[]{:S(2)}) copy-start(f32[2,8,128]{2,1,0:T(8,128)} %get-tuple-element.140) | copy-start | bytes 24580
  200.2 121.5 %copy-start.3 = (f32[2,8,128]{2,1,0:T(8,128)S(1)}, f32[2,8,128]{2,1,0:T(8,128)}, u32[]{:S(2)}) copy-start(f32[2,8,128]{2,1,0:T(8,128)} %get-tuple-element.146) | copy-start | bytes 24580
  326.9 15.0 %copy-start = (bf16[1504,1008]{1,0:T(8,128)(2,1)S(1)}, bf16[1504,1008]{1,0:T(8,128)(2,1)}, u32[]{:S(2)}) copy-start(bf16[1504,1008]{1,0:T(8,128)(2,1)} %get-tuple-element.168) | copy-start | bytes 9096196

commit v4 on v3

--- a/solution.py
+++ b/solution.py
@@ -232,29 +232,41 @@
     return jnp.concatenate(pieces, axis=0)
 
 
-def build_bands(kernel, bands):
-    for span, (first, end) in enumerate(WINDOWS):
-        base = first * 128
-        depth = (end - first) * 128
-        lane = lax.broadcasted_iota(jnp.int32, (GROUP_WIDTH, 256), 1) + span * 256
-        groups = range(span * 256 // GROUP_WIDTH, min(18, (span * 256 + 255) // GROUP_WIDTH + 1))
-        masks = [
-            (lane >= g * GROUP_WIDTH) & (lane < (g + 1) * GROUP_WIDTH) for g in groups
-        ]
-        head = groups[0] * GROUP_WIDTH - base
-        tail = depth - head - len(groups) * GROUP_WIDTH
-        for tap in range(9):
-            piece = kernel[
-                tap * GROUP_WIDTH : (tap + 1) * GROUP_WIDTH, span * 256 : span * 256 + 256
-            ]
-            parts = [jnp.where(m, piece, 0.0) for m in masks]
-            if head:
-                parts.insert(0, jnp.zeros((head, 256), F32))
-            if tail:
-                parts.append(jnp.zeros((tail, 256), F32))
-            bands[span][:, tap * 256 : tap * 256 + 256] = jnp.concatenate(parts, axis=0).astype(
-                BF16
-            )
+def span_groups(span):
+    return range(span * 256 // GROUP_WIDTH, min(18, (span * 256 + 255) // GROUP_WIDTH + 1))
+
+
+def span_masks(span):
+    lane = lax.broadcasted_iota(jnp.int32, (GROUP_WIDTH, 256), 1) + span * 256
+    return [(lane >= g * GROUP_WIDTH) & (lane < (g + 1) * GROUP_WIDTH) for g in span_groups(span)]
+
+
+def tap_rows(kernel, tap, span):
+    first = tap * GROUP_WIDTH
+    start = first // 16 * 16
+    end = min(9 * GROUP_WIDTH, (first + GROUP_WIDTH + 15) // 16 * 16)
+    a, b = SPANS[span]
+    piece = kernel[start:end, a:b].astype(F32)[first - start : first - start + GROUP_WIDTH]
+    if b - a < 256:
+        piece = jnp.concatenate([piece, jnp.zeros((GROUP_WIDTH, 256 - (b - a)), F32)], axis=1)
+    return piece
+
+
+def build_band(kernel, span, band):
+    first, end = WINDOWS[span]
+    depth = (end - first) * 128
+    groups = span_groups(span)
+    masks = span_masks(span)
+    head = groups[0] * GROUP_WIDTH - first * 128
+    tail = depth - head - len(groups) * GROUP_WIDTH
+    for tap in range(9):
+        piece = tap_rows(kernel, tap, span)
+        parts = [jnp.where(m, piece, 0.0) for m in masks]
+        if head:
+            parts.insert(0, jnp.zeros((head, 256), F32))
+        if tail:
+            parts.append(jnp.zeros((tail, 256), F32))
+        band[0:depth, tap * 256 : tap * 256 + 256] = jnp.concatenate(parts, axis=0).astype(BF16)
 
 
 def zero_pads(ref, j):
@@ -302,19 +314,22 @@
     r = Refs(refs)
     pixels_any, weight1_any, weight3_any, kernel_any, squeeze_any, excite_any, output_any = r.take(7)
     counts, live, vectors, squeeze_b, excite_b = r.take(5)
-    first_out, far_out, padded_out, group_out, scaled_out, scaled_far_out = r.take(6)
+    first_out, pixels_out, far_out, padded_out, group_out, scaled_out, scaled_far_out = r.take(7)
     last_out, merged_out, block_out = r.take(3)
     far1, far3 = r.take(2)
     split_outs = r.take(4)
     stats1, stats2, stats3, sums3 = r.take(4)
     pooled, pooled_far, squeezed, squeezed_far, squeeze_pre, excited = r.take(6)
+    factor_sums = r.take()
     consts, norm, local, buf_a, buf_b, pixels, far, weight, zone = r.take(9)
-    kernel_low, kernel, squeeze_w, excite_w = r.take(4)
+    kernel_low, squeeze_w, excite_w = r.take(3)
     splits = r.take(4)
     turned, mask, mask10 = r.take(3)
     bands = r.take(4)
     load, store, swap_s, swap_r, tile_s, tile_r, small_s, small_r = r.take(8)
     gathers = [r.take(2) for _ in range(4)]
+    factor_column, factors = r.take(2)
+    factor = Part(n, ORDERS[0], r.take(2))
     ch = lax.axis_index("ch")
     wait_all = greet(n)
     loads = [
@@ -361,19 +376,31 @@
     for s in weight_swaps:
         s.start()
     load_weight = fetch(weight3_any, weight, load.at[0])
-    store_far = fetch(far, far_out, store.at[0])
+    mine_rows, far_rows = pl.ds(0, ROWS), pl.ds(ROWS, ROWS)
+    for source, start in ((pixels, 0), (far, ROWS)):
+        for j in range(TILES):
+            width = 128 if j < 7 else LAST
+            lanes = slice(j * 128, j * 128 + width)
+            zone[j, start : start + ROWS, 0:width] = source[:, lanes]
+    zone[7, :, LAST:128] = jnp.zeros((2 * ROWS, 128 - LAST), BF16)
+    store_pixels = [
+        fetch(zone.at[:, mine_rows], pixels_out, store.at[0]),
+        fetch(zone.at[:, far_rows], far_out, store.at[12]),
+    ]
     stores = []
     store_first = fetch(buf_a, first_out, store.at[1])
     loads[2].wait()
-    kernel[:, 0:HALF] = kernel_low[...].astype(F32)
-    kernel[:, HALF:1024] = jnp.zeros((9 * GROUP_WIDTH, 1024 - HALF), F32)
-    build_bands(kernel, bands)
+    for span in range(4):
+        build_band(kernel_low, span, bands[span])
     loads[3].wait()
     loads[4].wait()
     for k, w in enumerate((squeeze_w, excite_w)):
         splits[2 * k][...], splits[2 * k + 1][...] = halves(w[...])
     stores += [fetch(splits[k], split_outs[k], store.at[2 + k]) for k in range(4)]
     load_vectors(vectors, 0, norm)
+    load_output = fetch(output_any, far, load.at[1])
+    for s in store_pixels:
+        s.wait()
     gather.wait()
     norm_constants(n, stats1, live, norm, consts)
 
@@ -409,8 +436,6 @@
     load_vectors(vectors, 2, norm)
     store_first.wait()
     store_padded.wait()
-    store_far.wait()
-    load_output = fetch(output_any, far, load.at[1])
     gather.wait()
     norm_constants(n, stats2, live, norm, consts)
     inverse = 1.0 / (BIG_ROWS + 9.0 * counts[...].astype(F32))
@@ -453,7 +478,9 @@
     for j in range(TILES - 1):
         excited[j] = gate[:, j * 128 : j * 128 + 128]
     excited[7, :, 0:LAST] = gate[:, 7 * 128 :]
-    mine_rows, far_rows = pl.ds(0, ROWS), pl.ds(ROWS, ROWS)
+    pack_factors((pooled, pooled_far), (squeezed, squeezed_far), factors)
+    factor_column[factor.place[2]] = factors[...]
+    factor.spread2(factor_column)
 
     def tile_swap(j):
         return swap(zone.at[j, mine_rows], zone.at[j, far_rows], tile_s.at[j], tile_r.at[j])
@@ -475,6 +502,7 @@
         left = jnp.concatenate([zone[j, 0:ROWS, :] for j in range(TILES)], axis=1)[:, :HALF]
         put_span(buf_b, t, slice(0, ROWS), dot(left, weight[pl.ds(own, HALF), a:b]))
     buf_b[7, :, LAST:128] = jnp.zeros((ROWS, 128 - LAST), F32)
+    factor.spread1(factor_column, factor_sums)
     for_tiles(lambda j: tile_swap(j).wait())
     stores.append(fetch(zone.at[:, far_rows], scaled_far_out, store.at[9]))
     for t, (a, b) in enumerate(SPANS):
@@ -485,6 +513,7 @@
     gather.start()
     stores.append(fetch(buf_b, last_out, store.at[10]))
     load_vectors(vectors, 4, norm)
+    factor.spread0(factor_sums)
     buf_a[7, :, LAST:128] = jnp.zeros((ROWS, 128 - LAST), F32)
     load_output.wait()
     gather.wait()
@@ -509,9 +538,10 @@
     gather = Gather(n, local, sums3, *gathers[3])
     gather.start()
     stores.append(fetch(buf_a, merged_out, store.at[11]))
-    stores.append(fetch(far, block_out, store.at[12]))
+    stores.append(fetch(far, block_out, store.at[13]))
     for s in weight_swaps + stores:
         s.wait()
+    factor.settle()
     gather.wait()
 
 
@@ -549,16 +579,16 @@
             put_blocks(target, 2 * k + 1, 1024, a, value[:, 128:])
 
 
-def tile_span(ref):
+def tile_span(tile):
     def span(a, b):
         tiles = range(a // 128, (b + 127) // 128)
-        return jnp.concatenate([ref[t] for t in tiles], axis=1)[:, : b - a]
+        return jnp.concatenate([tile(t) for t in tiles], axis=1)[:, : b - a]
 
     return span
 
 
 def image_axes(n):
-    return {16: (2, 2, 4), 128: (8, 4, 4)}.get(n, (n, 1, 1))
+    return {16: (2, 2, 4), 128: (4, 4, 8)}.get(n, (n, 1, 1))
 
 
 class Part:
@@ -681,6 +711,9 @@
 
 
 ORDERS = ((0, 1, 2), (1, 0, 2), (0, 1, 2), (1, 0, 2))
+KERNEL_ORDERS = ORDERS[:2]
+AHEAD_TILES = 20
+BACK_TILES = 10
 
 
 def last_grad_kernel(n, *refs):
@@ -690,13 +723,12 @@
     stats2, counts, vectors_in, excited, squeeze_pre = r.take(5)
     split_anys = r.take(4)
     pre_grad, sums2, excite_grad, squeeze_grad, vectors = r.take(5)
-    mid1, mid3 = r.take(2), r.take(2)
-    arrive1 = r.take(2)
+    done1, arrive2, mid3 = r.take(2), r.take(2), r.take(2)
     consts, consts2, local, buf_a, buf_b, low, low_far, scaled, scaled_far = r.take(9)
     weight, weight_far, norm, mask, mask10 = r.take(5)
     splits = r.take(4)
     terms, terms_in, pool_terms, pool_in, pool_tiles = r.take(5)
-    grads, rooms = r.take(4), r.take(4)
+    grads, rooms, mid1, arrive1 = r.take(4), r.take(4), r.take(2), r.take(2)
     load, swap_s, swap_r, small_s, small_r, send, recv = r.take(7)
     sems = r.take(8)
     ch = lax.axis_index("ch")
@@ -740,7 +772,8 @@
     for part in range(4):
         if part < 2:
             loads[2 + part].wait()
-        left = tile_span((scaled, scaled_far)[part % 2])
+        rows = (scaled, scaled_far)[part % 2]
+        left = tile_span(lambda t: rows[t])
         weight_grad(left, lambda t: low[t], grads[part], (0, 1) if part < 2 else (2, 3))
         if part < 2:
             parts[part].send0(grads[part], rooms[part])
@@ -774,7 +807,6 @@
     for k in range(2):
         parts[k].sum0(grads[k], rooms[k], mid1[k])
         parts[k].send1(mid1[k], arrive1[k])
-        parts[k + 2].send0(grads[k + 2], rooms[k + 2])
     wide = jnp.concatenate([excite_grad[j] for j in range(TILES)], axis=1)[:, :HALF]
     width = squeeze_pre.shape[1]
     is_low = ch == 0
@@ -798,6 +830,10 @@
     pool_swap = swap(pool_terms, pool_in, small_s.at[1], small_r.at[1])
     pool_swap.start()
     pool_swap.wait()
+    for k in range(2):
+        parts[k].sum1(mid1[k], arrive1[k], done1[k])
+        parts[k].send2(done1[k], arrive2[k])
+        parts[k + 2].send0(grads[k + 2], rooms[k + 2])
     pool = jnp.where(is_low, pool0, pool1) + pool_in[...]
     pool_tiles[7, :, LAST:128] = jnp.zeros((IMGS, 128 - LAST), F32)
     for j in range(TILES):
@@ -834,53 +870,127 @@
     store.wait()
 
 
-def group_grad_kernel(n, *refs):
+def pack_factors(wides, narrows, factors):
+    tiles = [part[j] for part in wides for j in range(TILES)]
+    for part in narrows:
+        rest = part[:, 128:]
+        blank = jnp.zeros((IMGS, 128 - rest.shape[1]), F32)
+        tiles += [part[:, 0:128], jnp.concatenate([rest, blank], axis=1)]
+    for k in range(0, len(tiles), 2):
+        both = jnp.concatenate(tiles[k : k + 2], axis=0)
+        factors[k * IMGS : (k + 2) * IMGS, :] = both.astype(BF16)
+
+
+def tail_kernel(n, *refs):
     r = Refs(refs)
     pre_any, group_any, padded_any, first_any = r.take(4)
-    stats2, live, sums2, counts, vectors_in, kernel_low, stats1 = r.take(7)
-    mid1, mid3, arrive1 = r.take(2), r.take(2), r.take(2)
-    first_pre_grad, sums1, vectors = r.take(3)
-    kernel_grads, kernel_arrive = r.take(2), r.take(2)
-    columns = r.take(2)
-    last_sums = r.take(2)
-    early_columns = r.take(2)
-    consts, consts1, norm, mask10, kernel = r.take(5)
-    local, buf_a, buf_b, padded_grad, padded, full = r.take(6)
-    bands = r.take(4)
-    arrive3, a1, r2 = r.take(2), r.take(4), r.take(4)
-    load, send, recv = r.take(3)
-    sems = r.take(12)
-    wait_all = greet(n, partner=False)
-    columns = early_columns + columns
+    pixels_any, pixels_far_any, weight_any, weight_far_any, merged_any = r.take(5)
+    stats2, live, sums2, counts, vectors_in, kernel, stats1 = r.take(7)
+    done1, arrive2, mid3 = r.take(2), r.take(2), r.take(2)
+    factor_parts = r.take(2)
+    pixels_grad, group_vectors, first_vectors = r.take(3)
+    last_sums, first_sums, kernel_sums = r.take(4), r.take(4), r.take(2)
+    factor_sums = r.take()
+    consts, consts1, norm, mask10, local, sums1 = r.take(6)
+    buf_a, buf_b, zone1, zone2, weight, weight_far, turned = r.take(7)
+    bands = r.take(2)
+    arrive3, done3, arrive4, last_columns = r.take(2), r.take(2), r.take(2), r.take(4)
+    grads = r.take(4)
+    first_rooms = [r.take(6) for _ in range(4)]
+    kernel_grads = r.take(2)
+    kernel_rooms = [r.take(6) for _ in range(2)]
+    factor_column, factors = r.take(2)
+    load, swap_s, swap_r, send, recv, free = r.take(6)
+    sems = [r.take(2) for _ in range(11)]
+    own = pl.multiple_of(lax.axis_index("ch") * HALF, 16)
+    mine_rows, far_rows = pl.ds(0, ROWS), pl.ds(ROWS, ROWS)
+    wait_all = greet(n)
     loads = [
         fetch(source, target, load.at[k])
         for k, (source, target) in enumerate(
-            ((pre_any, buf_a), (group_any, buf_b), (padded_any, padded))
+            (
+                (pre_any, buf_a),
+                (group_any, buf_b),
+                (padded_any, zone1.at[:, pl.ds(0, PAD_ROWS)]),
+                (weight_any.at[pl.ds(own, HALF)], weight),
+                (weight_far_any, weight_far),
+            )
         )
     ]
-    parts = [Part(n, order, sems[2 * k : 2 * k + 2]) for k, order in enumerate(ORDERS)]
-    kernels = [Part(n, ORDERS[k], sems[8 + 2 * k : 10 + 2 * k]) for k in range(2)]
+    firsts = [Part(n, order, sems[k]) for k, order in enumerate(ORDERS)]
+    lasts = [Part(n, order, sems[4 + k]) for k, order in enumerate(ORDERS)]
+    kernels = [Part(n, KERNEL_ORDERS[k], sems[8 + k]) for k in range(2)]
+    factor = Part(n, ORDERS[0], sems[10])
     live_slots(counts, mask10)
     load_vectors(vectors_in, 2, norm)
     norm_constants(n, stats2, live, norm, consts)
-    back_constants(n, sums2, consts, vectors)
+    back_constants(n, sums2, consts, group_vectors)
     load_vectors(vectors_in, 0, norm)
     norm_constants(n, stats1, live, norm, consts1)
     wait_all()
-    for k in range(2):
-        parts[k].sum1(mid1[k], arrive1[k], a1[k])
-        parts[k].send2(a1[k], r2[k])
-        parts[k + 2].send1(mid3[k], arrive3[k])
-    kernel[:, 0:HALF] = kernel_low[...].astype(F32)
-    kernel[:, HALF:1024] = jnp.zeros((9 * GROUP_WIDTH, 1024 - HALF), F32)
-    build_bands(kernel, bands)
+
+    def each(step, ks):
+        for k in ks:
+            step(k)
+
+    def last1(k):
+        lasts[k].sum1(mid3[k - 2], arrive3[k - 2], done3[k - 2])
+        lasts[k].send2(done3[k - 2], arrive4[k - 2])
+
+    def last2(k):
+        lasts[k].sum2((*done1, *done3)[k], (*arrive2, *arrive4)[k], last_columns[k])
+        lasts[k].spread2(last_columns[k])
+
+    def last3(k):
+        lasts[k].spread1(last_columns[k], last_sums[k])
+
+    def last4(k):
+        lasts[k].spread0(last_sums[k])
+
+    def reducer(part, source, room, result):
+        r0, a0, r1, a1, r2, column = room
+
+        def stage0():
+            part.send0(source, r0)
+
+        def stage1():
+            part.sum0(source, r0, a0)
+            part.send1(a0, r1)
+
+        def stage2():
+            part.sum1(a0, r1, a1)
+            part.send2(a1, r2)
+
+        def stage3():
+            part.sum2(a1, r2, column)
+            part.spread2(column)
+
+        return (
+            stage0,
+            stage1,
+            stage2,
+            stage3,
+            lambda: part.spread1(column, result),
+            lambda: part.spread0(result),
+        )
+
+    first = [reducer(firsts[k], grads[k], first_rooms[k], first_sums[k]) for k in range(4)]
+    kernel_sum = [
+        reducer(kernels[k], kernel_grads[k], kernel_rooms[k], kernel_sums[k]) for k in range(2)
+    ]
+    head, back, two = (0, 1), (2, 3), range(2)
+    each(last2, head)
+    for k in two:
+        lasts[k + 2].send1(mid3[k], arrive3[k])
+    for span in range(2):
+        build_band(kernel, span, bands[span])
     loads[0].wait()
     loads[1].wait()
 
-    def step(j):
+    def group_step(j):
         average, scale = row_of(consts, 0, j), row_of(consts, 1, j)
         less, slope, front = row_of(consts, 5, j), row_of(consts, 6, j), row_of(consts, 7, j)
-        zero_pads(padded_grad, j)
+        zero_pads(zone2, j)
         for tile in range(0, ROWS_IMG, 2):
             both = []
             for half in range(2):
@@ -891,43 +1001,27 @@
                     grad = grad * mask10[(tile + half - BIG_ROWS) % 10]
                 both.append(grad)
             row = padded_row(tile)
-            padded_grad[j, row : row + 16, :] = jnp.concatenate(both, axis=0).astype(BF16)
-
-    for_tiles(step)
+            zone2[j, row : row + 16, :] = jnp.concatenate(both, axis=0).astype(BF16)
+
+    for_tiles(group_step)
     load_first = fetch(first_any, buf_b, load.at[0])
+    each(last1, back)
+    pack_factors(factor_parts[:1], factor_parts[1:], factors)
+    factor_column[factor.place[2]] = factors[...]
+    factor.spread2(factor_column)
     loads[2].wait()
-
-    for k in range(2):
-        parts[k].sum2(a1[k], r2[k], columns[k])
-        parts[k].spread2(columns[k])
-
-    def advance(span):
-        if span == 0:
-            for k in range(2, 4):
-                parts[k].sum1(mid3[k - 2], arrive3[k - 2], a1[k])
-                parts[k].send2(a1[k], r2[k])
-        elif span == 1:
-            for k in range(2):
-                parts[k].spread1(columns[k], last_sums[k])
-        elif span == 2:
-            for k in range(2):
-                parts[k].spread0(last_sums[k])
-            for k in range(2, 4):
-                parts[k].sum2(a1[k], r2[k], columns[k])
-                parts[k].spread2(columns[k])
-        else:
-            for k in range(2):
-                kernels[k].send0(kernel_grads[k], kernel_arrive[k])
-
     started = 0
     for span, (start, end) in enumerate(WINDOWS):
         tiles = (2 * span, 2 * span + 1)
+        depth = (end - start) * 128
+        band = bands[span % 2]
+        if span >= 2:
+            build_band(kernel, span, band)
         shifted = [
-            jnp.concatenate([window(padded_grad, tiles, -dy, -dx, big) for dy, dx in TAPS], axis=1)
-            for big in (True, False)
+            [window(zone2, tiles, -dy, -dx, big) for dy, dx in TAPS] for big in (True, False)
         ]
         for rows, left in ((slice(0, 784), shifted[0]), (slice(784, ROWS), shifted[1])):
-            value = dot(left, bands[span][...], ((1,), (1,)))
+            value = dot(jnp.concatenate(left, axis=1), band[0:depth, :], ((1,), (1,)))
             for t in range(start, end):
                 part = value[:, (t - start) * 128 : (t - start) * 128 + 128]
                 if t < started:
@@ -935,21 +1029,18 @@
                 else:
                     buf_a[t, rows, :] = part
         started = end
-        right = jnp.concatenate(shifted, axis=0)
-        for t in range(start, end, 2):
-            pair = range(t, min(t + 2, end))
-            left = jnp.concatenate([window(padded, pair, 0, 0, big) for big in (True, False)], axis=0)
-            base = (t - start) * 128
-            full[base : base + 128 * len(pair), :] = dot(left, right, ((0,), (0,)))
-        lane = lax.broadcasted_iota(jnp.int32, (GROUP_WIDTH, 256), 1) + span * 256
+        masks = span_masks(span)
+        left = jnp.concatenate(
+            [window(zone1, range(start, end), 0, 0, big) for big in (True, False)], axis=0
+        )
         pieces = []
         for tap in range(9):
+            right = jnp.concatenate([shifted[0][tap], shifted[1][tap]], axis=0)
+            value = dot(left, right, ((0,), (0,)))
             piece = jnp.zeros((GROUP_WIDTH, 256), F32)
-            for g in range(span * 256 // GROUP_WIDTH, min(18, (span * 256 + 255) // GROUP_WIDTH + 1)):
+            for g, inside in zip(span_groups(span), masks):
                 row = g * GROUP_WIDTH - start * 128
-                inside = (lane >= g * GROUP_WIDTH) & (lane < (g + 1) * GROUP_WIDTH)
-                block = full[row : row + GROUP_WIDTH, tap * 256 : tap * 256 + 256]
-                piece = jnp.where(inside, block, piece)
+                piece = jnp.where(inside, value[row : row + GROUP_WIDTH], piece)
             pieces.append(piece)
         pieces.append(jnp.zeros((8, 256), F32))
         value = jnp.concatenate(pieces, axis=0).astype(BF16)
@@ -957,10 +1048,27 @@
             rows = slice(half * 256, half * 256 + 256)
             put_blocks(kernel_grads[half], 2 * span, 256, 0, value[rows, :128])
             put_blocks(kernel_grads[half], 2 * span + 1, 256, 0, value[rows, 128:])
-        advance(span)
+        if span == 0:
+            each(last3, head)
+        elif span == 1:
+            each(last4, head)
+            factor.spread1(factor_column, factor_sums)
+        elif span == 2:
+            each(last2, back)
+        else:
+            for k in two:
+                kernel_sum[k][0]()
+            factor.spread0(factor_sums)
+    pl.semaphore_signal(
+        free, 1, device_id={"ch": 1 - lax.axis_index("ch")}, device_id_type=MESH
+    )
+    load_pixels = [
+        fetch(pixels_any, zone2.at[:, mine_rows], load.at[1]),
+        fetch(pixels_far_any, zone2.at[:, far_rows], load.at[2]),
+    ]
     load_first.wait()
 
-    def slopes(j):
+    def first_slopes(j):
         average, scale = row_of(consts1, 0, j), row_of(consts1, 1, j)
         gain, shift = row_of(consts1, 2, j), row_of(consts1, 3, j)
         total = jnp.zeros((IMGS, 128), F32)
@@ -979,69 +1087,19 @@
         local[0, pl.ds(j, 1), :] = jnp.sum(total, axis=0, keepdims=True)
         local[1, pl.ds(j, 1), :] = jnp.sum(total_normed, axis=0, keepdims=True)
 
-    for_tiles(slopes)
+    for_tiles(first_slopes)
     gather = Gather(n, local, sums1, send, recv)
     gather.start()
-    store = fetch(buf_a, first_pre_grad, load.at[0])
+    each(last3, back)
     gather.wait()
-    for part in parts + kernels:
-        part.settle()
-    store.wait()
-
-
-def first_grad_kernel(n, *refs):
-    r = Refs(refs)
-    pre_any, first_any, pixels_any, pixels_far_any, weight_any, weight_far_any, merged_any = r.take(7)
-    stats1, live, sums1, counts, vectors_in, factors = r.take(6)
-    kernel_grads, kernel_arrive, columns = r.take(2), r.take(2), r.take(2)
-    pixels_grad, vectors = r.take(2)
-    last_sums, first_sums, kernel_sums = r.take(2), r.take(4), r.take(2)
-    factor_sums = r.take()
-    consts, norm, mask10 = r.take(3)
-    buf_a, buf_b, low, low_far, pixels, pixels_far, weight, weight_far, turned = r.take(9)
-    grads = r.take(4)
-    first_rooms = [r.take(6) for _ in range(4)]
-    kernel_rooms = [r.take(5) for _ in range(2)]
-    factor_column = r.take()
-    load, swap_s, swap_r = r.take(3)
-    sems = [r.take(2) for _ in range(9)]
-    own = pl.multiple_of(lax.axis_index("ch") * HALF, 16)
-    wait_all = greet(n)
-    loads = [
-        fetch(source, target, load.at[k])
-        for k, (source, target) in enumerate(
-            (
-                (pre_any, buf_a),
-                (first_any, buf_b),
-                (pixels_any, pixels),
-                (pixels_far_any, pixels_far),
-                (weight_any.at[pl.ds(own, HALF)], weight),
-                (weight_far_any, weight_far),
-            )
-        )
-    ]
-    firsts = [Part(n, order, sems[k]) for k, order in enumerate(ORDERS)]
-    lasts = [Part(n, ORDERS[2 + k], sems[4 + k]) for k in range(2)]
-    kernels = [Part(n, ORDERS[k], sems[6 + k]) for k in range(2)]
-    factor = Part(n, ORDERS[0], sems[8])
-    live_slots(counts, mask10)
-    load_vectors(vectors_in, 0, norm)
-    norm_constants(n, stats1, live, norm, consts)
-    back_constants(n, sums1, consts, vectors)
-    wait_all()
-    for k in range(2):
-        lasts[k].spread1(columns[k], last_sums[k])
-        a0, r1, a1, r2, column = kernel_rooms[k]
-        kernels[k].sum0(kernel_grads[k], kernel_arrive[k], a0)
-        kernels[k].send1(a0, r1)
-    factor_column[factor.place[2]] = factors[...]
-    factor.spread2(factor_column)
-    loads[0].wait()
-    loads[1].wait()
-
-    def step(j):
-        average, scale = row_of(consts, 0, j), row_of(consts, 1, j)
-        less, slope, front = row_of(consts, 5, j), row_of(consts, 6, j), row_of(consts, 7, j)
+    back_constants(n, sums1, consts1, first_vectors)
+
+    def tile_swap(j):
+        return swap(zone1.at[j, mine_rows], zone1.at[j, far_rows], swap_s.at[j], swap_r.at[j])
+
+    def first_step(j):
+        average, scale = row_of(consts1, 0, j), row_of(consts1, 1, j)
+        less, slope, front = row_of(consts1, 5, j), row_of(consts1, 6, j), row_of(consts1, 7, j)
         for tile in range(ROWS_IMG):
             there = pl.ds(natural_row(tile), IMGS, stride=ROWS_IMG)
             normed = (buf_b[j, there, :] - average) * scale
@@ -1049,76 +1107,60 @@
             if tile >= BIG_ROWS:
                 grad = grad * mask10[(tile - BIG_ROWS) % 10]
             turned[there, :] = grad
-        low[j] = turned[...].astype(BF16)
-        swap(low.at[j], low_far.at[j], swap_s.at[j], swap_r.at[j]).start()
-
-    for_tiles(step)
+        zone1[j, 0:ROWS, :] = turned[...].astype(BF16)
+        tile_swap(j).start()
+
+    pl.semaphore_wait(free, 1)
+    for_tiles(first_step)
     load_merged = fetch(merged_any, buf_a, load.at[0])
+    for s in load_pixels:
+        s.wait()
     for part in range(4):
-        if part < 2:
-            loads[2 + part].wait()
-        rows = (pixels, pixels_far)[part % 2]
+        side = slice(0, ROWS) if part % 2 == 0 else slice(ROWS, 2 * ROWS)
         weight_grad(
-            lambda a, b: rows[:, a:b], lambda t: low[t], grads[part], (0, 1) if part < 2 else (2, 3)
+            tile_span(lambda t: zone2[t, side, :]),
+            lambda t: zone1[t, 0:ROWS, :],
+            grads[part],
+            (0, 1) if part < 2 else (2, 3),
         )
         if part < 2:
-            firsts[part].send0(grads[part], first_rooms[part][0])
+            first[part][0]()
+    for k in two:
+        kernel_sum[k][1]()
     load_merged.wait()
+    loads[3].wait()
+    for t, (a, b) in enumerate(SPANS):
+        left = jnp.concatenate([zone1[j, 0:ROWS, :] for j in range(TILES)], axis=1)[:, :HALF]
+        put_span(buf_a, t, slice(0, ROWS), dot(left, weight[a:b, :], ((1,), (1,))), add=True)
+    for_tiles(lambda j: tile_swap(j).wait())
     loads[4].wait()
     for t, (a, b) in enumerate(SPANS):
-        left = jnp.concatenate([low[j] for j in range(TILES)], axis=1)[:, :HALF]
-        put_span(buf_a, t, slice(0, ROWS), dot(left, weight[a:b, :], ((1,), (1,))), add=True)
-    for k in range(2):
-        a0, r1, a1, r2, column = kernel_rooms[k]
-        kernels[k].sum1(a0, r1, a1)
-        kernels[k].send2(a1, r2)
-    for_tiles(lambda j: swap(low.at[j], low_far.at[j], swap_s.at[j], swap_r.at[j]).wait())
-    loads[5].wait()
-    for t, (a, b) in enumerate(SPANS):
-        left = jnp.concatenate([low_far[j] for j in range(TILES)], axis=1)[:, :HALF]
-        put_span(buf_a, t, slice(0, ROWS), dot(left, weight_far[a:b, :], ((1,), (1,))), add=True)
+        left = jnp.concatenate([zone1[j, ROWS : 2 * ROWS, :] for j in range(TILES)], axis=1)
+        put_span(
+            buf_a, t, slice(0, ROWS), dot(left[:, :HALF], weight_far[a:b, :], ((1,), (1,))), add=True
+        )
     store = fetch(buf_a, pixels_grad, load.at[0])
 
-    def reduce0(k):
-        r0, a0, r1, a1, r2, column = first_rooms[k]
-        firsts[k].sum0(grads[k], r0, a0)
-        firsts[k].send1(a0, r1)
-
-    def reduce1(k):
-        r0, a0, r1, a1, r2, column = first_rooms[k]
-        firsts[k].sum1(a0, r1, a1)
-        firsts[k].send2(a1, r2)
-
-    def reduce2(k):
-        r0, a0, r1, a1, r2, column = first_rooms[k]
-        firsts[k].sum2(a1, r2, column)
-        firsts[k].spread2(column)
-
-    def each(step, ks):
+    def stage(sums, ks, number):
         for k in ks:
-            step(k)
-
-    head, tail, two = (0, 1), (2, 3), range(2)
-    each(reduce0, head)
-    each(lambda k: firsts[k].send0(grads[k], first_rooms[k][0]), tail)
-    factor.spread1(factor_column, factor_sums)
-    for k in two:
-        a0, r1, a1, r2, column = kernel_rooms[k]
-        kernels[k].sum2(a1, r2, column)
-        kernels[k].spread2(column)
-    each(reduce1, head)
-    each(reduce0, tail)
-    each(lambda k: lasts[k].spread0(last_sums[k]), two)
-    factor.spread0(factor_sums)
-    each(lambda k: kernels[k].spread1(kernel_rooms[k][4], kernel_sums[k]), two)
-    each(reduce2, head)
-    each(reduce1, tail)
-    each(lambda k: kernels[k].spread0(kernel_sums[k]), two)
-    each(lambda k: firsts[k].spread1(first_rooms[k][5], first_sums[k]), head)
-    each(reduce2, tail)
-    each(lambda k: firsts[k].spread0(first_sums[k]), head)
-    each(lambda k: firsts[k].spread1(first_rooms[k][5], first_sums[k]), tail)
-    each(lambda k: firsts[k].spread0(first_sums[k]), tail)
+            sums[k][number]()
+
+    stage(first, head, 1)
+    stage(first, back, 0)
+    stage(kernel_sum, two, 2)
+    stage(first, head, 2)
+    each(last4, back)
+    stage(first, back, 1)
+    stage(kernel_sum, two, 3)
+    stage(first, head, 3)
+    stage(first, back, 2)
+    stage(kernel_sum, two, 4)
+    stage(first, head, 4)
+    stage(kernel_sum, two, 5)
+    stage(first, head, 5)
+    stage(first, back, 3)
+    stage(first, back, 4)
+    stage(first, back, 5)
     for part in (*firsts, *lasts, *kernels, factor):
         part.settle()
     store.wait()
@@ -1141,7 +1183,7 @@
     pixels_out[...] = pixels_wide[0]
 
 
-def finish_kernel(low_half, high_half, factors, group_out, squeeze_w, squeeze_b, excite_w, excite_b):
+def finish_kernel(low_half, high_half, ahead, back, group_out, squeeze_w, squeeze_b, excite_w, excite_b):
     ch = lax.axis_index("ch")
     se = squeeze_w.shape[1]
     split = low_half.shape[1]
@@ -1151,21 +1193,21 @@
         group_out[0:split, lanes] = low_half[j, :, 0:width].astype(F32)
         rest = 9 * GROUP_WIDTH - split
         group_out[split:, lanes] = high_half[j, :, 0:width].astype(F32)[:rest]
-    n = factors.shape[0]
-    whole = factors[...].astype(F32).reshape(n, -1, IMGS, 128)
-
-    def columns(start, tiles, width):
+    n = ahead.shape[0]
+
+    def columns(factors, start, tiles, width):
+        whole = factors[...].astype(F32).reshape(n, -1, IMGS, 128)
         parts = [whole[:, t].reshape(n * IMGS, 128) for t in range(start, start + tiles)]
         return jnp.concatenate(parts, axis=1)[:, :width]
 
-    excite_all, squeeze_all = columns(16, 8, HALF), columns(28, 2, se)
+    excite_all, squeeze_all = columns(back, 0, 8, HALF), columns(back, 8, 2, se)
     squeeze_b[...] = jnp.sum(squeeze_all, axis=0, keepdims=True)
     excite_b[...] = jnp.sum(excite_all, axis=0, keepdims=True)
     excite_all, squeeze_all = excite_all.astype(BF16), squeeze_all.astype(BF16)
     for start, place in ((0, ch), (8, 1 - ch)):
         rows = pl.ds(pl.multiple_of(place * HALF, 8), HALF)
-        squeeze_w[rows, :] = dot(columns(start, 8, HALF).astype(BF16), squeeze_all, ((0,), (0,)))
-    own, far = columns(24, 2, se), columns(26, 2, se)
+        squeeze_w[rows, :] = dot(columns(ahead, start, 8, HALF).astype(BF16), squeeze_all, ((0,), (0,)))
+    own, far = columns(ahead, 16, 2, se), columns(ahead, 18, 2, se)
     for k, left in enumerate((jnp.where(ch == 0, own, far), jnp.where(ch == 0, far, own))):
         excite_w[k * se : (k + 1) * se, :] = dot(left.astype(BF16), excite_all, ((0,), (0,)))
 
@@ -1225,13 +1267,15 @@
     bands = [pltpu.VMEM(((e - s) * 128, 9 * 256), BF16) for s, e in WINDOWS]
     mask10 = pltpu.VMEM((10, IMGS, 128), F32)
     mask = pltpu.VMEM((ROWS, 128), F32)
-    kernel_buf = pltpu.VMEM((9 * GROUP_WIDTH, 1024), F32)
     small = (TILES, IMGS, 128)
     wide_buf = pltpu.VMEM(wide, F32)
     tall = (ROWS, HALF)
+    ahead_shape = part_extents(n, ORDERS[0]) + (AHEAD_TILES * IMGS, 128)
+    back_shape = part_extents(n, ORDERS[0]) + (BACK_TILES * IMGS, 128)
     split_shapes = [(2 * HALF, se)] * 2 + [(2 * se, HALF)] * 2
     (
         first,
+        pixels_tiles,
         pixels_far,
         padded,
         group,
@@ -1261,7 +1305,8 @@
         ),
         [
             (wide, F32),
-            (tall, BF16),
+            (wide, BF16),
+            (wide, BF16),
             ((TILES, PAD_ROWS, 128), BF16),
             (wide, F32),
             (wide, BF16),
@@ -1276,7 +1321,7 @@
         + [(stat, F32)] * 4
         + [(small, F32)] * 2
         + [((IMGS, se), F32)] * 3
-        + [(small, F32)],
+        + [(small, F32), (ahead_shape, BF16)],
         [
             consts,
             local,
@@ -1288,7 +1333,6 @@
             pltpu.VMEM((2 * HALF, HALF), BF16),
             pltpu.VMEM((TILES, 2 * ROWS, 128), BF16),
             pltpu.VMEM((9 * GROUP_WIDTH, HALF), BF16),
-            kernel_buf,
             pltpu.VMEM((2 * HALF, se), F32),
             pltpu.VMEM((2 * se, HALF), F32),
             *(pltpu.VMEM(shape, BF16) for shape in split_shapes),
@@ -1297,7 +1341,7 @@
             mask10,
             *bands,
             DMA((6,)),
-            DMA((13,)),
+            DMA((14,)),
             DMA((6,)),
             DMA((6,)),
             DMA((TILES,)),
@@ -1305,14 +1349,17 @@
             DMA((2,)),
             DMA((2,)),
             *[sem] * 8,
+            pltpu.VMEM(ahead_shape[2:], BF16),
+            pltpu.VMEM(ahead_shape[3:], BF16),
+            *part_sems(n, 1),
         ],
         0,
         in_specs=[ANY] * 7 + [VMEM] * 5,
-        out_specs=[ANY] * 15 + [VMEM] * 10,
+        out_specs=[ANY] * 16 + [VMEM] * 10 + [ANY],
     )
     splits, rest = rest[:4], rest[4:]
     stats1, stats2, stats3, sums3, pooled, pooled_far = rest[:6]
-    squeezed, squeezed_far, squeeze_pre, excited = rest[6:]
+    squeezed, squeezed_far, squeeze_pre, excited, ahead_sums = rest[6:]
 
     def vmem(shape, dtype=BF16):
         return pltpu.VMEM(shape, dtype)
@@ -1342,8 +1389,9 @@
             *splits,
         ),
         [(wide, F32), (stat, F32), (small, F32), ((IMGS, se), F32), vectors]
-        + [(rooms[k][1], BF16) for k in range(4)]
-        + [(rooms[k][2], BF16) for k in range(2)],
+        + [(rooms[k][3], BF16) for k in range(2)]
+        + [(rooms[k][4], BF16) for k in range(2)]
+        + [(rooms[k][1], BF16) for k in (2, 3)],
         [
             consts,
             consts,
@@ -1367,6 +1415,8 @@
             vmem(small, F32),
             *(vmem(shape) for shape in shapes),
             *(vmem(room[0]) for room in rooms),
+            *(vmem(room[1]) for room in rooms[:2]),
+            *(vmem(room[2]) for room in rooms[:2]),
             DMA((10,)),
             DMA((TILES,)),
             DMA((TILES,)),
@@ -1380,16 +1430,28 @@
         in_specs=[ANY] * 7 + [VMEM] * 8 + [ANY] * 4,
         out_specs=[ANY] + [VMEM] * 10,
     )
-    mid1, mid3, arrive1 = carry[0:2], carry[2:4], carry[4:6]
-    kernel_shapes = [part_shape(n, ORDERS[k], TILES * 256) for k in range(2)]
-    kernel_rooms = [Part.room(n, ORDERS[k], kernel_shapes[k]) for k in range(2)]
-    first_pre_grad, sums1, vectors2, *carry = call(
-        functools.partial(group_grad_kernel, n),
+    done1, arrive2, mid3 = carry[0:2], carry[2:4], carry[4:6]
+    kernel_shapes = [part_shape(n, order, TILES * 256) for order in KERNEL_ORDERS]
+    kernel_rooms = [
+        Part.room(n, order, shape) for order, shape in zip(KERNEL_ORDERS, kernel_shapes)
+    ]
+    kernel_shapes = [part_shape(n, order, TILES * 256) for order in KERNEL_ORDERS]
+    kernel_rooms = [
+        Part.room(n, order, shape) for order, shape in zip(KERNEL_ORDERS, kernel_shapes)
+    ]
+    zone = vmem((TILES, 2 * ROWS, 128))
+    pixels_wide, vectors2, vectors1, *carry = call(
+        functools.partial(tail_kernel, n),
         (
             pre_grad,
             group,
             padded,
             first,
+            pixels_tiles,
+            pixels_far,
+            first_weight,
+            first_far,
+            merged_grad,
             stats2,
             live,
             sums2,
@@ -1397,110 +1459,53 @@
             gains,
             kernel,
             stats1,
-            *mid1,
+            *done1,
+            *arrive2,
             *mid3,
-            *arrive1,
+            excite_grad,
+            squeeze_grad,
         ),
-        [(wide, F32), (stat, F32), vectors]
-        + [(shape, BF16) for shape in kernel_shapes]
-        + [(room[0], BF16) for room in kernel_rooms]
-        + [(room[5], BF16) for room in rooms[2:]]
-        + [(shape, BF16) for shape in shapes[:2]],
+        [(wide, F32), vectors, vectors]
+        + [(shape, BF16) for shape in shapes * 2 + kernel_shapes]
+        + [(back_shape, BF16)],
         [
-            *(vmem(room[5]) for room in rooms[:2]),
             consts,
             consts,
             local,
             mask10,
-            kernel_buf,
             local,
+            vmem(stat, F32),
             wide_buf,
             wide_buf,
-            vmem((TILES, PAD_ROWS, 128)),
-            vmem((TILES, PAD_ROWS, 128)),
-            vmem((512, 9 * 256), F32),
-            *bands,
-            *(vmem(rooms[k][2]) for k in (2, 3)),
-            *(vmem(room[3]) for room in rooms),
-            *(vmem(room[4]) for room in rooms),
-            DMA((3,)),
-            sem,
-            sem,
-            *part_sems(n, 6),
-        ],
-        5,
-        in_specs=[ANY] * 4 + [VMEM] * 13,
-        out_specs=[ANY] + [VMEM] * 8 + [ANY] * 2,
-    )
-    kernel_grads, kernel_arrive, columns, last_early = carry[0:2], carry[2:4], carry[4:6], carry[6:8]
-
-    def tiles_of(value):
-        return jnp.pad(value, ((0, 0), (0, 256 - se))).reshape(IMGS, 2, 128).swapaxes(0, 1)
-
-    factors = jnp.concatenate(
-        [
-            pooled,
-            pooled_far,
-            excite_grad,
-            tiles_of(squeezed),
-            tiles_of(squeezed_far),
-            tiles_of(squeeze_grad),
-        ]
-    )
-    count_tiles = factors.shape[0]
-    factors = factors.reshape(count_tiles * IMGS, 128).astype(BF16)
-    factor_shape = part_extents(n, ORDERS[0]) + factors.shape
-    pixels_wide, vectors1, *carry = call(
-        functools.partial(first_grad_kernel, n),
-        (
-            first_pre_grad,
-            first,
-            pixels,
-            pixels_far,
-            first_weight,
-            first_far,
-            merged_grad,
-            stats1,
-            live,
-            sums1,
-            counts,
-            gains,
-            factors,
-            *kernel_grads,
-            *kernel_arrive,
-            *columns,
-        ),
-        [(wide, F32), vectors]
-        + [(shape, BF16) for shape in shapes[2:] + shapes + kernel_shapes]
-        + [(factor_shape, BF16)],
-        [
-            consts,
-            local,
-            mask10,
-            wide_buf,
-            wide_buf,
-            low_buf,
-            low_buf,
-            vmem((ROWS, HALF)),
-            vmem((ROWS, HALF)),
+            zone,
+            zone,
             weight_buf,
             weight_buf,
             vmem((ROWS, 128), F32),
+            vmem((512, 9 * 256)),
+            vmem((512, 9 * 256)),
+            *(vmem(rooms[k][kind]) for kind in (2, 3, 4) for k in (2, 3)),
+            *(vmem(room[5]) for room in rooms),
             *(vmem(shape) for shape in shapes),
             *(vmem(shape) for room in rooms for shape in room),
-            *(vmem(shape) for room in kernel_rooms for shape in room[1:]),
-            vmem(factor_shape[2:]),
-            DMA((6,)),
+            *(vmem(shape) for shape in kernel_shapes),
+            *(vmem(shape) for room in kernel_rooms for shape in room),
+            vmem(back_shape[2:]),
+            vmem(back_shape[3:]),
+            DMA((5,)),
             DMA((TILES,)),
             DMA((TILES,)),
-            *part_sems(n, 9),
+            sem,
+            sem,
+            pltpu.SemaphoreType.REGULAR,
+            *part_sems(n, 11),
         ],
-        6,
-        in_specs=[ANY] * 7 + [VMEM] * 12,
-        out_specs=[ANY, VMEM] + [ANY] * 9,
+        5,
+        in_specs=[ANY] * 9 + [VMEM] * 15,
+        out_specs=[ANY, VMEM, VMEM] + [ANY] * 11,
     )
-    sums = [s.reshape(4, 1024, 128) for s in (*last_early, *carry[0:6])]
-    kernel_sums = [s.reshape(TILES, 256, 128) for s in carry[6:8]]
+    sums = [s.reshape(4, 1024, 128) for s in carry[0:8]]
+    kernel_sums = [s.reshape(TILES, 256, 128) for s in carry[8:10]]
     late = pl.BlockSpec((1, 1024, 128), lambda j: (jnp.maximum(j - 4, 0), 0, 0))
     early = pl.BlockSpec((1, 1024, 128), lambda j: (jnp.minimum(j, 3), 0, 0))
     last_weight_grad, first_weight_grad, pixels_grad = call(
@@ -1518,7 +1523,7 @@
     )
     group_weight_grad, squeeze_weight_grad, squeeze_bias_grad, excite_weight_grad, excite_bias_grad = call(
         finish_kernel,
-        (*kernel_sums, carry[8].reshape(n, count_tiles * IMGS, 128)),
+        (*kernel_sums, ahead_sums.reshape(n, -1, 128), carry[10].reshape(n, -1, 128)),
         [
             ((9 * GROUP_WIDTH, HALF), F32),
             ((2 * HALF, se), F32),

time: 351 us -> 322 us (0.917)
  Pallas kernels: 330 us -> 306 us
  other arithmetic: 4.48 us -> 0.78 us
    pallas_call x6 -> x5, Pallas kernels: 330 us -> 306 us  [call(): pl.pallas_call(kernel, grid=grid, out_shape=[jax.ShapeDtypeStruct(shape,...]
where the time goes in v4:
time: 322 us; the launch traced here: 316 us
  Pallas kernels  306 us (95%)
  local copies, waits for them, and re-layouts  8.48 us (3%)
    pallas_call x5, Pallas kernels, call(): pl.pallas_call(kernel, grid=grid, out_shape=[jax.ShapeDtypeStruct(shape,...  306 us

profile of v4, /device:TPU:10, one launch (start us, length us, event | category | flops | bytes accessed | tf_op | source)
XLA Modules:
  0.0 316.1 jit_solution(4525871855611397958)
XLA Ops:
  0.6 0.7 dynamic_slice.3
  1.4 0.7 multiply_add_fusion
  2.0 0.7 broadcast_in_dim.8.refs_7_.refs_11_.refs_12_
  2.7 0.1 reshape.89
  2.8 0.1 reduce_sum.9
  2.9 1.4 stack.27.refs_9_.refs_12_.refs_13_
  4.3 0.7 broadcast_in_dim.9.refs_8_.refs_10_
  5.0 78.6 %shard_map.271 = (f32[8,1504,128]{2,1,0:T(8,128)}, bf16[8,1504,128]{2,1,0:T(8,128)(2,1)}, bf16[8,1504,128]{2,1,0:T(8,128)(2,1)}, bf16[8,2848,128]{2,1,0:T(8,128)...) custom-call(bf16[1504,1008]{1,0:T(8,128)(2,1)} %refs_0_.1, ...), custom_call_target="tpu_custom_call" | custom-call | tf_op jit(solution)/shard_map/pallas_call | solution.py:1219
  83.7 49.3 %shard_map.272 = (f32[8,1504,128]{2,1,0:T(8,128)}, f32[16,2,8,128]{3,2,1,0:T(8,128)}, f32[8,8,128]{2,1,0:T(8,128)}, f32[8,252]{1,0:T(8,128)}, f32[2,8,128]{2,1,0...) custom-call(f32[8,1504,128]{2,1,0:T(8,128)} %get-tuple-element.72.re, ...), custom_call_target="tpu_custom_call" | custom-call | tf_op jit(solution)/shard_map/pallas_call | solution.py:1219
  132.9 0.0 copy-start.1
  132.9 158.5 %shard_map.273 = (f32[8,1504,128]{2,1,0:T(8,128)}, f32[2,8,128]{2,1,0:T(8,128)}, f32[2,8,128]{2,1,0:T(8,128)}, bf16[2,2,4,256,128]{4,3,2,1,0:T(8,128)(2,1)}, bf1...) custom-call(f32[8,1504,128]{2,1,0:T(8,128)} %get-tuple-element.87.re, ...), custom_call_target="tpu_custom_call" | custom-call | tf_op jit(solution)/shard_map/pallas_call | solution.py:1219
  291.4 0.7 copy.39
  292.1 0.6 fusion.2
  292.7 0.7 copy.38
  293.4 0.6 fusion.1
  294.0 0.0 copy-done.1
  294.0 0.6 fusion
  294.6 4.6 %shard_map.275 = (f32[504,1008]{1,0:T(8,128)}, f32[2016,252]{1,0:T(8,128)}, f32[1,252]{1,0:T(1,128)}, f32[504,1008]{1,0:T(8,128)}, f32[1,1008]{1,0:T(1,128)}) custom-call(bf16[8,256,128]{2,1,0:T(8,128)(2,1)} %bitcast.53, bf16[8,256,128]{2,1,0:T(8,128)(2,1)} %bitcast.54, bf16[16,160,128]{2,1,0:T(8,128)(2,1)} %bitcast.52, bf16[16,80,128]{2,1,0:T(8,128)(2,1)} %bitcast.55), custom_call_target="tpu_custom_call" | custom-call | tf_op jit(solution)/shard_map/pallas_call | solution.py:1219
  299.2 0.0 copy-start
  299.2 14.9 %shard_map.274 = (f32[2016,1008]{1,0:T(8,128)}, f32[2016,1008]{1,0:T(8,128)}, f32[1504,1008]{1,0:T(8,128)}) custom-call(bf16[4,1024,128]{2,1,0:T(8,128)(2,1)} %bitcast.44, bf16[4,1024,128]{2,1,0:T(8,128)(2,1)} %bitcast.45, bf16[4,1024,128]{2,1,0:T(8,128)(2,1)} %bitcast.46, bf16[4,1024,128]{2,1,0:T(8,128)(2,1)} %bitcast.47, bf16[4,1024,128]{2,1,0:T(8,128)(2,1)} %bitcast.48, ...), custom_call_target="tpu_custom_call" | custom-call | tf_op jit(solution)/shard_map/pallas_call | solution.py:1219
  314.2 0.0 copy-done
  314.2 1.6 copy.41
  (2 shorter events, 0.0 us)
Async XLA Ops:
  132.9 161.1 %copy-start.1 = (f32[2,8,128]{2,1,0:T(8,128)S(1)}, f32[2,8,128]{2,1,0:T(8,128)}, u32[]{:S(2)}) copy-start(f32[2,8,128]{2,1,0:T(8,128)} %get-tuple-element.126) | copy-start | bytes 24580
  299.2 15.0 %copy-start = (bf16[1504,1008]{1,0:T(8,128)(2,1)S(1)}, bf16[1504,1008]{1,0:T(8,128)(2,1)}, u32[]{:S(2)}) copy-start(bf16[1504,1008]{1,0:T(8,128)(2,1)} %get-tuple-element.148) | copy-start | bytes 9096196

commit v5 on v4

--- a/solution.py
+++ b/solution.py
@@ -286,14 +286,27 @@
     return value[:IMGS] + value[IMGS:] + dot(both, right_low, dims)[:IMGS]
 
 
-def load_vectors(vectors, first, norm):
+def load_vectors(gain, shift, norm):
     norm[...] = jnp.zeros_like(norm)
-    for k in range(2):
+    for k, row in enumerate((gain, shift)):
         for j in range(TILES):
             width = 128 if j < 7 else LAST
-            norm[k, j : j + 1, 0:width] = vectors[
-                first + k : first + k + 1, j * 128 : j * 128 + width
-            ]
+            norm[k, j : j + 1, 0:width] = row[:, j * 128 : j * 128 + width]
+
+
+def load_counts(n, crops, counts, live):
+    me = lax.axis_index("img")
+    for image in range(IMGS):
+        counts[image : image + 1, :] = jnp.full((1, 128), crops[me * IMGS + image], jnp.int32)
+
+    def device(d):
+        total = crops[d * IMGS]
+        for image in range(1, IMGS):
+            total = total + crops[d * IMGS + image]
+        rows = (IMGS * BIG_ROWS + 9 * total).astype(F32)
+        live[d] = jnp.full((TILES, 128), rows, F32)
+
+    for_each(n, device)
 
 
 def live_slots(counts, mask10):
@@ -313,7 +326,7 @@
 def forward_kernel(n, *refs):
     r = Refs(refs)
     pixels_any, weight1_any, weight3_any, kernel_any, squeeze_any, excite_any, output_any = r.take(7)
-    counts, live, vectors, squeeze_b, excite_b = r.take(5)
+    crops, vectors, squeeze_b, excite_b = r.take(), r.take(6), r.take(), r.take()
     first_out, pixels_out, far_out, padded_out, group_out, scaled_out, scaled_far_out = r.take(7)
     last_out, merged_out, block_out = r.take(3)
     far1, far3 = r.take(2)
@@ -321,7 +334,8 @@
     stats1, stats2, stats3, sums3 = r.take(4)
     pooled, pooled_far, squeezed, squeezed_far, squeeze_pre, excited = r.take(6)
     factor_sums = r.take()
-    consts, norm, local, buf_a, buf_b, pixels, far, weight, zone = r.take(9)
+    counts, live, norms = r.take(), r.take(), r.take(3)
+    consts, local, buf_a, buf_b, pixels, far, weight, zone = r.take(8)
     kernel_low, squeeze_w, excite_w = r.take(3)
     splits = r.take(4)
     turned, mask, mask10 = r.take(3)
@@ -346,6 +360,9 @@
     ]
     own = pl.multiple_of(ch * HALF, 16)
     away = pl.multiple_of((1 - ch) * HALF, 16)
+    load_counts(n, crops, counts, live)
+    for k in range(3):
+        load_vectors(vectors[2 * k], vectors[2 * k + 1], norms[k])
     live_slots(counts, mask10)
     natural_mask(mask10, mask)
     count = live[lax.axis_index("img")][0:1, :]
@@ -397,12 +414,11 @@
     for k, w in enumerate((squeeze_w, excite_w)):
         splits[2 * k][...], splits[2 * k + 1][...] = halves(w[...])
     stores += [fetch(splits[k], split_outs[k], store.at[2 + k]) for k in range(4)]
-    load_vectors(vectors, 0, norm)
     load_output = fetch(output_any, far, load.at[1])
     for s in store_pixels:
         s.wait()
     gather.wait()
-    norm_constants(n, stats1, live, norm, consts)
+    norm_constants(n, stats1, live, norms[0], consts)
 
     def activate_first(j):
         average = row_of(consts, 0, j)
@@ -433,11 +449,10 @@
     gather = Gather(n, local, stats2, *gathers[1])
     gather.start()
     store_group = fetch(buf_b, group_out, store.at[7])
-    load_vectors(vectors, 2, norm)
     store_first.wait()
     store_padded.wait()
     gather.wait()
-    norm_constants(n, stats2, live, norm, consts)
+    norm_constants(n, stats2, live, norms[1], consts)
     inverse = 1.0 / (BIG_ROWS + 9.0 * counts[...].astype(F32))
 
     def activate_group(j):
@@ -512,12 +527,11 @@
     gather = Gather(n, local, stats3, *gathers[2])
     gather.start()
     stores.append(fetch(buf_b, last_out, store.at[10]))
-    load_vectors(vectors, 4, norm)
     factor.spread0(factor_sums)
     buf_a[7, :, LAST:128] = jnp.zeros((ROWS, 128 - LAST), F32)
     load_output.wait()
     gather.wait()
-    norm_constants(n, stats3, live, norm, consts)
+    norm_constants(n, stats3, live, norms[2], consts)
     local[...] = jnp.zeros_like(local)
 
     def merge(j, lanes, width):
@@ -720,12 +734,12 @@
     r = Refs(refs)
     last_any, merged_any, group_any, scaled_any, scaled_far_any, weight_any, weight_far_any = r.take(7)
     stats3, live, sums3 = r.take(3)
-    stats2, counts, vectors_in, excited, squeeze_pre = r.take(5)
+    stats2, counts, norm2, norm3, excited, squeeze_pre = r.take(6)
     split_anys = r.take(4)
     pre_grad, sums2, excite_grad, squeeze_grad, vectors = r.take(5)
     done1, arrive2, mid3 = r.take(2), r.take(2), r.take(2)
     consts, consts2, local, buf_a, buf_b, low, low_far, scaled, scaled_far = r.take(9)
-    weight, weight_far, norm, mask, mask10 = r.take(5)
+    weight, weight_far, mask, mask10 = r.take(4)
     splits = r.take(4)
     terms, terms_in, pool_terms, pool_in, pool_tiles = r.take(5)
     grads, rooms, mid1, arrive1 = r.take(4), r.take(4), r.take(2), r.take(2)
@@ -751,11 +765,9 @@
     live_slots(counts, mask10)
     natural_mask(mask10, mask)
     inverse = 1.0 / (BIG_ROWS + 9.0 * counts[...].astype(F32))
-    load_vectors(vectors_in, 4, norm)
-    norm_constants(n, stats3, live, norm, consts)
+    norm_constants(n, stats3, live, norm3, consts)
     back_constants(n, sums3, consts, vectors)
-    load_vectors(vectors_in, 2, norm)
-    norm_constants(n, stats2, live, norm, consts2)
+    norm_constants(n, stats2, live, norm2, consts2)
     parts = [Part(n, order, sems[2 * k : 2 * k + 2]) for k, order in enumerate(ORDERS)]
     wait_all()
     loads[0].wait()
@@ -885,13 +897,13 @@
     r = Refs(refs)
     pre_any, group_any, padded_any, first_any = r.take(4)
     pixels_any, pixels_far_any, weight_any, weight_far_any, merged_any = r.take(5)
-    stats2, live, sums2, counts, vectors_in, kernel, stats1 = r.take(7)
+    stats2, live, sums2, counts, norm1, norm2, kernel, stats1 = r.take(8)
     done1, arrive2, mid3 = r.take(2), r.take(2), r.take(2)
     factor_parts = r.take(2)
     pixels_grad, group_vectors, first_vectors = r.take(3)
     last_sums, first_sums, kernel_sums = r.take(4), r.take(4), r.take(2)
     factor_sums = r.take()
-    consts, consts1, norm, mask10, local, sums1 = r.take(6)
+    consts, consts1, mask10, local, sums1 = r.take(5)
     buf_a, buf_b, zone1, zone2, weight, weight_far, turned = r.take(7)
     bands = r.take(2)
     arrive3, done3, arrive4, last_columns = r.take(2), r.take(2), r.take(2), r.take(4)
@@ -922,11 +934,9 @@
     kernels = [Part(n, KERNEL_ORDERS[k], sems[8 + k]) for k in range(2)]
     factor = Part(n, ORDERS[0], sems[10])
     live_slots(counts, mask10)
-    load_vectors(vectors_in, 2, norm)
-    norm_constants(n, stats2, live, norm, consts)
+    norm_constants(n, stats2, live, norm2, consts)
     back_constants(n, sums2, consts, group_vectors)
-    load_vectors(vectors_in, 0, norm)
-    norm_constants(n, stats1, live, norm, consts1)
+    norm_constants(n, stats1, live, norm1, consts1)
     wait_all()
 
     def each(step, ks):
@@ -1166,11 +1176,39 @@
     store.wait()
 
 
-def spread_kernel(*refs):
-    lasts, firsts, pixels_wide = refs[0:4], refs[4:8], refs[8]
-    last_out, first_out, pixels_out = refs[9:12]
+def finish_kernel(*refs):
+    r = Refs(refs)
+    lasts, firsts, pixels_wide, kernels = r.take(4), r.take(4), r.take(), r.take(2)
+    ahead, back, vectors = r.take(), r.take(), r.take(3)
+    last_out, first_out, pixels_out, group_out, excite_w, excite_b = r.take(6)
+    squeeze_w, squeeze_b, rows_out = r.take(), r.take(), r.take(6)
+    behind, left0, left1 = r.take(3)
     ch = lax.axis_index("ch")
     j = pl.program_id(0)
+    n = ahead.shape[0]
+    se = squeeze_w.shape[1]
+
+    @pl.when(j == 0)
+    def _():
+        behind[...] = back[...].astype(F32)
+        before = ahead[...].astype(F32).reshape(n, AHEAD_TILES, IMGS, 128)
+
+        def columns(start, tiles, width):
+            parts = [before[:, t].reshape(n * IMGS, 128) for t in range(start, start + tiles)]
+            return jnp.concatenate(parts, axis=1)[:, :width]
+
+        tiles = [behind[:, t * IMGS : (t + 1) * IMGS, :].reshape(n * IMGS, 128) for t in (8, 9)]
+        squeeze_all = jnp.concatenate(tiles, axis=1)[:, :se]
+        squeeze_b[...] = jnp.sum(squeeze_all, axis=0, keepdims=True)
+        squeeze_all = squeeze_all.astype(BF16)
+        for start, place in ((0, ch), (8, 1 - ch)):
+            rows = pl.ds(pl.multiple_of(place * HALF, 8), HALF)
+            left = columns(start, 8, HALF).astype(BF16)
+            squeeze_w[rows, :] = dot(left, squeeze_all, ((0,), (0,)))
+        own, far = columns(16, 2, se), columns(18, 2, se)
+        left0[...] = jnp.where(ch == 0, own, far).astype(BF16)
+        left1[...] = jnp.where(ch == 0, far, own).astype(BF16)
+
     for sums, out in ((lasts, last_out), (firsts, first_out)):
         for late in range(2):
 
@@ -1181,35 +1219,16 @@
                     out[rows, :] = sums[2 * late + k][0, 0:HALF, :].astype(F32)
 
     pixels_out[...] = pixels_wide[0]
-
-
-def finish_kernel(low_half, high_half, ahead, back, group_out, squeeze_w, squeeze_b, excite_w, excite_b):
-    ch = lax.axis_index("ch")
-    se = squeeze_w.shape[1]
-    split = low_half.shape[1]
-    for j in range(TILES):
-        width = 128 if j < 7 else LAST
-        lanes = slice(j * 128, j * 128 + width)
-        group_out[0:split, lanes] = low_half[j, :, 0:width].astype(F32)
-        rest = 9 * GROUP_WIDTH - split
-        group_out[split:, lanes] = high_half[j, :, 0:width].astype(F32)[:rest]
-    n = ahead.shape[0]
-
-    def columns(factors, start, tiles, width):
-        whole = factors[...].astype(F32).reshape(n, -1, IMGS, 128)
-        parts = [whole[:, t].reshape(n * IMGS, 128) for t in range(start, start + tiles)]
-        return jnp.concatenate(parts, axis=1)[:, :width]
-
-    excite_all, squeeze_all = columns(back, 0, 8, HALF), columns(back, 8, 2, se)
-    squeeze_b[...] = jnp.sum(squeeze_all, axis=0, keepdims=True)
-    excite_b[...] = jnp.sum(excite_all, axis=0, keepdims=True)
-    excite_all, squeeze_all = excite_all.astype(BF16), squeeze_all.astype(BF16)
-    for start, place in ((0, ch), (8, 1 - ch)):
-        rows = pl.ds(pl.multiple_of(place * HALF, 8), HALF)
-        squeeze_w[rows, :] = dot(columns(ahead, start, 8, HALF).astype(BF16), squeeze_all, ((0,), (0,)))
-    own, far = columns(ahead, 16, 2, se), columns(ahead, 18, 2, se)
-    for k, left in enumerate((jnp.where(ch == 0, own, far), jnp.where(ch == 0, far, own))):
-        excite_w[k * se : (k + 1) * se, :] = dot(left.astype(BF16), excite_all, ((0,), (0,)))
+    split = kernels[0].shape[1]
+    group_out[0:split, :] = kernels[0][0].astype(F32)
+    group_out[split:, :] = kernels[1][0].astype(F32)[: 9 * GROUP_WIDTH - split]
+    rows = pl.ds(pl.multiple_of(j * IMGS, IMGS), IMGS)
+    excite = behind[:, rows, :].reshape(n * IMGS, 128)
+    excite_b[...] = jnp.sum(excite, axis=0, keepdims=True)
+    for k, left in enumerate((left0, left1)):
+        excite_w[k * se : (k + 1) * se, :] = dot(left[...], excite.astype(BF16), ((0,), (0,)))
+    for k in range(6):
+        rows_out[k][...] = vectors[k // 2][k % 2, pl.ds(j, 1), :]
 
 
 def call(kernel, ins, outs, scratch, ident=None, in_specs=None, out_specs=None, grid=()):
@@ -1246,20 +1265,12 @@
     last_shift,
     output_grad,
 ):
-    me = lax.axis_index("img")
     assert pixels.shape == (ROWS, HALF)
     se = squeeze_weight.shape[1]
     wide = (TILES, ROWS, 128)
     stat = (n, 2, TILES, 128)
     sem = DMA((n - 1,))
 
-    local_counts = lax.dynamic_slice_in_dim(crop_counts, me * IMGS, IMGS)
-    counts = jnp.broadcast_to(local_counts[:, None], (IMGS, 128))
-    live = jnp.sum((BIG_ROWS + 9 * crop_counts).reshape(n, IMGS), axis=1).astype(F32)
-    live = jnp.broadcast_to(live[:, None, None], (n, TILES, 128))
-    gains = jnp.stack(
-        [first_gain, first_shift, group_gain, group_shift, last_gain, last_shift]
-    )
     kernel = group_weight.reshape(9 * GROUP_WIDTH, HALF)
     local = pltpu.VMEM((2, TILES, 128), F32)
     consts = pltpu.VMEM((8, TILES, 128), F32)
@@ -1297,9 +1308,13 @@
             squeeze_weight,
             excite_weight,
             output_grad,
-            counts,
-            live,
-            gains,
+            crop_counts,
+            first_gain[None],
+            first_shift[None],
+            group_gain[None],
+            group_shift[None],
+            last_gain[None],
+            last_shift[None],
             squeeze_bias[None],
             excite_bias[None],
         ),
@@ -1321,10 +1336,10 @@
         + [(stat, F32)] * 4
         + [(small, F32)] * 2
         + [((IMGS, se), F32)] * 3
-        + [(small, F32), (ahead_shape, BF16)],
+        + [(small, F32), (ahead_shape, BF16), ((IMGS, 128), jnp.int32), ((n, TILES, 128), F32)]
+        + [vectors] * 3,
         [
             consts,
-            local,
             local,
             wide_buf,
             wide_buf,
@@ -1354,12 +1369,13 @@
             *part_sems(n, 1),
         ],
         0,
-        in_specs=[ANY] * 7 + [VMEM] * 5,
-        out_specs=[ANY] * 16 + [VMEM] * 10 + [ANY],
+        in_specs=[ANY] * 7 + [pl.BlockSpec(memory_space=pltpu.SMEM)] + [VMEM] * 8,
+        out_specs=[ANY] * 16 + [VMEM] * 10 + [ANY] + [VMEM] * 5,
     )
     splits, rest = rest[:4], rest[4:]
     stats1, stats2, stats3, sums3, pooled, pooled_far = rest[:6]
-    squeezed, squeezed_far, squeeze_pre, excited, ahead_sums = rest[6:]
+    squeezed, squeezed_far, squeeze_pre, excited, ahead_sums = rest[6:11]
+    counts, live, norm1, norm2, norm3 = rest[11:]
 
     def vmem(shape, dtype=BF16):
         return pltpu.VMEM(shape, dtype)
@@ -1383,7 +1399,8 @@
             sums3,
             stats2,
             counts,
-            gains,
+            norm2,
+            norm3,
             excited,
             squeeze_pre,
             *splits,
@@ -1404,7 +1421,6 @@
             low_buf,
             weight_buf,
             weight_buf,
-            local,
             mask,
             mask10,
             *(vmem(shape) for shape in split_shapes),
@@ -1427,7 +1443,7 @@
             *part_sems(n, 4),
         ],
         4,
-        in_specs=[ANY] * 7 + [VMEM] * 8 + [ANY] * 4,
+        in_specs=[ANY] * 7 + [VMEM] * 9 + [ANY] * 4,
         out_specs=[ANY] + [VMEM] * 10,
     )
     done1, arrive2, mid3 = carry[0:2], carry[2:4], carry[4:6]
@@ -1456,7 +1472,8 @@
             live,
             sums2,
             counts,
-            gains,
+            norm1,
+            norm2,
             kernel,
             stats1,
             *done1,
@@ -1471,7 +1488,6 @@
         [
             consts,
             consts,
-            local,
             mask10,
             local,
             vmem(stat, F32),
@@ -1501,48 +1517,66 @@
             *part_sems(n, 11),
         ],
         5,
-        in_specs=[ANY] * 9 + [VMEM] * 15,
+        in_specs=[ANY] * 9 + [VMEM] * 16,
         out_specs=[ANY, VMEM, VMEM] + [ANY] * 11,
     )
     sums = [s.reshape(4, 1024, 128) for s in carry[0:8]]
     kernel_sums = [s.reshape(TILES, 256, 128) for s in carry[8:10]]
     late = pl.BlockSpec((1, 1024, 128), lambda j: (jnp.maximum(j - 4, 0), 0, 0))
     early = pl.BlockSpec((1, 1024, 128), lambda j: (jnp.minimum(j, 3), 0, 0))
-    last_weight_grad, first_weight_grad, pixels_grad = call(
-        spread_kernel,
-        (*sums, pixels_wide),
-        [((2 * HALF, HALF), F32), ((2 * HALF, HALF), F32), ((ROWS, HALF), F32)],
-        [],
-        in_specs=[early, early, late, late] * 2 + [pl.BlockSpec((1, ROWS, 128), lambda j: (j, 0, 0))],
+
+    def by_tile(rows):
+        return pl.BlockSpec((rows, 128), lambda j: (0, j))
+
+    def whole(shape):
+        return pl.BlockSpec(shape, lambda j: (0,) * len(shape))
+
+    ahead_all, back_all = ahead_sums.reshape(n, -1, 128), carry[10].reshape(n, -1, 128)
+    half_kernel = pl.BlockSpec((1, 256, 128), lambda j: (j, 0, 0))
+    results = call(
+        finish_kernel,
+        (*sums, pixels_wide, *kernel_sums, ahead_all, back_all, vectors1, vectors2, vectors3),
+        [
+            ((2 * HALF, HALF), F32),
+            ((2 * HALF, HALF), F32),
+            ((ROWS, HALF), F32),
+            ((9 * GROUP_WIDTH, HALF), F32),
+            ((2 * se, HALF), F32),
+            ((1, HALF), F32),
+            ((2 * HALF, se), F32),
+            ((1, se), F32),
+        ]
+        + [((1, HALF), F32)] * 6,
+        [
+            vmem(back_all.shape, F32),
+            vmem((n * IMGS, se)),
+            vmem((n * IMGS, se)),
+        ],
+        in_specs=[early, early, late, late] * 2
+        + [pl.BlockSpec((1, ROWS, 128), lambda j: (j, 0, 0)), half_kernel, half_kernel]
+        + [whole(ahead_all.shape), whole(back_all.shape)]
+        + [whole(vectors[0])] * 3,
         out_specs=[
-            pl.BlockSpec((2 * HALF, 128), lambda j: (0, j)),
-            pl.BlockSpec((2 * HALF, 128), lambda j: (0, j)),
-            pl.BlockSpec((ROWS, 128), lambda j: (0, j)),
-        ],
+            by_tile(2 * HALF),
+            by_tile(2 * HALF),
+            by_tile(ROWS),
+            by_tile(9 * GROUP_WIDTH),
+            by_tile(2 * se),
+            by_tile(1),
+            whole((2 * HALF, se)),
+            whole((1, se)),
+        ]
+        + [by_tile(1)] * 6,
         grid=(TILES,),
     )
-    group_weight_grad, squeeze_weight_grad, squeeze_bias_grad, excite_weight_grad, excite_bias_grad = call(
-        finish_kernel,
-        (*kernel_sums, ahead_sums.reshape(n, -1, 128), carry[10].reshape(n, -1, 128)),
-        [
-            ((9 * GROUP_WIDTH, HALF), F32),
-            ((2 * HALF, se), F32),
-            ((1, se), F32),
-            ((2 * se, HALF), F32),
-            ((1, HALF), F32),
-        ],
-        [],
-    )
+    last_weight_grad, first_weight_grad, pixels_grad, group_weight_grad = results[:4]
+    excite_weight_grad, excite_bias_grad, squeeze_weight_grad, squeeze_bias_grad = results[4:8]
+    rows = [result[0] for result in results[8:]]
+    first_gain_grad, first_shift_grad = rows[0:2]
+    group_gain_grad, group_shift_grad = rows[2:4]
+    last_gain_grad, last_shift_grad = rows[4:6]
     group_weight_grad = group_weight_grad.reshape(3, 3, GROUP_WIDTH, HALF)
     squeeze_bias_grad, excite_bias_grad = squeeze_bias_grad[0], excite_bias_grad[0]
-
-    def pair(vector):
-        flat = vector.reshape(2, 1024)[:, :HALF]
-        return flat[0], flat[1]
-
-    first_gain_grad, first_shift_grad = pair(vectors1)
-    group_gain_grad, group_shift_grad = pair(vectors2)
-    last_gain_grad, last_shift_grad = pair(vectors3)
     return (
         block_out,
         pixels_grad,

time: 322 us -> 314 us (0.975)
  local copies, waits for them, and re-layouts: 8.48 us -> 1.65 us
    pallas_call x5 -> x4, Pallas kernels: 306 us -> 307 us  [call(): pl.pallas_call(kernel, grid=grid, out_shape=[jax.ShapeDtypeStruct(shape,...]
where the time goes in v5:
time: 314 us; the launch traced here: 310 us
  Pallas kernels  307 us (98%)
    pallas_call x4, Pallas kernels, call(): pl.pallas_call(kernel, grid=grid, out_shape=[jax.ShapeDtypeStruct(shape,...  307 us

profile of v5, /device:TPU:10, one launch (start us, length us, event | category | flops | bytes accessed | tf_op | source)
XLA Modules:
  0.0 309.6 jit_solution(15168674546702020731)
XLA Ops:
  0.7 79.3 %shard_map.271 = (f32[8,1504,128]{2,1,0:T(8,128)}, bf16[8,1504,128]{2,1,0:T(8,128)(2,1)}, bf16[8,1504,128]{2,1,0:T(8,128)(2,1)}, bf16[8,2848,128]{2,1,0:T(8,128)...) custom-call(bf16[1504,1008]{1,0:T(8,128)(2,1)} %refs_0_.1, ...), custom_call_target="tpu_custom_call" | custom-call | tf_op jit(solution)/shard_map/pallas_call | solution.py:1238
  79.9 49.0 %shard_map.272 = (f32[8,1504,128]{2,1,0:T(8,128)}, f32[16,2,8,128]{3,2,1,0:T(8,128)}, f32[8,8,128]{2,1,0:T(8,128)}, f32[8,252]{1,0:T(8,128)}, f32[2,8,128]{2,1,0...) custom-call(f32[8,1504,128]{2,1,0:T(8,128)} %get-tuple-element.83.re, ...), custom_call_target="tpu_custom_call" | custom-call | tf_op jit(solution)/shard_map/pallas_call | solution.py:1238
  128.9 160.9 %shard_map.273 = (f32[8,1504,128]{2,1,0:T(8,128)}, f32[2,8,128]{2,1,0:T(8,128)}, f32[2,8,128]{2,1,0:T(8,128)}, bf16[2,2,4,256,128]{4,3,2,1,0:T(8,128)(2,1)}, bf1...) custom-call(f32[8,1504,128]{2,1,0:T(8,128)} %get-tuple-element.102.r, ...), custom_call_target="tpu_custom_call" | custom-call | tf_op jit(solution)/shard_map/pallas_call | solution.py:1238
  289.8 0.0 copy-start
  289.9 17.8 %shard_map.274 = (f32[2016,1008]{1,0:T(8,128)}, f32[2016,1008]{1,0:T(8,128)}, f32[1504,1008]{1,0:T(8,128)}, f32[504,1008]{1,0:T(8,128)}, f32[504,1008]{1,0:T(8,1...) custom-call(bf16[4,1024,128]{2,1,0:T(8,128)(2,1)} %bitcast.32, ...), custom_call_target="tpu_custom_call" | custom-call | tf_op jit(solution)/shard_map/pallas_call | solution.py:1238
  307.6 0.0 copy-done
  307.6 1.6 copy.32
Async XLA Ops:
  289.8 17.8 %copy-start = (bf16[1504,1008]{1,0:T(8,128)(2,1)S(1)}, bf16[1504,1008]{1,0:T(8,128)(2,1)}, u32[]{:S(2)}) copy-start(bf16[1504,1008]{1,0:T(8,128)(2,1)} %get-tuple-element.164) | copy-start | bytes 9096196
